TPU v7x, 32 devices: a whole 2x2x4 slice. The times are simulated.
32 devices in a mesh: blk: 8 (over z, x), states: 4 (over y, core).
Axes of the slice: x: 2, y: 2, z: 4, core: 2. Of those that a mesh axis runs over, the one named last changes fastest.
Arguments:
- start_states: float32 [16, 16, 128, 512], P('blk', None, None, 'states'), may hold values from -6 to 6
- couplings: float32 [16, 128, 128], replicated, may hold values from -0.1875 to 0.1875
- potential: float32 [16, 16, 128], P('blk'), may hold values from -18 to 18
- site_offsets: int32 [16, 6, 16], P('blk'), may hold values from 0 to 15
- coupling_index: int32 [16, 7, 16], P('blk'), may hold values from 0 to 15
- degrees: int32 [512], P('states'), may hold values from 1 to 3, as said below
Outputs:
- orthonormal: float32 [16, 16, 128, 512], P('blk', 'states')
Inputs may be any that keep to these rules, and one draw needn't show every extreme that they name: `degrees`: every degree from 1 to 3 belongs to some state.
All inputs are finite; a program needn't handle non-finite values.
Results may differ from a plain program's by a relative error of at most 0.0003.
Values sent between devices are 32-bit elements; how exact they have to be, the bound alone decides.
No kernel may reach another device: no remote copies, remote signals or barrier semaphores. Data moves between devices by JAX's collectives and lax.ppermute only.
A program may use at most 128 MiB of HBM per device.

v0:
```python
import jax
import jax.numpy as jnp
from jax import lax
from jax.sharding import PartitionSpec as P

cut_share = 0.3
exact = lax.Precision.HIGHEST


def padded_2(shard, sides, width):
    for axis, dim in sides:
        devices, length = (lax.axis_size(axis), shard.shape[dim])
        up = [(i, (i + 1) % devices) for i in range(devices)]
        down = [(j, i) for i, j in up]
        last = lax.slice_in_dim(shard, length - width, length, axis=dim)
        first = lax.slice_in_dim(shard, 0, width, axis=dim)
        before = lax.ppermute(last, axis, up)
        after = lax.ppermute(first, axis, down)
        shard = jnp.concatenate([before, shard, after], axis=dim)
    return shard


def merged(shard, axis, combine):
    everything = jax.tree.map(lambda part: lax.all_gather(part, axis), shard)
    first = jax.tree.map(lambda part: part[0], everything)

    def turn(k, so_far):
        return combine(so_far, jax.tree.map(lambda part: part[k], everything))

    return lax.fori_loop(1, lax.axis_size(axis), turn, first)


def coupling_blocks(couplings, index_rows):
    return jnp.take(couplings, index_rows, axis=0)


def apply_inner(padded, blocks_used, onsite, offset_rows):
    middle = padded[1:-1]
    lower_layers = padded[:-2]
    upper_layers = padded[2:]
    count = onsite.shape[1]
    site_ids = jnp.arange(count, dtype=jnp.int32)
    layer_ids = jnp.arange(middle.shape[0], dtype=jnp.int32)
    pieces = [middle]
    for slot in range(1, 7):
        if slot == 5:
            source = lower_layers
        elif slot == 6:
            source = upper_layers
        else:
            source = middle
        neighbour = (site_ids[None, :] + offset_rows[:, slot - 1, :]) % count
        pieces.append(source[layer_ids[:, None], neighbour])
    stacked = jnp.stack(pieces, axis=1)
    summed = jnp.einsum("lksij,lksjn->lsin", blocks_used, stacked, precision=exact)
    return summed + onsite[..., None] * middle


def extrema_of(couplings, onsite, index_rows):
    row_abs = jnp.sum(jnp.abs(couplings), axis=2)
    diag_all = jnp.diagonal(couplings, axis1=1, axis2=2)
    table_ids = jnp.arange(couplings.shape[0], dtype=jnp.int32)
    onehot = (index_rows[..., None] == table_ids).astype(jnp.float32)
    picked_abs = jnp.einsum("lksc,ci->lksi", onehot, row_abs, precision=exact)
    picked_diag = jnp.einsum("lsc,ci->lsi", onehot[:, 0], diag_all, precision=exact)
    centers = picked_diag + onsite
    radii = picked_abs[:, 0] - jnp.abs(picked_diag) + jnp.sum(picked_abs[:, 1:], axis=1)
    return (jnp.max(centers + radii), jnp.min(centers - radii))


def combine(first, second):
    return (jnp.maximum(first[0], second[0]), jnp.minimum(first[1], second[1]))


def faces(field):
    return padded_2(field, (("blk", 0),), 1)


def per_device(start_states, couplings, potential, site_offsets, coupling_index, degrees):
    upper, lower = merged(extrema_of(couplings, potential, coupling_index), "blk", combine)
    cut_edge = lower + cut_share * (upper - lower)
    middle_value = (upper + cut_edge) / 2.0
    half_width = (upper - cut_edge) / 2.0

    def scaled(applied, field):
        return (applied - middle_value * field) / half_width

    local_blocks = coupling_blocks(couplings, coupling_index)
    first_step = scaled(
        apply_inner(faces(start_states), local_blocks, potential, site_offsets), start_states
    )
    second = (
        2.0
        * scaled(apply_inner(faces(first_step), local_blocks, potential, site_offsets), first_step)
        - start_states
    )
    third = (
        2.0 * scaled(apply_inner(faces(second), local_blocks, potential, site_offsets), second)
        - first_step
    )
    chosen = jnp.where(degrees == 1, first_step, jnp.where(degrees == 2, second, third))
    regrouped = lax.all_to_all(chosen, "states", split_axis=1, concat_axis=3, tiled=True)
    rows = regrouped.reshape(-1, regrouped.shape[-1])
    partial_gram = lax.dot_general(
        rows, rows, (((0,), (0,)), ((), ())), precision=exact, preferred_element_type=jnp.float32
    )
    gram = lax.psum(partial_gram, ("blk", "states"))
    factor = jnp.linalg.cholesky(gram)
    identity = jnp.eye(gram.shape[0], dtype=jnp.float32)
    inverse_factor = jax.scipy.linalg.solve_triangular(factor, identity, lower=True)
    orthonormal = jnp.dot(
        rows, inverse_factor.T, precision=exact, preferred_element_type=jnp.float32
    )
    return orthonormal.reshape(regrouped.shape)


def solution(mesh):
    in_specs = (
        P("blk", None, None, "states"),
        P(),
        P("blk", None, None),
        P("blk", None, None),
        P("blk", None, None),
        P("states"),
    )
    out_specs = P("blk", "states", None, None)
    return jax.shard_map(
        per_device, mesh=mesh, in_specs=in_specs, out_specs=out_specs, check_vma=False
    )
```

profile of v0, /device:TPU:1, one launch (start us, length us, event | category | flops | bytes accessed | tf_op | source)
XLA Modules:
  0.0 655.3 jit_solution(10604853302595501179)
XLA Ops:
  9.7 5.1 collective-permute-start.1
  15.2 4.6 copy.33
  25.9 43.0 %all-reduce.3 = (f32[8]{0:T(128)S(1)}, f32[8]{0:T(128)S(1)}) all-reduce(f32[8]{0:T(128)S(1)} %dynamic-update-slice.23, f32[8]{0:T(128)S(1)} %dynamic-update-slice.24), channel_id=1, replica_groups=mesh['blk'=8,'states'=4] {'blk'}, use_global_device_ids=true, to_apply=%add.1 | all-reduce | flops 16 | bytes 128
  69.0 16.2 %while.18 = (s32[]{:T(128)}, f32[]{:T(128)}, f32[]{:T(128)}, f32[8]{0:T(128)S(1)}, f32[8]{0:T(128)S(1)}, /*index=5*/s32[]{:T(128)}, s32[]{:T(128)}, s32[]{:T(128)}) while((s32[]{:T(128)}, f32[]{:T(128)}, f32[]{:T(128)}, f32[8]{0:T(128)S(1)}, f32[8]{0:T(128)S(1)}, /*index=5*/s32[]{:T(128)}, s32[]{:T(128)}, s32[]{:T(128)}) %tuple.75), condition=%wide.region_5.6_spmd, body=%wide.region_4.5_spmd.sunk | while | flops 7 | bytes 175 | solution.py:30
  93.9 6.7 %gather_fusion = f32[224,128,128]{2,1,0:T(8,128)} fusion(f32[16,128,128]{2,1,0:T(8,128)S(1)} %copy-done, s32[1024]{0:T(1024)S(1)} %pad_clamp_fusion), kind=kCustom, calls=%fused_computation | custom fusion | bytes 29361024 | tf_op jit(solution)/shard_map/jit(_take)/gather | solution.py:34
  111.5 3.9 pad_maximum_fusion.4
  122.2 3.6 gather_fusion.6
  129.0 21.4 %bitcast_dynamic-update-slice_fusion.2 = (f32[2,7,16,128,128]{4,3,2,0,1:T(8,128)}, f32[2,16,128,128]{3,2,1,0:T(8,128)}) fusion(f32[]{:T(128)S(6)} %div.29, f32[2,16,128,128]{3,2,1,0:T(8,128)S(1)} %copy-done.1, f32[]{:T(128)S(6)} %div.28, f32[2,16,128]{2,1,0:T(8,128)S(1)} %copy-done.21, f32[2,7,16,128,128]{4,3,1,2,0:T(8,128)} %constant_dynamic-update-slice_fusion, ...), kind=kOutput, calls=%fused_computation.56 | convolution fusion | flops 5643436032 | bytes 35668200 | tf_op jit(solution)/shard_map/lksij,lksjn->lsin/dot_general | solution.py:55
  155.1 3.6 gather_fusion.8
  158.6 3.6 gather_fusion.9
  162.3 3.6 gather_fusion.10
  178.9 19.3 %collective-permute-done.3 = f32[1,16,128,128]{3,2,1,0:T(8,128)} collective-permute-done((f32[1,16,128,128]{3,2,1,0:T(8,128)}, f32[1,16,128,128]{3,2,1,0:T(8,128)}, u32[]{:S(2)}, u32[]{:S(2)}) %collective-permute-start.3) | collective-permute-done | bytes 1048608 | tf_op jit(solution)/shard_map/ppermute | solution.py:18
  198.1 4.0 pad_maximum_fusion.2
  202.2 3.6 gather_fusion.12
  214.2 21.6 %bitcast_dynamic-update-slice_fusion.1 = (f32[2,7,16,128,128]{4,3,2,0,1:T(8,128)}, f32[2,16,128,128]{3,2,1,0:T(8,128)}) fusion(f32[2,16,128,128]{3,2,1,0:T(8,128)S(1)} %copy-done.1, f32[]{:T(128)S(6)} %div.29, f32[2,16,128,128]{3,2,1,0:T(8,128)} %get-tuple-element.205, f32[]{:T(128)S(6)} %div.28, f32[2,16,128]{2,1,0:T(8,128)S(1)} %copy-done.21, ...), kind=kOutput, calls=%fused_computation.50 | convolution fusion | flops 5644484608 | bytes 37765352 | tf_op jit(solution)/shard_map/lksij,lksjn->lsin/dot_general | solution.py:55
  258.7 25.2 %collective-permute-done.5 = f32[1,16,128,128]{3,2,1,0:T(8,128)} collective-permute-done((f32[1,16,128,128]{3,2,1,0:T(8,128)}, f32[1,16,128,128]{3,2,1,0:T(8,128)}, u32[]{:S(2)}, u32[]{:S(2)}) %collective-permute-start.5) | collective-permute-done | bytes 1048608 | tf_op jit(solution)/shard_map/ppermute | solution.py:18
  285.9 4.0 pad_maximum_fusion
  293.6 3.6 gather_fusion.19
  302.8 21.2 %fusion.19 = f32[2,16,128,128]{3,2,1,0:T(8,128)} fusion(f32[2,16,128,128]{3,2,1,0:T(8,128)S(1)} %copy-done.3, f32[2,16,128,128]{3,2,1,0:T(8,128)S(1)} %copy-done.4, f32[2,7,16,128,128]{4,3,2,0,1:T(8,128)} %constant_dynamic-update-slice_fusion.12, f32[2,7,16,128,128]{4,3,2,1,0:T(8,128)} %bitcast.201, pred[2,7,16]{1,2,0:T(8,128)(4,1)S(1)} %copy.30, ...), kind=kOutput, calls=%fused_computation.49 | convolution fusion | flops 5645533184 | bytes 35668456 | tf_op jit(solution)/shard_map/lksij,lksjn->lsin/dot_general | solution.py:55
  325.8 29.1 %all_to_all.15 = f32[2,16,128,128]{3,2,0,1:T(8,128)S(1)} all-to-all(f32[2,16,128,128]{3,2,0,1:T(8,128)S(1)} %copy.39), channel_id=1, replica_groups=mesh['blk'=8,'states'=4] {'states'}, dimensions={1} | all-to-all | bytes 4194304 | tf_op jit(solution)/shard_map/all_to_all | solution.py:102
  356.3 4.5 fusion.11
  365.2 123.7 %all-reduce.6.cloned.1.call-done = f32[512,512]{0,1:T(8,128)} async-done(((f32[512,512]{0,1:T(8,128)}), f32[512,512]{0,1:T(8,128)}) %all-reduce.6.cloned.1.call-update) | async-done | bytes 1048592 | tf_op jit(solution)/shard_map/psum | solution.py:107
  494.0 11.7 %cholesky.104 = f32[128,128]{1,0:T(8,128)S(1)} custom-call(f32[128,128]{1,0:T(8,128)S(1)} %cholesky.266), custom_call_target="Cholesky" | custom-call | tf_op jit(solution)/shard_map/jit(cholesky)/cholesky | solution.py:108
  505.9 9.8 %custom-call.31 = f32[1,128,128]{1,2,0:T(8,128)S(1)} custom-call(f32[1,128,128]{2,1,0:T(8,128)S(1)} %get-tuple-element.195), custom_call_target="InvertDiagBlocksLowerTriangular" | custom-call | tf_op jit(solution)/shard_map/jit(cholesky)/cholesky | solution.py:108
  518.2 11.7 %cholesky.217 = f32[128,128]{1,0:T(8,128)S(1)} custom-call(f32[128,128]{1,0:T(8,128)S(1)} %cholesky.270), custom_call_target="Cholesky" | custom-call | tf_op jit(solution)/shard_map/jit(cholesky)/cholesky | solution.py:108
  530.0 10.0 %custom-call.32 = f32[1,128,128]{1,2,0:T(8,128)S(1)} custom-call(f32[1,128,128]{2,1,0:T(8,128)S(1)} %get-tuple-element.192), custom_call_target="InvertDiagBlocksLowerTriangular" | custom-call | tf_op jit(solution)/shard_map/jit(cholesky)/cholesky | solution.py:108
  541.5 11.7 %cholesky.238 = f32[128,128]{1,0:T(8,128)S(1)} custom-call(f32[128,128]{1,0:T(8,128)S(1)} %cholesky.275), custom_call_target="Cholesky" | custom-call | tf_op jit(solution)/shard_map/jit(cholesky)/cholesky | solution.py:108
  553.2 9.8 %custom-call.33 = f32[1,128,128]{1,2,0:T(8,128)S(1)} custom-call(f32[1,128,128]{2,1,0:T(8,128)S(1)} %get-tuple-element.189), custom_call_target="InvertDiagBlocksLowerTriangular" | custom-call | tf_op jit(solution)/shard_map/jit(cholesky)/cholesky | solution.py:108
  564.5 11.7 %cholesky.255 = f32[128,128]{1,0:T(8,128)S(1)} custom-call(f32[128,128]{1,0:T(8,128)S(1)} %convolution_subtract_fusion.5), custom_call_target="Cholesky" | custom-call | tf_op jit(solution)/shard_map/jit(cholesky)/cholesky | solution.py:108
  582.2 14.4 %while.19 = (s32[]{:T(128)}, f32[512,512]{1,0:T(8,128)}, s32[4,2]{0,1:T(2,128)S(1)}, f32[4,128,128]{2,1,0:T(8,128)}, s32[]{:T(128)}) while((s32[]{:T(128)}, f32[512,512]{1,0:T(8,128)}, s32[4,2]{0,1:T(2,128)S(1)}, f32[4,128,128]{2,1,0:T(8,128)}, s32[]{:T(128)}) %tuple.78), condition=%wide.while_cond, body=%wide.while_body.sunk | while | flops 2 | bytes 132205 | solution.py:110
  596.6 40.1 %custom-call.34 = f32[4,128,128]{1,2,0:T(8,128)S(1)} custom-call(f32[4,128,128]{2,1,0:T(8,128)} %get-tuple-element.147), custom_call_target="InvertDiagBlocksLowerTriangular" | custom-call | tf_op jit(solution)/shard_map/jit(_solve_triangular)/triangular_solve | solution.py:110
  643.4 4.8 fusion.30
  (184 shorter events, 150.2 us)
Async XLA Ops:
  6.5 8.3 %copy-start = (f32[16,128,128]{2,1,0:T(8,128)S(1)}, f32[16,128,128]{2,1,0:T(8,128)}, u32[]{:S(2)}) copy-start(f32[16,128,128]{2,1,0:T(8,128)} %param.9) | copy-start | bytes 3145732
  6.5 482.4 %all-reduce.6.cloned.1.call-start = ((), (), s32[]{:S(2)}) async-start(), calls=%async_computation.1 | async-start | bytes 2097152 | tf_op jit(solution)/shard_map/psum | solution.py:107
  9.7 101.8 %collective-permute-start.1 = (f32[1,16,128,128]{3,2,1,0:T(8,128)}, f32[1,16,128,128]{3,2,1,0:T(8,128)}, u32[]{:S(2)}, u32[]{:S(2)}) collective-permute-start(f32[1,16,128,128]{3,2,1,0:T(8,128)} %get-tuple-element.184), channel_id=1, source_target_pairs={{4,0},{8,4},{12,8},{16,12},{20,16},{24,20},{28,24},{0,28},{5,1},{9... | collective-permute-start | bytes 3145736 | tf_op jit(solution)/shard_map/ppermute | solution.py:18
  14.8 96.7 %collective-permute-start = (f32[1,16,128,128]{3,2,1,0:T(8,128)}, f32[1,16,128,128]{3,2,1,0:T(8,128)}, u32[]{:S(2)}, u32[]{:S(2)}) collective-permute-start(f32[1,16,128,128]{3,2,1,0:T(8,128)} %get-tuple-element.185), channel_id=1, source_target_pairs={{0,4},{4,8},{8,12},{12,16},{16,20},{20,24},{24,28},{28,0},{1,5},{5... | collective-permute-start | bytes 3145736 | tf_op jit(solution)/shard_map/ppermute | solution.py:17
  15.1 4.7 copy-start.22
  15.1 6.8 %copy-start.25 = (u32[32]{0:T(128)S(1)}, u32[32]{0:T(128)}, u32[]{:S(2)}) copy-start(u32[32]{0:T(128)} %constant.565) | copy-start | bytes 388
  15.2 7.4 %copy-start.21 = (f32[2,16,128]{2,1,0:T(8,128)S(1)}, f32[2,16,128]{2,1,0:T(8,128)}, u32[]{:S(2)}) copy-start(f32[2,16,128]{2,1,0:T(8,128)} %param.10) | copy-start | bytes 49156
  15.2 70.0 %copy-start.23 = (s32[2,6,16]{2,0,1:T(2,128)S(1)}, s32[2,6,16]{2,0,1:T(2,128)}, u32[]{:S(2)}) copy-start(s32[2,6,16]{2,0,1:T(2,128)} %param.11) | copy-start | bytes 2308
  15.2 70.1 %copy-start.1 = (f32[2,16,128,128]{3,2,1,0:T(8,128)S(1)}, f32[2,16,128,128]{3,2,1,0:T(8,128)}, u32[]{:S(2)}) copy-start(f32[2,16,128,128]{3,2,1,0:T(8,128)} %param.8) | copy-start | bytes 6291460
  100.7 2.3 copy-start.5
  103.0 2.3 copy-start.6
  105.4 2.3 copy-start.7
  107.7 2.3 copy-start.8
  153.2 44.9 %collective-permute-start.3 = (f32[1,16,128,128]{3,2,1,0:T(8,128)}, f32[1,16,128,128]{3,2,1,0:T(8,128)}, u32[]{:S(2)}, u32[]{:S(2)}) collective-permute-start(f32[1,16,128,128]{3,2,1,0:T(8,128)} %get-tuple-element.180), channel_id=1, source_target_pairs={{4,0},{8,4},{12,8},{16,12},{20,16},{24,20},{28,24},{0,28},{5,1},{9... | collective-permute-start | bytes 3145736 | tf_op jit(solution)/shard_map/ppermute | solution.py:18
  153.2 44.9 %collective-permute-start.2 = (f32[1,16,128,128]{3,2,1,0:T(8,128)S(1)}, f32[1,16,128,128]{3,2,1,0:T(8,128)}, u32[]{:S(2)}, u32[]{:S(2)}) collective-permute-start(f32[1,16,128,128]{3,2,1,0:T(8,128)S(1)} %get-tuple-element.181), channel_id=1, source_target_pairs={{0,4},{4,8},{8,12},{12,16},{16,20},{20,24},{24,28},{28,0},{1,5},{5... | collective-permute-start | bytes 3145736 | tf_op jit(solution)/shard_map/ppermute | solution.py:17
  169.4 3.3 copy-start.15
  172.7 2.3 copy-start.14
  175.1 2.3 copy-start.11
  177.4 20.7 %copy-start.2 = (f32[2,16,128,128]{3,2,1,0:T(8,128)S(1)}, f32[2,16,128,128]{3,2,1,0:T(8,128)}, u32[]{:S(2)}) copy-start(f32[2,16,128,128]{3,2,1,0:T(8,128)} %get-tuple-element.205) | copy-start | bytes 6291460
  209.4 3.3 copy-start.17
  235.8 5.3 copy-start.24
  235.8 5.3 copy-start.4
  239.1 44.8 %collective-permute-start.5 = (f32[1,16,128,128]{3,2,1,0:T(8,128)}, f32[1,16,128,128]{3,2,1,0:T(8,128)}, u32[]{:S(2)}, u32[]{:S(2)}) collective-permute-start(f32[1,16,128,128]{3,2,1,0:T(8,128)} %get-tuple-element.176), channel_id=1, source_target_pairs={{4,0},{8,4},{12,8},{16,12},{20,16},{24,20},{28,24},{0,28},{5,1},{9... | collective-permute-start | bytes 3145736 | tf_op jit(solution)/shard_map/ppermute | solution.py:18
  240.3 45.6 %collective-permute-start.4 = (f32[1,16,128,128]{3,2,1,0:T(8,128)}, f32[1,16,128,128]{3,2,1,0:T(8,128)}, u32[]{:S(2)}, u32[]{:S(2)}) collective-permute-start(f32[1,16,128,128]{3,2,1,0:T(8,128)} %get-tuple-element.177), channel_id=1, source_target_pairs={{0,4},{4,8},{8,12},{12,16},{16,20},{20,24},{24,28},{28,0},{1,5},{5... | collective-permute-start | bytes 3145736 | tf_op jit(solution)/shard_map/ppermute | solution.py:17
  249.2 3.3 copy-start.13
  252.5 2.3 copy-start.12
  254.8 2.3 copy-start.10
  297.1 3.3 copy-start.16
  300.5 2.3 copy-start.3
  356.3 4.5 copy-start.9
  488.9 2.6 copy-start.18
  582.2 57.4 %copy-start.19 = (f32[512,512]{1,0:T(8,128)S(1)}, f32[512,512]{1,0:T(8,128)}, u32[]{:S(2)}) copy-start(f32[512,512]{1,0:T(8,128)} %fusion.46) | copy-start | bytes 3145732
  (1 other events, 1.0 us)
Sparse Core Ops, SparseCore 0:
  361.0 127.9 all-reduce.5
where the time goes:
time: 661 us; the launch traced here: 655 us
  waiting for transfers between devices  170 us (26%)
  local copies, waits for them, and re-layouts  157 us (24%)
  other arithmetic  136 us (21%)
  matrix products  86.7 us (13%)
  blocking collectives  72.1 us (11%)
  between operations  16.7 us (3%)
  starting transfers between devices  8.95 us (1%)
  loops' own time  8.05 us (1%)
    psum x1, waiting for transfers between devices, per_device(): gram = lax.psum(partial_gram, ('blk', 'states'))  124 us
    another operation x14, other arithmetic, per_device(): factor = jnp.linalg.cholesky(gram)  78.6 us
    dot_general x3, matrix products, apply_inner(): jnp.einsum('lksij,lksjn->lsin', blocks_used, stacked, precision=exact)  64.3 us
    gather x18, local copies, waits for them, and re-layouts, apply_inner(): pieces.append(source[layer_ids[:, None], neighbour])  52 us
    unnamed x74, local copies, waits for them, and re-layouts  49.2 us
    ppermute x3, waiting for transfers between devices, padded_2(): after = lax.ppermute(first, axis, down)  44.5 us
    unnamed x1, blocking collectives  43 us
    another operation x3, other arithmetic, per_device(): jax.scipy.linalg.solve_triangular(factor, identity, lower=True)  41.4 us
  transfers between devices with their start and end apart: 7, of which 4 were waited for; matrix products, arithmetic and copies ran while one was open for 13% of the time, Pallas kernels for 0%

commit v1 on v0

v1 whole, which is shorter than its diff:
```python
import functools

import jax
import jax.numpy as jnp
import numpy as np
from jax import lax
from jax.experimental import pallas as pl
from jax.experimental.pallas import tpu as pltpu
from jax.sharding import Mesh
from jax.sharding import PartitionSpec as P

cut_share = 0.3
exact = lax.Precision.HIGHEST
f32 = jnp.float32
bf16 = jnp.bfloat16
pivots = 4
vmem_limit = 48 * 1024 * 1024
NT = (((1,), (1,)), ((), ()))
TN = (((0,), (0,)), ((), ()))


def vmem():
    return pl.BlockSpec(memory_space=pltpu.VMEM)


def smem():
    return pl.BlockSpec(memory_space=pltpu.SMEM)


def call(body, args, specs, out_shape, scratch=(), flops=0, moved=0):
    return pl.pallas_call(
        body,
        out_shape=out_shape,
        in_specs=specs,
        out_specs=jax.tree.map(lambda _: vmem(), out_shape),
        scratch_shapes=list(scratch),
        compiler_params=pltpu.CompilerParams(vmem_limit_bytes=vmem_limit),
        cost_estimate=pl.CostEstimate(flops=flops, bytes_accessed=moved, transcendentals=0),
    )(*args)


def halves(value):
    high = value.astype(bf16)
    return high, (value - high.astype(f32)).astype(bf16)


def swap(value, axis):
    return lax.ppermute(value, axis, [(0, 1), (1, 0)])


def turn_body(x_ref, v_ref, mine_b, mine_i, other_b, other_i):
    layers, sites, _, count = v_ref.shape
    half = count // 2
    x = x_ref[0]
    for j in range(layers):
        layer = x * (layers - 1) + (1 - 2 * x) * j

        def one(s, carry):
            turned = v_ref[layer, s].T
            first, second = turned[:half], turned[half:]
            mine = jnp.where(x == 0, first, second)
            other = jnp.where(x == 0, second, first)
            if j == 0:
                mine_b[s] = mine
                other_b[s] = other
            else:
                mine_i[j - 1, s] = mine
                other_i[j - 1, s] = other
            return carry

        lax.fori_loop(0, sites, one, 0, unroll=2)


def table_body(index_ref, coup_ref, pot_ref, table_ref, ends_ref, row_abs, diag):
    entries, orb, _ = coup_ref.shape
    rows = lax.broadcasted_iota(jnp.int32, (orb, orb), 0)
    cols = lax.broadcasted_iota(jnp.int32, (orb, orb), 1)

    def entry(c, carry):
        turned = coup_ref[c].T
        high, low = halves(turned)
        table_ref[c, :, :orb] = high
        table_ref[c, :, orb:] = low
        row_abs[c] = jnp.sum(jnp.abs(turned), axis=0, keepdims=True)
        diag[c] = jnp.sum(jnp.where(rows == cols, turned, 0.0), axis=0, keepdims=True)
        return carry

    lax.fori_loop(0, entries, entry, 0)
    layers, sites, _ = pot_ref.shape
    slots = index_ref.shape[0] // (layers * sites)

    def block(r, carry):
        top, low = carry
        layer, s = r // sites, lax.rem(r, sites)
        at = layer * slots * sites + s
        own = diag[index_ref[at]]
        center = own + pot_ref[layer, pl.ds(s, 1), :]
        radius = row_abs[index_ref[at]] - jnp.abs(own)
        for k in range(1, slots):
            radius = radius + row_abs[index_ref[at + k * sites]]
        return jnp.maximum(top, center + radius), jnp.maximum(low, radius - center)

    start = jnp.full((1, orb), -jnp.inf, f32)
    top, low = lax.fori_loop(0, layers * sites, block, (start, start))
    ends_ref[...] = jnp.concatenate(
        [jnp.broadcast_to(top, (4, orb)), jnp.broadcast_to(low, (4, orb))], axis=0
    )


def step_body(order, layers_out, total, n_src, has_prev, last, *refs):
    refs = list(refs)
    take = lambda count: [refs.pop(0) for _ in range(count)]
    (source_ref, entry_ref, x_ref) = take(3)
    table_ref, pot_ref, ends_ref = take(3)
    pieces = take(n_src)
    prevs = take(has_prev)
    degree_ref = take(1)[0] if last else None
    out_ref, split = take(2)

    lookup = {}
    for piece, chain_layers in zip(pieces, order, strict=True):
        for at, layer in enumerate(chain_layers):
            lookup[layer] = (piece, at)
    sites, half, orb = pieces[0].shape[1:]
    slots = source_ref.shape[0] // (total * sites)

    top = jnp.max(ends_ref[0:1, :], axis=1, keepdims=True)
    low = -jnp.max(ends_ref[4:5, :], axis=1, keepdims=True)
    cut_edge = low + cut_share * (top - low)
    middle = (top + cut_edge) / 2.0
    gain = (1.0 if has_prev == 0 else 2.0) / ((top - cut_edge) / 2.0)

    for layer, (piece, at) in lookup.items():

        def one(s, carry):
            high, low_part = halves(piece[at, s])
            split[layer * sites + s, :half, :] = high
            split[layer * sites + s, half:, :] = low_part
            return carry

        lax.fori_loop(0, sites, one, 0, unroll=4)

    for n, layer in enumerate(layers_out):
        piece, at = lookup[layer]

        def block(s, carry):
            row = (layer - 1) * sites + s
            left = [split[source_ref[row * slots + k]] for k in range(slots)]
            right = [table_ref[entry_ref[row * slots + k]] for k in range(slots)]
            both = jnp.dot(
                jnp.concatenate(left, axis=1),
                jnp.concatenate(right, axis=0),
                preferred_element_type=f32,
            )
            applied = both[:half, :orb] + (both[:half, orb:] + both[half:, :orb])
            field = piece[at, s]
            shift = pot_ref[pl.ds(row, 1), :] - middle
            result = (applied + shift * field) * gain
            if has_prev:
                before = prevs[0][n, s]
                result = result - before
            if last:
                degree = degree_ref[...]
                result = jnp.where(degree == 1, before, jnp.where(degree == 2, field, result))
                x = x_ref[0]
                share = out_ref.shape[3]
                own = layer <= total // 2
                place = layer - 1 if own else total - layer
                place = max(place - 1, 0)
                side = x if own else 1 - x
                out_ref[side, s // share, place, lax.rem(s, share)] = result
            else:
                out_ref[n, s] = result
            return carry

        lax.fori_loop(0, sites, block, 0, unroll=2)


def step(consts, pieces, order, layers_out, total, prevs, last_shape=None, degree=None):
    source, entry, x, table, pot, ends = consts
    sites, half, orb = pieces[0].shape[1:]
    last = last_shape is not None
    shape = last_shape if last else (len(layers_out), sites, half, orb)
    args = [source, entry, x, table, pot, ends, *pieces, *prevs] + ([degree] if last else [])
    specs = [smem()] * 3 + [vmem()] * (len(args) - 3)
    return call(
        functools.partial(step_body, order, layers_out, total, len(pieces), len(prevs), last),
        args,
        specs,
        jax.ShapeDtypeStruct(shape, f32),
        [pltpu.VMEM(((total + 2) * sites, 2 * half, orb), bf16)],
        flops=2 * len(layers_out) * sites * 7 * orb * 4 * half * 2 * orb,
        moved=4 * sites * half * orb * (total + 2 + len(layers_out)),
    )


def state_order(outer, states):
    return [a * states + b for b in range(states) for a in range(outer)]


def gram_body(outer, states, *refs):
    *pieces, gram_ref, high, low = refs
    width = pieces[0].shape[4]
    col = 0
    for piece in pieces:
        _, _, layers, share, half, _ = piece.shape
        for layer in range(layers):
            for s in range(share):
                for n, src in enumerate(state_order(outer, states)):
                    part = halves(piece[src // states, src % states, layer, s])
                    at = (slice(n * half, (n + 1) * half), slice(col, col + part[0].shape[1]))
                    high[at] = part[0]
                    low[at] = part[1]
                col += part[0].shape[1]
    count = high.shape[0]
    tile = gram_ref.shape[1]
    wide = 2 * tile
    place = 0
    blocks = {}
    for i in range(0, count, wide):
        for j in range(0, i + 1, wide):
            a = [r[i : i + wide, :] for r in (high, high, low)]
            b = [r[j : j + wide, :] for r in (high, low, high)]
            blocks[i, j] = lax.dot_general(
                jnp.concatenate(a, axis=1),
                jnp.concatenate(b, axis=1),
                NT,
                preferred_element_type=f32,
            )
    for i in range(0, count, tile):
        for j in range(0, i + 1, tile):
            block = blocks[i // wide * wide, j // wide * wide]
            gram_ref[place : place + tile, :] = block[
                i % wide : i % wide + tile, j % wide : j % wide + tile
            ]
            place += tile


def rows_body(outer, states, n_pieces, *refs):
    x_ref, *pieces, high, low = refs
    x = x_ref[0]
    chain = 0
    total = sum(p.shape[2] for p in pieces)
    for piece in pieces:
        _, _, layers, share, half, orb = piece.shape
        for layer in range(layers):
            natural = x * (total - 1) + (1 - 2 * x) * chain
            for s in range(share):
                parts = [
                    piece[src // states, src % states, layer, s]
                    for src in state_order(outer, states)
                ]
                turned = jnp.concatenate(parts, axis=0).T
                a, b = halves(turned)
                high[natural, s] = a
                low[natural, s] = b
            chain += 1


def mat_mul(a, b):
    rows, inner, cols = len(a), len(b), len(b[0])
    out = []
    for i in range(rows):
        line = []
        for j in range(cols):
            total = a[i][0] * b[0][j]
            for k in range(1, inner):
                total = total + a[i][k] * b[k][j]
            line.append(total)
        out.append(line)
    return out


def flip(a):
    return [list(line) for line in zip(*a, strict=True)]


def inverse_small(a):
    size = len(a)
    if size == 1:
        return [[1.0 / a[0][0]]]
    if size == 2:
        one = 1.0 / (a[0][0] * a[1][1] - a[0][1] * a[0][1])
        off = -(a[0][1] * one)
        return [[a[1][1] * one, off], [off, a[0][0] * one]]
    h = size // 2
    corner = [line[:h] for line in a[:h]]
    side = [line[h:] for line in a[:h]]
    rest = [line[h:] for line in a[h:]]
    ci = inverse_small(corner)
    c = mat_mul(ci, side)
    update = mat_mul(flip(side), c)
    schur = [[rest[i][j] - update[i][j] for j in range(size - h)] for i in range(size - h)]
    si = inverse_small(schur)
    off = [[-v for v in line] for line in mat_mul(c, si)]
    add = mat_mul(off, flip(c))
    first = [[ci[i][j] - add[i][j] for j in range(h)] for i in range(h)]
    return [first[i] + off[i] for i in range(h)] + [
        flip(off)[i] + si[i] for i in range(size - h)
    ]


def lower_inverse_small(a):
    size = len(a)
    low = [[None] * size for _ in range(size)]
    scale = [None] * size
    for j in range(size):
        d = a[j][j]
        for k in range(j):
            d = d - low[j][k] * low[j][k]
        scale[j] = lax.rsqrt(d)
        for i in range(j + 1, size):
            v = a[i][j]
            for k in range(j):
                v = v - low[i][k] * low[j][k]
            low[i][j] = v * scale[j]
    inv = [[None] * size for _ in range(size)]
    for i in range(size):
        inv[i][i] = scale[i]
        for j in range(i):
            v = low[i][j] * inv[j][j]
            for k in range(j + 1, i):
                v = v + low[i][k] * inv[k][j]
            inv[i][j] = -(v * scale[i])
    return inv


def lower_inverse(block_ref, out_ref):
    size = block_ref.shape[0]
    lanes = lax.broadcasted_iota(jnp.int32, (8, size), 1)
    subs = lax.broadcasted_iota(jnp.int32, (8, size), 0)
    rows = [block_ref[8 * g : 8 * g + 8, :] for g in range(size // 8)]
    shape = (8, size)
    for start in range(0, size, pivots):
        group, offset = divmod(start, 8)
        inside = (lanes >= start) & (lanes < start + pivots)
        here = rows[group]
        columns = {}
        for g in range(group, size // 8):
            columns[g] = [
                jnp.broadcast_to(rows[g][:, start + k : start + k + 1], shape)
                for k in range(pivots)
            ]
        corner = [
            [
                jnp.broadcast_to(columns[group][j][offset + i : offset + i + 1, :], shape)
                for j in range(pivots)
            ]
            for i in range(pivots)
        ]
        lines = [
            jnp.where(
                inside,
                jnp.where(lanes == start + k, 1.0, 0.0),
                jnp.broadcast_to(here[offset + k : offset + k + 1, :], shape),
            )
            for k in range(pivots)
        ]
        inv = inverse_small(corner)
        weights = [functools.reduce(jnp.add, [inv[k][m] * lines[m] for m in range(pivots)]) for k in range(pivots)]
        for g in range(group, size // 8):
            change = functools.reduce(
                jnp.add, [columns[g][k] * weights[k] for k in range(pivots)]
            )
            updated = jnp.where(inside, 0.0, rows[g]) - change
            if g == group:
                updated = jnp.where(subs >= offset + pivots, updated, rows[g])
            rows[g] = updated
        low = lower_inverse_small(corner)
        for r in range(pivots):
            line = functools.reduce(jnp.add, [low[r][k] * lines[k] for k in range(r + 1)])
            rows[group] = jnp.where(subs == offset + r, line, rows[group])
    for g in range(size // 8):
        out_ref[8 * g : 8 * g + 8, :] = jnp.where(lanes <= subs + 8 * g, rows[g], 0.0)


def finish_body(gram_ref, high_ref, low_ref, out_ref, work, diag, lower, panel, inv_high, inv_low):
    size = work.shape[0]
    tile = diag.shape[0]
    place = 0
    for i in range(0, size, tile):
        for j in range(0, i + 1, tile):
            block = gram_ref[place : place + tile, :]
            place += tile
            work[i : i + tile, j : j + tile] = block
            if i != j:
                work[j : j + tile, i : i + tile] = block.T
    cols = lax.broadcasted_iota(jnp.int32, (tile, size), 1)
    local = lax.broadcasted_iota(jnp.int32, (tile, size), 0)

    def outer(b, carry):
        at = pl.multiple_of(b * tile, tile)
        diag[...] = work[pl.ds(at, tile), pl.ds(at, tile)]
        lower_inverse(diag, lower)
        inside = (cols >= at) & (cols < at + tile)
        line = jnp.where(
            inside, jnp.where(cols - at == local, 1.0, 0.0), work[pl.ds(at, tile), :]
        )
        panel[...] = jnp.dot(lower[...], line, precision=exact, preferred_element_type=f32)
        kept = jnp.where(cols < at + tile, panel[...], 0.0)
        high, low = halves(kept)
        inv_high[pl.ds(at, tile), :] = high
        inv_low[pl.ds(at, tile), :] = low

        def trailing(i, carry):
            to = pl.multiple_of(i * tile, tile)
            change = lax.dot_general(
                panel[:, pl.ds(to, tile)], panel[...], TN, precision=exact, preferred_element_type=f32
            )
            work[pl.ds(to, tile), :] = jnp.where(inside, 0.0, work[pl.ds(to, tile), :]) - change
            return carry

        lax.fori_loop(b + 1, size // tile, trailing, 0)
        return carry

    lax.fori_loop(0, size // tile, outer, 0)

    layers, share, orb, _ = out_ref.shape

    def result(r, carry):
        layer, s = r // share, lax.rem(r, share)
        a, b = high_ref[layer, s], low_ref[layer, s]
        c, d = inv_high[...], inv_low[...]
        out_ref[layer, s] = lax.dot_general(
            a, c, NT, preferred_element_type=f32
        ) + (
            lax.dot_general(a, d, NT, preferred_element_type=f32)
            + lax.dot_general(b, c, NT, preferred_element_type=f32)
        )
        return carry

    lax.fori_loop(0, layers * share, result, 0)


def group_sum(value, axis_sets):
    if not axis_sets:
        return value
    axes, *rest = axis_sets
    count = lax.axis_size(axes)
    if count == 1:
        return group_sum(value, rest)
    if count > 8 or value.shape[0] % (8 * count):
        return group_sum(lax.psum(value, axes), rest)
    me = lax.axis_index(axes)
    share = value.shape[0] // count

    def piece(k):
        return lax.dynamic_slice_in_dim(value, lax.rem(me + k, count) * share, share, axis=0)

    total = piece(0)
    got = [
        lax.ppermute(piece(k), axes, [(i, (i + k) % count) for i in range(count)])
        for k in range(1, count)
    ]
    for part in got:
        total = total + part
    total = group_sum(total, rest)
    back = [
        lax.ppermute(total, axes, [(i, (i - k) % count) for i in range(count)])
        for k in range(1, count)
    ]
    out = jnp.zeros_like(value)
    out = lax.dynamic_update_slice_in_dim(out, total, me * share, axis=0)
    for k, part in enumerate(back, 1):
        out = lax.dynamic_update_slice_in_dim(out, part, lax.rem(me + k, count) * share, axis=0)
    return out


def per_device(start_states, couplings, potential, site_offsets, coupling_index, degrees):
    layers, sites, orb, count = start_states.shape
    half = count // 2
    total = 2 * layers
    x = lax.axis_index("x").astype(jnp.int32)
    x_arr = x[None]
    depth = lax.axis_size("z")
    states_axes = ("y", "c")
    states = lax.axis_size(states_axes)
    share = sites // states

    def z_move(value, near):
        pairs = []
        for z in range(depth):
            for xx in range(2):
                d = (1 if xx else -1) * (1 if near else -1)
                pairs.append((z * 2 + xx, (z + d) % depth * 2 + xx))
        return lax.ppermute(value, ("z", "x"), pairs)

    def chained(value):
        return jnp.where(x == 1, value[::-1], value)

    with jax.named_scope("prepare"):
        mine_b, mine_i, other_b, other_i = call(
            turn_body,
            (x_arr, start_states),
            [smem(), vmem()],
            [
                jax.ShapeDtypeStruct((sites, half, orb), f32),
                jax.ShapeDtypeStruct((layers - 1, sites, half, orb), f32),
                jax.ShapeDtypeStruct((sites, half, orb), f32),
                jax.ShapeDtypeStruct((layers - 1, sites, half, orb), f32),
            ],
            moved=4 * 2 * start_states.size,
        )
        far = z_move(mine_b, True)
        partner_b = swap(other_b, "x")
        near = z_move(partner_b, False)
        partner_i = swap(other_i, "x")

        indices = jnp.concatenate([site_offsets, coupling_index], axis=1)
        lists = jnp.concatenate(
            [chained(potential), chained(jnp.swapaxes(indices, 1, 2)).astype(f32)], axis=2
        )
        their_lists = swap(lists, "x")
        table, ends = call(
            table_body,
            (coupling_index.reshape(-1), couplings, potential),
            [smem(), vmem(), vmem()],
            [
                jax.ShapeDtypeStruct((couplings.shape[0], orb, 2 * orb), bf16),
                jax.ShapeDtypeStruct((8, orb), f32),
            ],
            [pltpu.VMEM((couplings.shape[0], 1, orb), f32)] * 2,
            moved=8 * couplings.size,
        )
        ends = jnp.maximum(ends, swap(ends, "x"))
        hop = 1
        while hop < depth:
            ends = jnp.maximum(
                ends, lax.ppermute(ends, "z", [(i, (i + hop) % depth) for i in range(depth)])
            )
            hop *= 2

        chain = jnp.concatenate([lists, their_lists[::-1]], axis=0)
        pot = chain[..., :orb].reshape(total * sites, orb)
        whole = chain[..., orb:].astype(jnp.int32)
        offsets, entry = whole[..., : site_offsets.shape[1]], whole[..., site_offsets.shape[1] :]
        layer_id = jnp.arange(1, total + 1, dtype=jnp.int32)[:, None, None]
        site_id = jnp.arange(sites, dtype=jnp.int32)[None, :, None]
        slots = entry.shape[2]
        one = 1 - 2 * x
        shifts = jnp.where(
            jnp.arange(slots) == slots - 2, -one, jnp.where(jnp.arange(slots) == slots - 1, one, 0)
        ).astype(jnp.int32)
        moved = jnp.concatenate([jnp.zeros_like(offsets[..., :1]), offsets], axis=2)
        source = (layer_id + shifts) * sites + (site_id + moved) % sites
        consts = (source.reshape(-1), entry.reshape(-1), x_arr, table, pot, ends)
        degree = lax.dynamic_slice_in_dim(degrees, x * half, half)
        degree = jnp.broadcast_to(degree[:, None], (half, orb))

    outside = [1, total]
    inside = list(range(2, total))
    near, far = near[None], far[None]
    first = [mine_b[None], mine_i, partner_i[::-1], partner_b[None]]
    first_order = [[1], list(range(2, layers + 1)), list(range(layers + 1, total)), [total]]
    with jax.named_scope("first"):
        in1 = step(consts, first, first_order, inside, total, [])
        out1 = step(consts, first + [near, far], first_order + [[0], [total + 1]], outside, total, [])
    order = [outside, inside]
    ends_order = [[0], [total + 1]]
    with jax.named_scope("second"):
        far1 = z_move(out1[0], True)
        near1 = z_move(out1[1], False)
        in0 = jnp.concatenate([mine_i, partner_i[::-1]], axis=0)
        out0 = jnp.concatenate([mine_b[None], partner_b[None]], axis=0)
        in2 = step(consts, [out1, in1], order, inside, total, [in0])
        out2 = step(
            consts, [out1, in1, near1[None], far1[None]], order + ends_order, outside, total, [out0]
        )
    with jax.named_scope("third"):
        far2 = z_move(out2[0], True)
        near2 = z_move(out2[1], False)
        in3 = step(
            consts, [out2, in2], order, inside, total, [in1],
            (2, states, layers - 1, share, half, orb), degree,
        )
        group = ("x",) + states_axes

        def regroup(value):
            flat = value.reshape((2 * states,) + value.shape[2:])
            return lax.all_to_all(flat, group, 0, 0, tiled=True).reshape(value.shape)

        in3 = regroup(in3)
        out3 = step(
            consts, [out2, in2, near2[None], far2[None]], order + ends_order, outside, total, [out1],
            (2, states, 1, share, half, orb), degree,
        )
        out3 = regroup(out3)
    pieces = [out3, in3]
    width = 2 * states * half
    depth_rows = layers * share * orb
    tiles = width // orb
    with jax.named_scope("gram"):
        gram = call(
            functools.partial(gram_body, 2, states),
            pieces,
            [vmem()] * 2,
            jax.ShapeDtypeStruct((tiles * (tiles + 1) // 2 * orb, orb), f32),
            [pltpu.VMEM((width, depth_rows), bf16)] * 2,
            flops=6 * width * width * depth_rows,
            moved=4 * width * depth_rows,
        )
        high, low = call(
            functools.partial(rows_body, 2, states, 2),
            (x_arr, *pieces),
            [smem()] + [vmem()] * 2,
            [jax.ShapeDtypeStruct((layers, share, orb, width), bf16)] * 2,
            moved=8 * width * depth_rows,
        )
        gram = group_sum(gram, [("c",), ("x", "y"), ("z",)])
    with jax.named_scope("finish"):
        return call(
            finish_body,
            (gram, high, low),
            [vmem()] * 3,
            jax.ShapeDtypeStruct((layers, share, orb, width), f32),
            [
                pltpu.VMEM((width, width), f32),
                pltpu.VMEM((orb, orb), f32),
                pltpu.VMEM((orb, orb), f32),
                pltpu.VMEM((orb, width), f32),
                pltpu.VMEM((width, width), bf16),
                pltpu.VMEM((width, width), bf16),
            ],
            flops=8 * width * width * depth_rows,
            moved=8 * width * depth_rows,
        )


def solution(mesh):
    blk, states = mesh.shape["blk"], mesh.shape["states"]
    grid = Mesh(
        np.asarray(mesh.devices).reshape(blk // 2, 2, states // 2, 2), ("z", "x", "y", "c")
    )
    b, s = ("z", "x"), ("y", "c")
    in_specs = (
        P(b, None, None, s),
        P(),
        P(b, None, None),
        P(b, None, None),
        P(b, None, None),
        P(s),
    )
    return jax.shard_map(
        per_device, mesh=grid, in_specs=in_specs, out_specs=P(b, s, None, None), check_vma=False
    )
```

time: 661 us -> 225 us (0.34)
  local copies, waits for them, and re-layouts: 157 us -> 7.57 us
  other arithmetic: 136 us -> 3.65 us
  waiting for transfers between devices: 170 us -> 81.3 us
  matrix products: 86.7 us -> 0 us
  Pallas kernels: 0 us -> 83.7 us
  blocking collectives: 72.1 us -> 0 us
  starting transfers between devices: 8.95 us -> 47.1 us
  between operations: 16.7 us -> 0.3 us
  loops' own time: 8.05 us -> 0 us
    psum x1 -> x0, waiting for transfers between devices: 124 us -> none  [per_device(): gram = lax.psum(partial_gram, ('blk', 'states'))]
    another operation x17 -> x0, other arithmetic: 120 us -> none  [the longest x14 78.6 us: per_device(): factor = jnp.linalg.cholesky(gram)]
    pallas_call x0 -> x11, Pallas kernels: none -> 83.7 us  [call(): pl.pallas_call(body, out_shape=out_shape, in_specs=specs, out_specs=jax.t...]
    dot_general x7 -> x0, matrix products: 74.6 us -> none  [the longest x3 64.3 us: apply_inner(): jnp.einsum('lksij,lksjn->lsin', blocks_used, stacked, precision=exact)]
    gather x20 -> x0, local copies, waits for them, and re-layouts: 60.5 us -> none  [the longest x18 52 us: apply_inner(): pieces.append(source[layer_ids[:, None], neighbour])]
    unnamed x1 -> x0, blocking collectives: 43 us -> none
    unnamed x74 -> x21, local copies, waits for them, and re-layouts: 49.2 us -> 6.44 us
    all_to_all x1 -> x0, blocking collectives: 29.1 us -> none  [per_device(): lax.all_to_all(chosen, 'states', split_axis=1, concat_axis=3, tiled=True)]
  transfers between devices with their start and end apart: 7 -> 28, of which waited for: 4 -> 21; matrix products, arithmetic and copies ran while one was open for 13% -> 1% of each run, Pallas kernels for 0% -> 11%
where the time goes in v1:
time: 225 us; the launch traced here: 224 us
  Pallas kernels  83.7 us (37%)
  waiting for transfers between devices  81.3 us (36%)
  starting transfers between devices  47.1 us (21%)
  local copies, waits for them, and re-layouts  7.57 us (3%)
  other arithmetic  3.65 us (2%)
    pallas_call x11, Pallas kernels, call(): pl.pallas_call(body, out_shape=out_shape, in_specs=specs, out_specs=jax.t...  83.7 us
    ppermute x6, waiting for transfers between devices, z_move(): return lax.ppermute(value, ('z', 'x'), pairs)  36.8 us
    all_to_all x2, waiting for transfers between devices, regroup(): return lax.all_to_all(flat, group, 0, 0, tiled=True).reshape(value.shape)  13.6 us
    ppermute x2, waiting for transfers between devices, per_device(): lax.ppermute(ends, 'z', [(i, (i + hop) % depth) for i in range(depth)])  13.2 us
    ppermute x7, starting transfers between devices, group_sum(): lax.ppermute(total, axes, [(i, (i - k) % count) for i in range(count)])  12.2 us
    ppermute x6, starting transfers between devices, z_move(): return lax.ppermute(value, ('z', 'x'), pairs)  12 us
    all_to_all x2, starting transfers between devices, regroup(): return lax.all_to_all(flat, group, 0, 0, tiled=True).reshape(value.shape)  10.9 us
    ppermute x7, waiting for transfers between devices, group_sum(): lax.ppermute(total, axes, [(i, (i - k) % count) for i in range(count)])  8.74 us
  transfers between devices with their start and end apart: 28, of which 21 were waited for; matrix products, arithmetic and copies ran while one was open for 1% of the time, Pallas kernels for 11%

profile of v1, /device:TPU:1, one launch (start us, length us, event | category | flops | bytes accessed | tf_op | source)
XLA Modules:
  0.0 223.7 jit_solution(423246479817124895)
XLA Ops:
  2.4 2.1 collective-permute-start
  7.2 3.0 %prepare.2 = (bf16[16,128,256]{2,1,0:T(8,128)(2,1)S(1)}, f32[8,128]{1,0:T(8,128)S(1)}) custom-call(s32[224]{0:T(256)S(1)} %reshape.73.index_ref, f32[16,128,128]{2,1,0:T(8,128)S(1)} %copy-done.1, f32[2,16,128]{2,1,0:T(8,128)S(1)} %copy-done.3), custom_call_target="tpu_custom_call" | custom-call | bytes 2097152 | tf_op jit(solution)/shard_map/prepare/pallas_call | solution.py:31
  12.8 2.4 %prepare.3 = (f32[16,64,128]{2,1,0:T(8,128)S(1)}, f32[1,16,64,128]{3,2,1,0:T(8,128)S(1)}, f32[16,64,128]{2,1,0:T(8,128)}, f32[1,16,64,128]{3,2,1,0:T(8,128)S(1)}) custom-call(s32[1]{0:T(128)} %bitcast.1.x_ref.refs_2_.refs_0_, f32[2,16,128,128]{3,2,1,0:T(8,128)S(1)} %copy-done), custom_call_target="tpu_custom_call" | custom-call | bytes 4194304 | tf_op jit(solution)/shard_map/prepare/pallas_call | solution.py:31
  16.6 3.5 %collective-permute-start.7 = (f32[16,64,128]{2,1,0:T(8,128)S(1)}, f32[16,64,128]{2,1,0:T(8,128)}, u32[]{:S(2)}, u32[]{:S(2)}) collective-permute-start(f32[16,64,128]{2,1,0:T(8,128)S(1)} %get-tuple-element.15), channel_id=1, source_target_pairs={{0,24},{4,12},{8,0},{12,20},{16,8},{20,28},{24,16},{28,4},{1,25},{... | collective-permute-start | bytes 1572872 | tf_op jit(solution)/shard_map/prepare/ppermute | solution.py:486
  20.3 10.0 %collective-permute-done.2 = f32[8,128]{1,0:T(8,128)S(1)} collective-permute-done((f32[8,128]{1,0:T(8,128)S(1)}, f32[8,128]{1,0:T(8,128)S(1)}, u32[]{:S(2)}, u32[]{:S(2)}) %collective-permute-start.2) | collective-permute-done | bytes 4128 | tf_op jit(solution)/shard_map/prepare/ppermute | solution.py:529
  30.4 3.2 %collective-permute-done.3 = f32[8,128]{1,0:T(8,128)S(1)} collective-permute-done((f32[8,128]{1,0:T(8,128)S(1)}, f32[8,128]{1,0:T(8,128)S(1)}, u32[]{:S(2)}, u32[]{:S(2)}) %collective-permute-start.3) | collective-permute-done | bytes 4128 | tf_op jit(solution)/shard_map/prepare/ppermute | solution.py:529
  33.8 1.7 collective-permute-start.6
  35.8 3.2 %collective-permute-done.4.refs_8_ = f32[1,16,64,128]{3,2,1,0:T(8,128)S(1)} collective-permute-done((f32[1,16,64,128]{3,2,1,0:T(8,128)S(1)}, f32[1,16,64,128]{3,2,1,0:T(8,128)S(1)}, u32[]{:S(2)}, u32[]{:S(2)}) %collective-permute-start.4) | collective-permute-done | bytes 524320 | tf_op jit(solution)/shard_map/prepare/ppermute | solution.py:48
  40.3 5.9 %first.3.refs_7_.refs_8_ = f32[2,16,64,128]{3,2,1,0:T(8,128)S(1)} custom-call(s32[448]{0:T(512)S(1)} %reshape.71.refs_0_, s32[448]{0:T(512)S(1)} %reshape.72.refs_1_, s32[1]{0:T(128)} %bitcast.1.x_ref.refs_2_.refs_0_, bf16[16,128,256]{2,1,0:T(8,128)(2,1)S(1)} %copy-done.5, f32[64,128]{1,0:T(8,128)S(1)} %bitcast.41, f32[8,128]{1,0:T(8,128)S(1)} %max.11.refs_5_, ...), custom_call_target="tpu_custom_call" | custom-call | flops 3758096384 | bytes 4194304 | tf_op jit(solution)/shard_map/first/pallas_call | solution.py:31
  46.3 6.7 %first.2.refs_6_.refs_10_ = f32[2,16,64,128]{3,2,1,0:T(8,128)S(1)} custom-call(s32[448]{0:T(512)S(1)} %reshape.71.refs_0_, s32[448]{0:T(512)S(1)} %reshape.72.refs_1_, s32[1]{0:T(128)} %bitcast.1.x_ref.refs_2_.refs_0_, bf16[16,128,256]{2,1,0:T(8,128)(2,1)S(1)} %copy-done.5, f32[64,128]{1,0:T(8,128)S(1)} %bitcast.42, f32[8,128]{1,0:T(8,128)S(1)} %max.11.refs_5_, ...), custom_call_target="tpu_custom_call" | custom-call | flops 3758096384 | bytes 4194304 | tf_op jit(solution)/shard_map/first/pallas_call | solution.py:31
  53.1 3.4 %collective-permute-start.9 = (f32[16,64,128]{2,1,0:T(8,128)S(1)}, f32[16,64,128]{2,1,0:T(8,128)S(1)}, u32[]{:S(2)}, u32[]{:S(2)}) collective-permute-start(f32[16,64,128]{2,1,0:T(8,128)S(1)} %get-tuple-element.25), channel_id=1, source_target_pairs={{0,24},{4,12},{8,0},{12,20},{16,8},{20,28},{24,16},{28,4},{1,25},{... | collective-permute-start | bytes 1572872 | tf_op jit(solution)/shard_map/second/ppermute | solution.py:486
  57.7 6.0 %second.3.refs_7_ = f32[2,16,64,128]{3,2,1,0:T(8,128)S(1)} custom-call(s32[448]{0:T(512)S(1)} %reshape.71.refs_0_, s32[448]{0:T(512)S(1)} %reshape.72.refs_1_, s32[1]{0:T(128)} %bitcast.1.x_ref.refs_2_.refs_0_, bf16[16,128,256]{2,1,0:T(8,128)(2,1)S(1)} %copy-done.5, f32[64,128]{1,0:T(8,128)S(1)} %bitcast.43, f32[8,128]{1,0:T(8,128)S(1)} %max.11.refs_5_, ...), custom_call_target="tpu_custom_call" | custom-call | flops 3758096384 | bytes 4194304 | tf_op jit(solution)/shard_map/second/pallas_call | solution.py:31
  63.7 2.1 collective-permute-done.9
  65.8 11.7 %collective-permute-done.8 = f32[16,64,128]{2,1,0:T(8,128)S(1)} collective-permute-done((f32[16,64,128]{2,1,0:T(8,128)S(1)}, f32[16,64,128]{2,1,0:T(8,128)S(1)}, u32[]{:S(2)}, u32[]{:S(2)}) %collective-permute-start.8) | collective-permute-done | bytes 524320 | tf_op jit(solution)/shard_map/second/ppermute | solution.py:486
  77.6 6.7 %second.2.refs_6_ = f32[2,16,64,128]{3,2,1,0:T(8,128)S(1)} custom-call(s32[448]{0:T(512)S(1)} %reshape.71.refs_0_, s32[448]{0:T(512)S(1)} %reshape.72.refs_1_, s32[1]{0:T(128)} %bitcast.1.x_ref.refs_2_.refs_0_, bf16[16,128,256]{2,1,0:T(8,128)(2,1)S(1)} %copy-done.5, f32[64,128]{1,0:T(8,128)S(1)} %bitcast.44, f32[8,128]{1,0:T(8,128)S(1)} %max.11.refs_5_, ...), custom_call_target="tpu_custom_call" | custom-call | flops 3758096384 | bytes 4194304 | tf_op jit(solution)/shard_map/second/pallas_call | solution.py:31
  84.4 7.1 %third.3 = f32[2,4,1,4,64,128]{5,4,3,2,1,0:T(8,128)} custom-call(s32[448]{0:T(512)S(1)} %reshape.71.refs_0_, s32[448]{0:T(512)S(1)} %reshape.72.refs_1_, s32[1]{0:T(128)} %bitcast.1.x_ref.refs_2_.refs_0_, bf16[16,128,256]{2,1,0:T(8,128)(2,1)S(1)} %copy-done.5, f32[64,128]{1,0:T(8,128)S(1)} %bitcast.45, f32[8,128]{1,0:T(8,128)S(1)} %max.11.refs_5_, ...), custom_call_target="tpu_custom_call" | custom-call | flops 3758096384 | bytes 4194304 | tf_op jit(solution)/shard_map/third/pallas_call | solution.py:31
  91.4 6.6 %all-to-all-start.1 = ((f32[8,1,4,64,128]{4,3,2,1,0:T(8,128)}), f32[8,1,4,64,128]{4,3,2,1,0:T(8,128)S(1)}, u32[]{:S(2)}, u32[]{:S(2)}) async-start(f32[8,1,4,64,128]{4,3,2,1,0:T(8,128)} %bitcast.19), calls=%async_computation.1 | async-start | bytes 2097152 | tf_op jit(solution)/shard_map/third/all_to_all | solution.py:580
  99.6 1.8 collective-permute-start.11
  101.4 12.0 %collective-permute-done.10 = f32[16,64,128]{2,1,0:T(8,128)S(1)} collective-permute-done((f32[16,64,128]{2,1,0:T(8,128)S(1)}, f32[16,64,128]{2,1,0:T(8,128)S(1)}, u32[]{:S(2)}, u32[]{:S(2)}) %collective-permute-start.10) | collective-permute-done | bytes 524320 | tf_op jit(solution)/shard_map/third/ppermute | solution.py:486
  113.4 11.0 %collective-permute-done.11 = f32[16,64,128]{2,1,0:T(8,128)S(1)} collective-permute-done((f32[16,64,128]{2,1,0:T(8,128)S(1)}, f32[16,64,128]{2,1,0:T(8,128)S(1)}, u32[]{:S(2)}, u32[]{:S(2)}) %collective-permute-start.11) | collective-permute-done | bytes 524320 | tf_op jit(solution)/shard_map/third/ppermute | solution.py:486
  124.4 7.7 %third.2 = f32[2,4,1,4,64,128]{5,4,3,2,1,0:T(8,128)} custom-call(s32[448]{0:T(512)S(1)} %reshape.71.refs_0_, s32[448]{0:T(512)S(1)} %reshape.72.refs_1_, s32[1]{0:T(128)} %bitcast.1.x_ref.refs_2_.refs_0_, bf16[16,128,256]{2,1,0:T(8,128)(2,1)S(1)} %copy-done.6, f32[64,128]{1,0:T(8,128)S(1)} %bitcast.46, f32[8,128]{1,0:T(8,128)S(1)} %max.11.refs_5_, ...), custom_call_target="tpu_custom_call" | custom-call | flops 3758096384 | bytes 4194304 | tf_op jit(solution)/shard_map/third/pallas_call | solution.py:31
  132.1 4.3 %all-to-all-start = ((f32[8,1,4,64,128]{4,3,2,1,0:T(8,128)}), f32[8,1,4,64,128]{4,3,2,1,0:T(8,128)S(1)}, u32[]{:S(2)}, u32[]{:S(2)}) async-start(f32[8,1,4,64,128]{4,3,2,1,0:T(8,128)} %bitcast.16), calls=%async_computation | async-start | bytes 2097152 | tf_op jit(solution)/shard_map/third/all_to_all | solution.py:580
  136.4 13.6 %all-to-all-done = f32[8,1,4,64,128]{4,3,2,1,0:T(8,128)S(1)} async-done(((f32[8,1,4,64,128]{4,3,2,1,0:T(8,128)}), f32[8,1,4,64,128]{4,3,2,1,0:T(8,128)S(1)}, u32[]{:S(2)}, u32[]{:S(2)}) %all-to-all-start) | async-done | bytes 1048608 | tf_op jit(solution)/shard_map/third/all_to_all | solution.py:580
  155.3 2.1 collective-permute-start.15
  158.6 1.9 collective-permute-done.15
  161.1 1.7 collective-permute-start.17
  162.8 1.6 collective-permute-start.18
  165.8 3.4 %collective-permute-start.19 = (f32[40,128]{1,0:T(8,128)S(1)}, f32[40,128]{1,0:T(8,128)S(1)}, u32[]{:S(2)}, u32[]{:S(2)}) collective-permute-start(f32[40,128]{1,0:T(8,128)S(1)} %get-tuple-element.22), channel_id=1, source_target_pairs={{0,24},{8,0},{16,8},{24,16},{1,25},{9,1},{17,9},{25,17},{2,26},{10... | collective-permute-start | bytes 61448 | tf_op jit(solution)/shard_map/gram/ppermute | solution.py:459
  170.1 2.6 %collective-permute-done.20 = f32[40,128]{1,0:T(8,128)S(1)} collective-permute-done((f32[40,128]{1,0:T(8,128)S(1)}, f32[40,128]{1,0:T(8,128)S(1)}, u32[]{:S(2)}, u32[]{:S(2)}) %collective-permute-start.20) | collective-permute-done | bytes 20512 | tf_op jit(solution)/shard_map/gram/ppermute | solution.py:459
  177.1 1.6 collective-permute-done.23
  180.2 6.1 %collective-permute-start.25 = (f32[640,128]{1,0:T(8,128)S(1)}, f32[640,128]{1,0:T(8,128)S(1)}, u32[]{:S(2)}, u32[]{:S(2)}) collective-permute-start(f32[640,128]{1,0:T(8,128)S(1)} %constant_dynamic-update-slice_fusion.2), channel_id=1, source_target_pairs={{0,1},{1,0},{2,3},{3,2},{4,5},{5,4},{6,7},{7,6},{8,9},{9,8},{10,11... | collective-permute-start | bytes 983048 | tf_op jit(solution)/shard_map/gram/ppermute | solution.py:459
  187.5 36.2 %finish.1 = f32[2,4,128,512]{3,2,1,0:T(8,128)} custom-call(f32[1280,128]{1,0:T(8,128)S(1)} %constant_dynamic-update-slice_fusion.gram_ref, bf16[2,4,128,512]{3,2,1,0:T(8,128)(2,1)S(1)} %get-tuple-element.19.high_ref, bf16[2,4,128,512]{3,2,1,0:T(8,128)(2,1)S(1)} %get-tuple-element.20.low_ref), custom_call_target="tpu_custom_call" | custom-call | flops 2147483648 | bytes 4194304 | tf_op jit(solution)/shard_map/finish/pallas_call | solution.py:31
  (101 shorter events, 30.5 us)
Async XLA Ops:
  0.0 30.4 %copy-start.9 = (s32[128]{0:T(128)S(1)}, s32[128]{0:T(128)}, u32[]{:S(2)}) copy-start(s32[128]{0:T(128)} %param.11) | copy-start | bytes 1540
  2.4 31.3 %collective-permute-start = (f32[2,16,141]{2,1,0:T(8,128)S(1)}, f32[2,16,141]{2,1,0:T(8,128)S(1)}, u32[]{:S(2)}, u32[]{:S(2)}) collective-permute-start(f32[2,16,141]{2,1,0:T(8,128)S(1)} %pad_maximum_fusion.3), channel_id=1, source_target_pairs={{0,4},{4,0},{1,5},{5,1},{2,6},{6,2},{3,7},{7,3},{8,12},{12,8},{9,1... | collective-permute-start | bytes 54152 | tf_op jit(solution)/shard_map/prepare/ppermute | solution.py:48
  11.2 9.0 %collective-permute-start.1 = (f32[8,128]{1,0:T(8,128)S(1)}, f32[8,128]{1,0:T(8,128)S(1)}, u32[]{:S(2)}, u32[]{:S(2)}) collective-permute-start(f32[8,128]{1,0:T(8,128)S(1)} %get-tuple-element.14), channel_id=1, source_target_pairs={{0,4},{4,0},{1,5},{5,1},{2,6},{6,2},{3,7},{7,3},{8,12},{12,8},{9,1... | collective-permute-start | bytes 12296 | tf_op jit(solution)/shard_map/prepare/ppermute | solution.py:48
  15.1 18.6 %collective-permute-start.5 = (f32[16,64,128]{2,1,0:T(8,128)}, f32[16,64,128]{2,1,0:T(8,128)S(1)}, u32[]{:S(2)}, u32[]{:S(2)}) collective-permute-start(f32[16,64,128]{2,1,0:T(8,128)} %get-tuple-element.18), channel_id=1, source_target_pairs={{0,4},{4,0},{1,5},{5,1},{2,6},{6,2},{3,7},{7,3},{8,12},{12,8},{9,1... | collective-permute-start | bytes 1572872 | tf_op jit(solution)/shard_map/prepare/ppermute | solution.py:48
  16.6 22.5 %collective-permute-start.4 = (f32[1,16,64,128]{3,2,1,0:T(8,128)S(1)}, f32[1,16,64,128]{3,2,1,0:T(8,128)S(1)}, u32[]{:S(2)}, u32[]{:S(2)}) collective-permute-start(f32[1,16,64,128]{3,2,1,0:T(8,128)S(1)} %get-tuple-element.17), channel_id=1, source_target_pairs={{0,4},{4,0},{1,5},{5,1},{2,6},{6,2},{3,7},{7,3},{8,12},{12,8},{9,1... | collective-permute-start | bytes 1572872 | tf_op jit(solution)/shard_map/prepare/ppermute | solution.py:48
  16.6 29.6 %collective-permute-start.7 = (f32[16,64,128]{2,1,0:T(8,128)S(1)}, f32[16,64,128]{2,1,0:T(8,128)}, u32[]{:S(2)}, u32[]{:S(2)}) collective-permute-start(f32[16,64,128]{2,1,0:T(8,128)S(1)} %get-tuple-element.15), channel_id=1, source_target_pairs={{0,24},{4,12},{8,0},{12,20},{16,8},{20,28},{24,16},{28,4},{1,25},{... | collective-permute-start | bytes 1572872 | tf_op jit(solution)/shard_map/prepare/ppermute | solution.py:486
  20.2 10.1 %collective-permute-start.2 = (f32[8,128]{1,0:T(8,128)S(1)}, f32[8,128]{1,0:T(8,128)S(1)}, u32[]{:S(2)}, u32[]{:S(2)}) collective-permute-start(f32[8,128]{1,0:T(8,128)S(1)} %max.9), channel_id=1, source_target_pairs={{0,8},{8,16},{16,24},{24,0},{1,9},{9,17},{17,25},{25,1},{2,10},{10... | collective-permute-start | bytes 12296 | tf_op jit(solution)/shard_map/prepare/ppermute | solution.py:529
  30.3 3.4 %collective-permute-start.3 = (f32[8,128]{1,0:T(8,128)S(1)}, f32[8,128]{1,0:T(8,128)S(1)}, u32[]{:S(2)}, u32[]{:S(2)}) collective-permute-start(f32[8,128]{1,0:T(8,128)S(1)} %max.10), channel_id=1, source_target_pairs={{0,16},{8,24},{16,0},{24,8},{1,17},{9,25},{17,1},{25,9},{2,18},{10... | collective-permute-start | bytes 12296 | tf_op jit(solution)/shard_map/prepare/ppermute | solution.py:529
  33.8 12.5 %collective-permute-start.6 = (f32[16,64,128]{2,1,0:T(8,128)S(1)}, f32[16,64,128]{2,1,0:T(8,128)}, u32[]{:S(2)}, u32[]{:S(2)}) collective-permute-start(f32[16,64,128]{2,1,0:T(8,128)S(1)} %collective-permute-done.5), channel_id=1, source_target_pairs={{0,8},{4,28},{8,16},{12,4},{16,24},{20,12},{24,0},{28,20},{1,9},{5... | collective-permute-start | bytes 1572872 | tf_op jit(solution)/shard_map/prepare/ppermute | solution.py:486
  53.0 24.6 %copy-start.2 = (f32[2,16,64,128]{3,2,1,0:T(8,128)}, f32[2,16,64,128]{3,2,1,0:T(8,128)S(1)}, u32[]{:S(2)}) copy-start(f32[2,16,64,128]{3,2,1,0:T(8,128)S(1)} %first.2.refs_6_.refs_10_) | copy-start | bytes 3145732
  53.1 12.7 %collective-permute-start.9 = (f32[16,64,128]{2,1,0:T(8,128)S(1)}, f32[16,64,128]{2,1,0:T(8,128)S(1)}, u32[]{:S(2)}, u32[]{:S(2)}) collective-permute-start(f32[16,64,128]{2,1,0:T(8,128)S(1)} %get-tuple-element.25), channel_id=1, source_target_pairs={{0,24},{4,12},{8,0},{12,20},{16,8},{20,28},{24,16},{28,4},{1,25},{... | collective-permute-start | bytes 1572872 | tf_op jit(solution)/shard_map/second/ppermute | solution.py:486
  56.6 21.0 %collective-permute-start.8 = (f32[16,64,128]{2,1,0:T(8,128)S(1)}, f32[16,64,128]{2,1,0:T(8,128)S(1)}, u32[]{:S(2)}, u32[]{:S(2)}) collective-permute-start(f32[16,64,128]{2,1,0:T(8,128)S(1)} %get-tuple-element.26), channel_id=1, source_target_pairs={{0,8},{4,28},{8,16},{12,4},{16,24},{20,12},{24,0},{28,20},{1,9},{5... | collective-permute-start | bytes 1572872 | tf_op jit(solution)/shard_map/second/ppermute | solution.py:486
  91.4 40.7 %all-to-all-start.1 = ((f32[8,1,4,64,128]{4,3,2,1,0:T(8,128)}), f32[8,1,4,64,128]{4,3,2,1,0:T(8,128)S(1)}, u32[]{:S(2)}, u32[]{:S(2)}) async-start(f32[8,1,4,64,128]{4,3,2,1,0:T(8,128)} %bitcast.19), calls=%async_computation.1 | async-start | bytes 2097152 | tf_op jit(solution)/shard_map/third/all_to_all | solution.py:580
  98.0 26.4 %copy-start.6 = (bf16[16,128,256]{2,1,0:T(8,128)(2,1)S(1)}, bf16[16,128,256]{2,1,0:T(8,128)(2,1)}, u32[]{:S(2)}) copy-start(bf16[16,128,256]{2,1,0:T(8,128)(2,1)} %copy-done.4) | copy-start | bytes 3145732
  98.0 26.4 %copy-start.8 = (f32[2,16,64,128]{3,2,1,0:T(8,128)S(1)}, f32[2,16,64,128]{3,2,1,0:T(8,128)}, u32[]{:S(2)}) copy-start(f32[2,16,64,128]{3,2,1,0:T(8,128)} %copy-done.7) | copy-start | bytes 3145732
  98.1 15.3 %collective-permute-start.10 = (f32[16,64,128]{2,1,0:T(8,128)S(1)}, f32[16,64,128]{2,1,0:T(8,128)S(1)}, u32[]{:S(2)}, u32[]{:S(2)}) collective-permute-start(f32[16,64,128]{2,1,0:T(8,128)S(1)} %get-tuple-element.24), channel_id=1, source_target_pairs={{0,8},{4,28},{8,16},{12,4},{16,24},{20,12},{24,0},{28,20},{1,9},{5... | collective-permute-start | bytes 1572872 | tf_op jit(solution)/shard_map/third/ppermute | solution.py:486
  99.6 24.7 %collective-permute-start.11 = (f32[16,64,128]{2,1,0:T(8,128)S(1)}, f32[16,64,128]{2,1,0:T(8,128)S(1)}, u32[]{:S(2)}, u32[]{:S(2)}) collective-permute-start(f32[16,64,128]{2,1,0:T(8,128)S(1)} %get-tuple-element.23), channel_id=1, source_target_pairs={{0,24},{4,12},{8,0},{12,20},{16,8},{20,28},{24,16},{28,4},{1,25},{... | collective-permute-start | bytes 1572872 | tf_op jit(solution)/shard_map/third/ppermute | solution.py:486
  132.1 17.9 %all-to-all-start = ((f32[8,1,4,64,128]{4,3,2,1,0:T(8,128)}), f32[8,1,4,64,128]{4,3,2,1,0:T(8,128)S(1)}, u32[]{:S(2)}, u32[]{:S(2)}) async-start(f32[8,1,4,64,128]{4,3,2,1,0:T(8,128)} %bitcast.16), calls=%async_computation | async-start | bytes 2097152 | tf_op jit(solution)/shard_map/third/all_to_all | solution.py:580
  151.5 2.2 collective-permute-start.12
  153.8 4.6 %collective-permute-start.13 = (f32[160,128]{1,0:T(8,128)S(1)}, f32[160,128]{1,0:T(8,128)S(1)}, u32[]{:S(2)}, u32[]{:S(2)}) collective-permute-start(f32[160,128]{1,0:T(8,128)S(1)} %get-tuple-element.27), channel_id=1, source_target_pairs={{0,2},{2,4},{4,6},{6,0},{1,3},{3,5},{5,7},{7,1},{8,10},{10,12},{12... | collective-permute-start | bytes 245768 | tf_op jit(solution)/shard_map/gram/ppermute | solution.py:452
  155.0 3.6 %collective-permute-start.14 = (f32[160,128]{1,0:T(8,128)S(1)}, f32[160,128]{1,0:T(8,128)S(1)}, u32[]{:S(2)}, u32[]{:S(2)}) collective-permute-start(f32[160,128]{1,0:T(8,128)S(1)} %get-tuple-element.29), channel_id=1, source_target_pairs={{0,4},{2,6},{4,0},{6,2},{1,5},{3,7},{5,1},{7,3},{8,12},{10,14},{12... | collective-permute-start | bytes 245768 | tf_op jit(solution)/shard_map/gram/ppermute | solution.py:452
  155.3 5.2 %collective-permute-start.15 = (f32[160,128]{1,0:T(8,128)S(1)}, f32[160,128]{1,0:T(8,128)S(1)}, u32[]{:S(2)}, u32[]{:S(2)}) collective-permute-start(f32[160,128]{1,0:T(8,128)S(1)} %get-tuple-element.28), channel_id=1, source_target_pairs={{0,6},{2,0},{4,2},{6,4},{1,7},{3,1},{5,3},{7,5},{8,14},{10,8},{12,... | collective-permute-start | bytes 245768 | tf_op jit(solution)/shard_map/gram/ppermute | solution.py:452
  160.6 4.5 %collective-permute-start.16 = (f32[40,128]{1,0:T(8,128)S(1)}, f32[40,128]{1,0:T(8,128)S(1)}, u32[]{:S(2)}, u32[]{:S(2)}) collective-permute-start(f32[40,128]{1,0:T(8,128)S(1)} %get-tuple-element.30), channel_id=1, source_target_pairs={{0,8},{8,16},{16,24},{24,0},{1,9},{9,17},{17,25},{25,1},{2,10},{10... | collective-permute-start | bytes 61448 | tf_op jit(solution)/shard_map/gram/ppermute | solution.py:452
  161.1 3.9 %collective-permute-start.17 = (f32[40,128]{1,0:T(8,128)S(1)}, f32[40,128]{1,0:T(8,128)S(1)}, u32[]{:S(2)}, u32[]{:S(2)}) collective-permute-start(f32[40,128]{1,0:T(8,128)S(1)} %get-tuple-element.32), channel_id=1, source_target_pairs={{0,16},{8,24},{16,0},{24,8},{1,17},{9,25},{17,1},{25,9},{2,18},{10... | collective-permute-start | bytes 61448 | tf_op jit(solution)/shard_map/gram/ppermute | solution.py:452
  162.8 2.9 %collective-permute-start.18 = (f32[40,128]{1,0:T(8,128)S(1)}, f32[40,128]{1,0:T(8,128)S(1)}, u32[]{:S(2)}, u32[]{:S(2)}) collective-permute-start(f32[40,128]{1,0:T(8,128)S(1)} %get-tuple-element.31), channel_id=1, source_target_pairs={{0,24},{8,0},{16,8},{24,16},{1,25},{9,1},{17,9},{25,17},{2,26},{10... | collective-permute-start | bytes 61448 | tf_op jit(solution)/shard_map/gram/ppermute | solution.py:452
  165.8 4.3 %collective-permute-start.19 = (f32[40,128]{1,0:T(8,128)S(1)}, f32[40,128]{1,0:T(8,128)S(1)}, u32[]{:S(2)}, u32[]{:S(2)}) collective-permute-start(f32[40,128]{1,0:T(8,128)S(1)} %get-tuple-element.22), channel_id=1, source_target_pairs={{0,24},{8,0},{16,8},{24,16},{1,25},{9,1},{17,9},{25,17},{2,26},{10... | collective-permute-start | bytes 61448 | tf_op jit(solution)/shard_map/gram/ppermute | solution.py:459
  169.2 3.5 %collective-permute-start.20 = (f32[40,128]{1,0:T(8,128)S(1)}, f32[40,128]{1,0:T(8,128)S(1)}, u32[]{:S(2)}, u32[]{:S(2)}) collective-permute-start(f32[40,128]{1,0:T(8,128)S(1)} %get-tuple-element.22), channel_id=1, source_target_pairs={{0,16},{8,24},{16,0},{24,8},{1,17},{9,25},{17,1},{25,9},{2,18},{10... | collective-permute-start | bytes 61448 | tf_op jit(solution)/shard_map/gram/ppermute | solution.py:459
  169.2 4.6 %collective-permute-start.21 = (f32[40,128]{1,0:T(8,128)S(1)}, f32[40,128]{1,0:T(8,128)S(1)}, u32[]{:S(2)}, u32[]{:S(2)}) collective-permute-start(f32[40,128]{1,0:T(8,128)S(1)} %get-tuple-element.22), channel_id=1, source_target_pairs={{0,8},{8,16},{16,24},{24,0},{1,9},{9,17},{17,25},{25,1},{2,10},{10... | collective-permute-start | bytes 61448 | tf_op jit(solution)/shard_map/gram/ppermute | solution.py:459
  173.8 3.3 %collective-permute-start.22 = (f32[160,128]{1,0:T(8,128)S(1)}, f32[160,128]{1,0:T(8,128)S(1)}, u32[]{:S(2)}, u32[]{:S(2)}) collective-permute-start(f32[160,128]{1,0:T(8,128)S(1)} %constant_dynamic-update-slice_fusion.6), channel_id=1, source_target_pairs={{0,6},{2,0},{4,2},{6,4},{1,7},{3,1},{5,3},{7,5},{8,14},{10,8},{12,... | collective-permute-start | bytes 245768 | tf_op jit(solution)/shard_map/gram/ppermute | solution.py:459
  174.5 4.2 %collective-permute-start.23 = (f32[160,128]{1,0:T(8,128)S(1)}, f32[160,128]{1,0:T(8,128)S(1)}, u32[]{:S(2)}, u32[]{:S(2)}) collective-permute-start(f32[160,128]{1,0:T(8,128)S(1)} %constant_dynamic-update-slice_fusion.6), channel_id=1, source_target_pairs={{0,4},{2,6},{4,0},{6,2},{1,5},{3,7},{5,1},{7,3},{8,12},{10,14},{12... | collective-permute-start | bytes 245768 | tf_op jit(solution)/shard_map/gram/ppermute | solution.py:459
  176.0 4.2 %collective-permute-start.24 = (f32[160,128]{1,0:T(8,128)S(1)}, f32[160,128]{1,0:T(8,128)S(1)}, u32[]{:S(2)}, u32[]{:S(2)}) collective-permute-start(f32[160,128]{1,0:T(8,128)S(1)} %constant_dynamic-update-slice_fusion.6), channel_id=1, source_target_pairs={{0,2},{2,4},{4,6},{6,0},{1,3},{3,5},{5,7},{7,1},{8,10},{10,12},{12... | collective-permute-start | bytes 245768 | tf_op jit(solution)/shard_map/gram/ppermute | solution.py:459
  180.2 7.3 %collective-permute-start.25 = (f32[640,128]{1,0:T(8,128)S(1)}, f32[640,128]{1,0:T(8,128)S(1)}, u32[]{:S(2)}, u32[]{:S(2)}) collective-permute-start(f32[640,128]{1,0:T(8,128)S(1)} %constant_dynamic-update-slice_fusion.2), channel_id=1, source_target_pairs={{0,1},{1,0},{2,3},{3,2},{4,5},{5,4},{6,7},{7,6},{8,9},{9,8},{10,11... | collective-permute-start | bytes 983048 | tf_op jit(solution)/shard_map/gram/ppermute | solution.py:459
  (6 other events, 26.5 us)

commit v2 on v1

--- a/solution.py
+++ b/solution.py
@@ -15,6 +15,8 @@
 bf16 = jnp.bfloat16
 pivots = 4
 vmem_limit = 48 * 1024 * 1024
+small = pl.CostEstimate(flops=1, bytes_accessed=1, transcendentals=0)
+large = pl.CostEstimate(flops=2 * 10**11, bytes_accessed=1, transcendentals=0)
 NT = (((1,), (1,)), ((), ()))
 TN = (((0,), (0,)), ((), ()))
 
@@ -27,16 +29,21 @@
     return pl.BlockSpec(memory_space=pltpu.SMEM)
 
 
-def call(body, args, specs, out_shape, scratch=(), flops=0, moved=0):
+def call(body, args, specs, out_shape, scratch=(), after=(), cost=small):
+    skipped = len(after)
+
+    def kernel(*refs):
+        body(*refs[: len(args)], *refs[len(args) + skipped :])
+
     return pl.pallas_call(
-        body,
+        kernel,
         out_shape=out_shape,
-        in_specs=specs,
+        in_specs=[*specs, *[pl.BlockSpec(memory_space=pl.ANY)] * skipped],
         out_specs=jax.tree.map(lambda _: vmem(), out_shape),
         scratch_shapes=list(scratch),
         compiler_params=pltpu.CompilerParams(vmem_limit_bytes=vmem_limit),
-        cost_estimate=pl.CostEstimate(flops=flops, bytes_accessed=moved, transcendentals=0),
-    )(*args)
+        cost_estimate=cost,
+    )(*args, *after)
 
 
 def halves(value):
@@ -44,31 +51,82 @@
     return high, (value - high.astype(f32)).astype(bf16)
 
 
+def hold(value, *after):
+    def kernel(*refs):
+        pass
+
+    return pl.pallas_call(
+        kernel,
+        out_shape=jax.ShapeDtypeStruct(value.shape, value.dtype),
+        in_specs=[pl.BlockSpec(memory_space=pl.ANY)] * (1 + len(after)),
+        out_specs=pl.BlockSpec(memory_space=pl.ANY),
+        input_output_aliases={0: 0},
+        cost_estimate=small,
+    )(value, *after)
+
+
 def swap(value, axis):
     return lax.ppermute(value, axis, [(0, 1), (1, 0)])
 
 
-def turn_body(x_ref, v_ref, mine_b, mine_i, other_b, other_i):
+def turn_body(first, x_ref, v_ref, *refs):
+    mine, other = refs[-2:]
     layers, sites, _, count = v_ref.shape
     half = count // 2
     x = x_ref[0]
+    for j in range(mine.shape[0]):
+        layer = x * (layers - 1) + (1 - 2 * x) * (first + j) if layers > 1 else 0
+
+        def one(s, carry):
+            turned = v_ref[layer, s].T
+            low, high = turned[:half], turned[half:]
+            mine[j, s] = jnp.where(x == 0, low, high)
+            other[j, s] = jnp.where(x == 0, high, low)
+            return carry
+
+        lax.fori_loop(0, sites, one, 0, unroll=4)
+
+
+def turn_first(x_arr, states):
+    layers, sites, orb, count = states.shape
+
+    def kernel(x_ref, v_ref, mine, other, mark):
+        turn_body(0, x_ref, v_ref, mine, other)
+        mark[...] = jnp.zeros_like(mark)
+
+    shape = (1, sites, count // 2, orb)
+    return pl.pallas_call(
+        kernel,
+        out_shape=[jax.ShapeDtypeStruct(shape, f32)] * 2 + [jax.ShapeDtypeStruct((8, orb), f32)],
+        grid_spec=pltpu.PrefetchScalarGridSpec(
+            num_scalar_prefetch=1,
+            grid=(1,),
+            in_specs=[
+                pl.BlockSpec((1, sites, orb, count), lambda i, x: (x[0] * (layers - 1), 0, 0, 0))
+            ],
+            out_specs=[pl.BlockSpec(shape, lambda i, x: (0, 0, 0, 0))] * 2
+            + [pl.BlockSpec((8, orb), lambda i, x: (0, 0))],
+        ),
+        compiler_params=pltpu.CompilerParams(vmem_limit_bytes=vmem_limit),
+        cost_estimate=small,
+    )(x_arr, states)
+
+
+def mark_body(out_ref):
+    out_ref[...] = jnp.zeros_like(out_ref)
+
+
+def lists_body(x_ref, pot_ref, offset_ref, entry_ref, out_ref):
+    layers, sites, _ = pot_ref.shape
+    x = x_ref[0]
+    out_ref[...] = jnp.zeros_like(out_ref)
     for j in range(layers):
         layer = x * (layers - 1) + (1 - 2 * x) * j
-
-        def one(s, carry):
-            turned = v_ref[layer, s].T
-            first, second = turned[:half], turned[half:]
-            mine = jnp.where(x == 0, first, second)
-            other = jnp.where(x == 0, second, first)
-            if j == 0:
-                mine_b[s] = mine
-                other_b[s] = other
-            else:
-                mine_i[j - 1, s] = mine
-                other_i[j - 1, s] = other
-            return carry
-
-        lax.fori_loop(0, sites, one, 0, unroll=2)
+        out_ref[j, :sites, :] = pot_ref[layer]
+        row = sites
+        for ref in (offset_ref, entry_ref):
+            out_ref[j, row : row + ref.shape[1], :sites] = ref[layer].astype(f32)
+            row += 8
 
 
 def table_body(index_ref, coup_ref, pot_ref, table_ref, ends_ref, row_abs, diag):
@@ -107,33 +165,46 @@
     )
 
 
-def step_body(order, layers_out, total, n_src, has_prev, last, *refs):
+def step_body(order, layers_out, total, number, last, *refs):
     refs = list(refs)
     take = lambda count: [refs.pop(0) for _ in range(count)]
     (source_ref, entry_ref, x_ref) = take(3)
-    table_ref, pot_ref, ends_ref = take(3)
-    pieces = take(n_src)
-    prevs = take(has_prev)
+    table_ref, pot_ref = take(2)
+    pieces = take(len(order))
+    ends_ref = take(1)[0] if number > 1 else None
+    starts = take(len(order)) if number == 2 else []
+    prev = take(1)[0] if number == 3 else None
     degree_ref = take(1)[0] if last else None
-    out_ref, split = take(2)
-
-    lookup = {}
-    for piece, chain_layers in zip(pieces, order, strict=True):
+    split = refs.pop()
+    scaled = refs.pop() if number == 2 else None
+    out_ref = refs.pop() if not last else refs[-1]
+
+    lookup, before_of = {}, {}
+    for n, chain_layers in enumerate(order):
         for at, layer in enumerate(chain_layers):
-            lookup[layer] = (piece, at)
+            lookup[layer] = (pieces[n], at)
+            before_of[layer] = (starts[n], at) if starts else None
     sites, half, orb = pieces[0].shape[1:]
     slots = source_ref.shape[0] // (total * sites)
 
-    top = jnp.max(ends_ref[0:1, :], axis=1, keepdims=True)
-    low = -jnp.max(ends_ref[4:5, :], axis=1, keepdims=True)
-    cut_edge = low + cut_share * (top - low)
-    middle = (top + cut_edge) / 2.0
-    gain = (1.0 if has_prev == 0 else 2.0) / ((top - cut_edge) / 2.0)
-
-    for layer, (piece, at) in lookup.items():
+    if number > 1:
+        top = jnp.max(ends_ref[0:1, :], axis=1, keepdims=True)
+        low = -jnp.max(ends_ref[4:5, :], axis=1, keepdims=True)
+        cut_edge = low + cut_share * (top - low)
+        middle = (top + cut_edge) / 2.0
+        gain = 1.0 / ((top - cut_edge) / 2.0)
+
+    def field_at(layer, s):
+        piece, at = lookup[layer]
+        if number != 2:
+            return piece[at, s]
+        start, at = before_of[layer]
+        return (piece[at, s] - middle * start[at, s]) * gain
+
+    for layer in lookup:
 
         def one(s, carry):
-            high, low_part = halves(piece[at, s])
+            high, low_part = halves(field_at(layer, s))
             split[layer * sites + s, :half, :] = high
             split[layer * sites + s, half:, :] = low_part
             return carry
@@ -141,7 +212,6 @@
         lax.fori_loop(0, sites, one, 0, unroll=4)
 
     for n, layer in enumerate(layers_out):
-        piece, at = lookup[layer]
 
         def block(s, carry):
             row = (layer - 1) * sites + s
@@ -153,65 +223,83 @@
                 preferred_element_type=f32,
             )
             applied = both[:half, :orb] + (both[:half, orb:] + both[half:, :orb])
-            field = piece[at, s]
-            shift = pot_ref[pl.ds(row, 1), :] - middle
-            result = (applied + shift * field) * gain
-            if has_prev:
-                before = prevs[0][n, s]
-                result = result - before
+            field = field_at(layer, s)
+            shift = pot_ref[pl.ds(row, 1), :]
+            if number == 1:
+                result = applied + shift * field
+            else:
+                start, start_at = before_of[layer] or (prev, n)
+                before = start[start_at, s]
+                result = (applied + (shift - middle) * field) * (2.0 * gain) - before
+            if number == 2:
+                scaled[n, s] = field
             if last:
                 degree = degree_ref[...]
                 result = jnp.where(degree == 1, before, jnp.where(degree == 2, field, result))
-                x = x_ref[0]
                 share = out_ref.shape[3]
                 own = layer <= total // 2
-                place = layer - 1 if own else total - layer
-                place = max(place - 1, 0)
-                side = x if own else 1 - x
+                place = max((layer - 1 if own else total - layer) - 1, 0)
+                side = (x_ref[0] if own else 1 - x_ref[0]) if out_ref.shape[0] == 2 else 0
                 out_ref[side, s // share, place, lax.rem(s, share)] = result
             else:
                 out_ref[n, s] = result
             return carry
 
-        lax.fori_loop(0, sites, block, 0, unroll=2)
-
-
-def step(consts, pieces, order, layers_out, total, prevs, last_shape=None, degree=None):
-    source, entry, x, table, pot, ends = consts
+        lax.fori_loop(0, sites, block, 0, unroll=4)
+
+
+def step(consts, pieces, order, layers_out, total, more=(), last_shape=None, number=1, after=(), cost=small, into=None):
     sites, half, orb = pieces[0].shape[1:]
     last = last_shape is not None
     shape = last_shape if last else (len(layers_out), sites, half, orb)
-    args = [source, entry, x, table, pot, ends, *pieces, *prevs] + ([degree] if last else [])
-    specs = [smem()] * 3 + [vmem()] * (len(args) - 3)
-    return call(
-        functools.partial(step_body, order, layers_out, total, len(pieces), len(prevs), last),
-        args,
-        specs,
-        jax.ShapeDtypeStruct(shape, f32),
-        [pltpu.VMEM(((total + 2) * sites, 2 * half, orb), bf16)],
-        flops=2 * len(layers_out) * sites * 7 * orb * 4 * half * 2 * orb,
-        moved=4 * sites * half * orb * (total + 2 + len(layers_out)),
-    )
-
-
-def state_order(outer, states):
-    return [a * states + b for b in range(states) for a in range(outer)]
-
-
-def gram_body(outer, states, *refs):
-    *pieces, gram_ref, high, low = refs
-    width = pieces[0].shape[4]
+    args = [*consts, *pieces, *more]
+    scratch = [pltpu.VMEM(((total + 2) * sites, 2 * half, orb), bf16)]
+    body = functools.partial(step_body, order, layers_out, total, number, last)
+    out = jax.ShapeDtypeStruct(shape, f32)
+    one_side = last and len(layers_out) == 1
+    if not one_side:
+        specs = [smem()] * 3 + [vmem()] * (len(args) - 3)
+        return call(body, args, specs, [out, out] if number == 2 else out, scratch, after, cost)
+    own = layers_out[0] == 1
+    extra = [*after] + ([into] if into is not None else [])
+    count = len(args)
+
+    def kernel(*refs):
+        body(*refs[:count], *refs[count + len(extra) :])
+
+    zeros = (0,) * (len(shape) - 1)
+    return pl.pallas_call(
+        kernel,
+        out_shape=out,
+        grid_spec=pltpu.PrefetchScalarGridSpec(
+            num_scalar_prefetch=3,
+            grid=(1,),
+            in_specs=[vmem()] * (count - 3) + [pl.BlockSpec(memory_space=pl.ANY)] * len(extra),
+            out_specs=pl.BlockSpec(
+                (1, *shape[1:]), lambda i, a, b, x: (x[0] if own else 1 - x[0], *zeros)
+            ),
+            scratch_shapes=scratch,
+        ),
+        input_output_aliases={count + len(after): 0} if into is not None else {},
+        compiler_params=pltpu.CompilerParams(vmem_limit_bytes=vmem_limit),
+        cost_estimate=cost,
+    )(*args, *extra)
+
+
+def all_states(edge_ref, inner_ref, chain, s):
+    ref, layer = (edge_ref, 0) if chain == 0 else (inner_ref, chain - 1)
+    return [ref[a, b, layer, s] for b in range(ref.shape[1]) for a in range(2)]
+
+
+def gram_body(edge_ref, inner_ref, gram_ref, high, low):
+    _, _, inner_layers, share, half, orb = inner_ref.shape
     col = 0
-    for piece in pieces:
-        _, _, layers, share, half, _ = piece.shape
-        for layer in range(layers):
-            for s in range(share):
-                for n, src in enumerate(state_order(outer, states)):
-                    part = halves(piece[src // states, src % states, layer, s])
-                    at = (slice(n * half, (n + 1) * half), slice(col, col + part[0].shape[1]))
-                    high[at] = part[0]
-                    low[at] = part[1]
-                col += part[0].shape[1]
+    for chain in range(inner_layers + 1):
+        for s in range(share):
+            for n, part in enumerate(all_states(edge_ref, inner_ref, chain, s)):
+                at = (slice(n * half, (n + 1) * half), slice(col, col + orb))
+                high[at], low[at] = halves(part)
+            col += orb
     count = high.shape[0]
     tile = gram_ref.shape[1]
     wide = 2 * tile
@@ -236,25 +324,16 @@
             place += tile
 
 
-def rows_body(outer, states, n_pieces, *refs):
-    x_ref, *pieces, high, low = refs
+def rows_body(x_ref, edge_ref, inner_ref, high, low):
     x = x_ref[0]
-    chain = 0
-    total = sum(p.shape[2] for p in pieces)
-    for piece in pieces:
-        _, _, layers, share, half, orb = piece.shape
-        for layer in range(layers):
-            natural = x * (total - 1) + (1 - 2 * x) * chain
-            for s in range(share):
-                parts = [
-                    piece[src // states, src % states, layer, s]
-                    for src in state_order(outer, states)
-                ]
-                turned = jnp.concatenate(parts, axis=0).T
-                a, b = halves(turned)
-                high[natural, s] = a
-                low[natural, s] = b
-            chain += 1
+    layers, share = high.shape[:2]
+    for chain in range(layers):
+        natural = x * (layers - 1) + (1 - 2 * x) * chain
+        for s in range(share):
+            parts = all_states(edge_ref, inner_ref, chain, s)
+            a, b = halves(jnp.concatenate(parts, axis=0).T)
+            high[natural, s] = a
+            low[natural, s] = b
 
 
 def mat_mul(a, b):
@@ -374,7 +453,17 @@
         out_ref[8 * g : 8 * g + 8, :] = jnp.where(lanes <= subs + 8 * g, rows[g], 0.0)
 
 
-def finish_body(gram_ref, high_ref, low_ref, out_ref, work, diag, lower, panel, inv_high, inv_low):
+def three(left, right):
+    a, b = halves(left)
+    c, d = halves(right)
+    return jnp.dot(
+        jnp.concatenate([a, a, b], axis=1),
+        jnp.concatenate([c, d, c], axis=0),
+        preferred_element_type=f32,
+    )
+
+
+def finish_body(gram_ref, high_ref, low_ref, out_ref, work, diag, lower, panel, inv):
     size = work.shape[0]
     tile = diag.shape[0]
     place = 0
@@ -396,17 +485,15 @@
         line = jnp.where(
             inside, jnp.where(cols - at == local, 1.0, 0.0), work[pl.ds(at, tile), :]
         )
-        panel[...] = jnp.dot(lower[...], line, precision=exact, preferred_element_type=f32)
+        panel[...] = three(lower[...], line)
         kept = jnp.where(cols < at + tile, panel[...], 0.0)
         high, low = halves(kept)
-        inv_high[pl.ds(at, tile), :] = high
-        inv_low[pl.ds(at, tile), :] = low
+        inv[pl.ds(at, tile), :size] = high
+        inv[pl.ds(at, tile), size:] = low
 
         def trailing(i, carry):
             to = pl.multiple_of(i * tile, tile)
-            change = lax.dot_general(
-                panel[:, pl.ds(to, tile)], panel[...], TN, precision=exact, preferred_element_type=f32
-            )
+            change = three(panel[:, pl.ds(to, tile)].T, panel[...])
             work[pl.ds(to, tile), :] = jnp.where(inside, 0.0, work[pl.ds(to, tile), :]) - change
             return carry
 
@@ -417,19 +504,24 @@
 
     layers, share, orb, _ = out_ref.shape
 
-    def result(r, carry):
-        layer, s = r // share, lax.rem(r, share)
-        a, b = high_ref[layer, s], low_ref[layer, s]
-        c, d = inv_high[...], inv_low[...]
-        out_ref[layer, s] = lax.dot_general(
-            a, c, NT, preferred_element_type=f32
-        ) + (
-            lax.dot_general(a, d, NT, preferred_element_type=f32)
-            + lax.dot_general(b, c, NT, preferred_element_type=f32)
-        )
+    def result(s, carry):
+        a = jnp.concatenate([high_ref[n, s] for n in range(layers)], axis=0)
+        b = jnp.concatenate([low_ref[n, s] for n in range(layers)], axis=0)
+        for first in range(0, size, 2 * tile):
+            last = first + 2 * tile
+            c = inv[first:last, :last]
+            d = inv[first:last, size : size + last]
+            total = lax.dot_general(
+                jnp.concatenate([a[:, :last], a[:, :last], b[:, :last]], axis=1),
+                jnp.concatenate([c, d, c], axis=1),
+                NT,
+                preferred_element_type=f32,
+            )
+            for n in range(layers):
+                out_ref[n, s, :, first:last] = total[n * orb : (n + 1) * orb]
         return carry
 
-    lax.fori_loop(0, layers * share, result, 0)
+    lax.fori_loop(0, share, result, 0)
 
 
 def group_sum(value, axis_sets):
@@ -439,6 +531,12 @@
     count = lax.axis_size(axes)
     if count == 1:
         return group_sum(value, rest)
+    if not rest and count & (count - 1) == 0:
+        hop = 1
+        while hop < count:
+            value = value + lax.ppermute(value, axes, [(i, i ^ hop) for i in range(count)])
+            hop *= 2
+        return value
     if count > 8 or value.shape[0] % (8 * count):
         return group_sum(lax.psum(value, axes), rest)
     me = lax.axis_index(axes)
@@ -485,32 +583,26 @@
                 pairs.append((z * 2 + xx, (z + d) % depth * 2 + xx))
         return lax.ppermute(value, ("z", "x"), pairs)
 
-    def chained(value):
-        return jnp.where(x == 1, value[::-1], value)
-
     with jax.named_scope("prepare"):
-        mine_b, mine_i, other_b, other_i = call(
-            turn_body,
+        mine_b, other_b, mark = turn_first(x_arr, start_states)
+        far = z_move(mine_b, True)
+        partner_b = swap(other_b, "x")
+        mark = swap(mark, "c")
+        lists = call(
+            lists_body,
+            (x_arr, potential, site_offsets, coupling_index),
+            [smem(), vmem(), vmem(), vmem()],
+            jax.ShapeDtypeStruct((layers, sites + 16, orb), f32),
+            after=(mine_b,),
+        )
+        their_lists = swap(lists, "x")
+        mine_i, other_i = call(
+            functools.partial(turn_body, 1),
             (x_arr, start_states),
             [smem(), vmem()],
-            [
-                jax.ShapeDtypeStruct((sites, half, orb), f32),
-                jax.ShapeDtypeStruct((layers - 1, sites, half, orb), f32),
-                jax.ShapeDtypeStruct((sites, half, orb), f32),
-                jax.ShapeDtypeStruct((layers - 1, sites, half, orb), f32),
-            ],
-            moved=4 * 2 * start_states.size,
-        )
-        far = z_move(mine_b, True)
-        partner_b = swap(other_b, "x")
-        near = z_move(partner_b, False)
-        partner_i = swap(other_i, "x")
-
-        indices = jnp.concatenate([site_offsets, coupling_index], axis=1)
-        lists = jnp.concatenate(
-            [chained(potential), chained(jnp.swapaxes(indices, 1, 2)).astype(f32)], axis=2
-        )
-        their_lists = swap(lists, "x")
+            [jax.ShapeDtypeStruct((layers - 1, sites, half, orb), f32)] * 2,
+            after=(mine_b,),
+        )
         table, ends = call(
             table_body,
             (coupling_index.reshape(-1), couplings, potential),
@@ -520,20 +612,19 @@
                 jax.ShapeDtypeStruct((8, orb), f32),
             ],
             [pltpu.VMEM((couplings.shape[0], 1, orb), f32)] * 2,
-            moved=8 * couplings.size,
-        )
-        ends = jnp.maximum(ends, swap(ends, "x"))
-        hop = 1
-        while hop < depth:
-            ends = jnp.maximum(
-                ends, lax.ppermute(ends, "z", [(i, (i + hop) % depth) for i in range(depth)])
-            )
-            hop *= 2
-
+            after=(mark,),
+        )
+        partner_b = hold(partner_b, far, table)
+        devices = 2 * depth
+        ends = jnp.broadcast_to(ends[None], (devices, *ends.shape))
+        ends = jnp.max(lax.all_to_all(ends, ("z", "x"), 0, 0, tiled=True), axis=0)
+        near = z_move(partner_b, False)
+        partner_i = swap(hold(other_i, partner_b), "x")
         chain = jnp.concatenate([lists, their_lists[::-1]], axis=0)
-        pot = chain[..., :orb].reshape(total * sites, orb)
-        whole = chain[..., orb:].astype(jnp.int32)
-        offsets, entry = whole[..., : site_offsets.shape[1]], whole[..., site_offsets.shape[1] :]
+        pot = chain[:, :sites].reshape(total * sites, orb)
+        whole = jnp.swapaxes(chain[:, sites:, :sites], 1, 2).astype(jnp.int32)
+        offsets = whole[..., : site_offsets.shape[1]]
+        entry = whole[..., 8 : 8 + coupling_index.shape[1]]
         layer_id = jnp.arange(1, total + 1, dtype=jnp.int32)[:, None, None]
         site_id = jnp.arange(sites, dtype=jnp.int32)[None, :, None]
         slots = entry.shape[2]
@@ -543,68 +634,86 @@
         ).astype(jnp.int32)
         moved = jnp.concatenate([jnp.zeros_like(offsets[..., :1]), offsets], axis=2)
         source = (layer_id + shifts) * sites + (site_id + moved) % sites
-        consts = (source.reshape(-1), entry.reshape(-1), x_arr, table, pot, ends)
+        consts = (source.reshape(-1), entry.reshape(-1), x_arr, table, pot)
         degree = lax.dynamic_slice_in_dim(degrees, x * half, half)
         degree = jnp.broadcast_to(degree[:, None], (half, orb))
 
-    outside = [1, total]
     inside = list(range(2, total))
-    near, far = near[None], far[None]
-    first = [mine_b[None], mine_i, partner_i[::-1], partner_b[None]]
-    first_order = [[1], list(range(2, layers + 1)), list(range(layers + 1, total)), [total]]
+
+    def sent_after(value):
+        mark = call(mark_body, (), [], jax.ShapeDtypeStruct((8, orb), f32), after=(value,))
+        return swap(mark, "c")
+    group = ("x",) + states_axes
+
+    def regroup(value, axes):
+        flat = value.reshape((-1,) + value.shape[2:])
+        return lax.all_to_all(flat, axes, 0, 0, tiled=True).reshape(value.shape)
+
+    own_order, their_order = list(range(2, layers + 1)), list(range(layers + 1, total))
+    theirs = partner_i[::-1]
     with jax.named_scope("first"):
-        in1 = step(consts, first, first_order, inside, total, [])
-        out1 = step(consts, first + [near, far], first_order + [[0], [total + 1]], outside, total, [])
-    order = [outside, inside]
-    ends_order = [[0], [total + 1]]
+        four1 = step(
+            consts, [partner_b, theirs, far], [[total], their_order, [total + 1]], [total], total,
+            after=(ends,),
+        )
+        near1 = z_move(four1, False)
+        one1 = step(consts, [mine_b, mine_i, near], [[1], own_order, [0]], [1], total, after=(four1,))
+        far1 = z_move(one1, True)
+        in1 = step(
+            consts, [mine_b, mine_i, theirs, partner_b], [[1], own_order, their_order, [total]],
+            inside, total, after=(one1,),
+        )
+    start_in = jnp.concatenate([mine_i, theirs], axis=0)
     with jax.named_scope("second"):
-        far1 = z_move(out1[0], True)
-        near1 = z_move(out1[1], False)
-        in0 = jnp.concatenate([mine_i, partner_i[::-1]], axis=0)
-        out0 = jnp.concatenate([mine_b[None], partner_b[None]], axis=0)
-        in2 = step(consts, [out1, in1], order, inside, total, [in0])
-        out2 = step(
-            consts, [out1, in1, near1[None], far1[None]], order + ends_order, outside, total, [out0]
-        )
+        one2, one1s = step(
+            consts, [one1, in1, near1], [[1], inside, [0]], [1], total,
+            [ends, mine_b, start_in, near], number=2,
+        )
+        far2 = z_move(one2, True)
+        in2, in1s = step(
+            consts, [one1, in1, four1], [[1], inside, [total]], inside, total,
+            [ends, mine_b, start_in, partner_b], number=2, after=(sent_after(one2),),
+        )
+        four2, four1 = step(
+            consts, [four1, in1, far1], [[total], inside, [total + 1]], [total], total,
+            [ends, partner_b, start_in, far], number=2, after=(in2,),
+        )
+    in1 = in1s
     with jax.named_scope("third"):
-        far2 = z_move(out2[0], True)
-        near2 = z_move(out2[1], False)
-        in3 = step(
-            consts, [out2, in2], order, inside, total, [in1],
-            (2, states, layers - 1, share, half, orb), degree,
-        )
-        group = ("x",) + states_axes
-
-        def regroup(value):
-            flat = value.reshape((2 * states,) + value.shape[2:])
-            return lax.all_to_all(flat, group, 0, 0, tiled=True).reshape(value.shape)
-
-        in3 = regroup(in3)
+        near2 = z_move(four2, False)
+        in3_local = step(
+            consts, [one2, in2, four2], [[1], inside, [total]], inside, total,
+            [ends, in1, degree], (2, states, layers - 1, share, half, orb), number=3,
+            after=(sent_after(four2),),
+        )
+        in3 = regroup(in3_local, group)
+        edge_shape = (2, states, 1, share, half, orb)
+        four3 = step(
+            consts, [four2, in2, far2], [[total], inside, [total + 1]], [total], total,
+            [ends, four1, degree], edge_shape, number=3, after=(in3_local,),
+        )
         out3 = step(
-            consts, [out2, in2, near2[None], far2[None]], order + ends_order, outside, total, [out1],
-            (2, states, 1, share, half, orb), degree,
-        )
-        out3 = regroup(out3)
-    pieces = [out3, in3]
+            consts, [one2, in2, near2], [[1], inside, [0]], [1], total,
+            [ends, one1s, degree], edge_shape, number=3, cost=large, into=four3,
+        )
+        out3 = regroup(out3, group)
+    pieces = (out3, in3)
     width = 2 * states * half
     depth_rows = layers * share * orb
     tiles = width // orb
     with jax.named_scope("gram"):
         gram = call(
-            functools.partial(gram_body, 2, states),
+            gram_body,
             pieces,
             [vmem()] * 2,
             jax.ShapeDtypeStruct((tiles * (tiles + 1) // 2 * orb, orb), f32),
             [pltpu.VMEM((width, depth_rows), bf16)] * 2,
-            flops=6 * width * width * depth_rows,
-            moved=4 * width * depth_rows,
         )
         high, low = call(
-            functools.partial(rows_body, 2, states, 2),
+            rows_body,
             (x_arr, *pieces),
             [smem()] + [vmem()] * 2,
             [jax.ShapeDtypeStruct((layers, share, orb, width), bf16)] * 2,
-            moved=8 * width * depth_rows,
         )
         gram = group_sum(gram, [("c",), ("x", "y"), ("z",)])
     with jax.named_scope("finish"):
@@ -618,11 +727,8 @@
                 pltpu.VMEM((orb, orb), f32),
                 pltpu.VMEM((orb, orb), f32),
                 pltpu.VMEM((orb, width), f32),
-                pltpu.VMEM((width, width), bf16),
-                pltpu.VMEM((width, width), bf16),
+                pltpu.VMEM((width, 2 * width), bf16),
             ],
-            flops=8 * width * width * depth_rows,
-            moved=8 * width * depth_rows,
         )
 
 

time: 225 us -> 189 us (0.84)
  waiting for transfers between devices: 81.3 us -> 46.7 us
  local copies, waits for them, and re-layouts: 7.57 us -> 16.1 us
  starting transfers between devices: 47.1 us -> 42.6 us
  other arithmetic: 3.65 us -> 0.26 us
    ppermute x6, waiting for transfers between devices: 36.8 us -> 2.71 us  [z_move(): return lax.ppermute(value, ('z', 'x'), pairs)]
    all_to_all x2 -> x3, waiting for transfers between devices: 13.6 us -> 24.8 us  [the longest x2 15.5 us: regroup(): return lax.all_to_all(flat, axes, 0, 0, tiled=True).reshape(value.shape)]
    unnamed x21 -> x59, local copies, waits for them, and re-layouts: 6.44 us -> 13.1 us
    ppermute x2, waiting for transfers between devices: 13.2 us -> 6.92 us  [group_sum(): lax.ppermute(value, axes, [(i, i ^ hop) for i in range(count)])]
    ppermute x7 -> x4, waiting for transfers between devices: 8.74 us -> 4.22 us  [group_sum(): lax.ppermute(total, axes, [(i, (i - k) % count) for i in range(count)])]
    ppermute x7 -> x4, starting transfers between devices: 12.2 us -> 7.77 us  [group_sum(): lax.ppermute(total, axes, [(i, (i - k) % count) for i in range(count)])]
    ppermute x4 -> x6, starting transfers between devices: 3.6 us -> 7.5 us  [swap(): return lax.ppermute(value, axis, [(0, 1), (1, 0)])]
    ppermute x7 -> x4, starting transfers between devices: 8.43 us -> 4.55 us  [group_sum(): lax.ppermute(piece(k), axes, [(i, (i + k) % count) for i in range(count)])]
  transfers between devices with their start and end apart: 28 -> 25, of which waited for: 21 -> 17; matrix products, arithmetic and copies ran while one was open for 1% -> 2% of each run, Pallas kernels for 11% -> 25%
where the time goes in v2:
time: 189 us; the launch traced here: 188 us
  Pallas kernels  81.7 us (43%)
  waiting for transfers between devices  46.7 us (25%)
  starting transfers between devices  42.6 us (23%)
  local copies, waits for them, and re-layouts  16.1 us (9%)
    pallas_call x15, Pallas kernels, call(): pl.pallas_call(kernel, out_shape=out_shape, in_specs=[*specs, *[pl.BlockS...  70.8 us
    all_to_all x2, waiting for transfers between devices, regroup(): return lax.all_to_all(flat, axes, 0, 0, tiled=True).reshape(value.shape)  15.5 us
    unnamed x59, local copies, waits for them, and re-layouts  13.1 us
    pallas_call x2, Pallas kernels, step(): pl.pallas_call(kernel, out_shape=out, grid_spec=pltpu.PrefetchScalarGridS...  9.57 us
    all_to_all x1, waiting for transfers between devices, per_device(): ends = jnp.max(lax.all_to_all(ends, ('z', 'x'), 0, 0, tiled=True), axis=0)  9.35 us
    all_to_all x2, starting transfers between devices, regroup(): return lax.all_to_all(flat, axes, 0, 0, tiled=True).reshape(value.shape)  8.8 us
    ppermute x6, starting transfers between devices, z_move(): return lax.ppermute(value, ('z', 'x'), pairs)  8.17 us
    ppermute x4, starting transfers between devices, group_sum(): lax.ppermute(total, axes, [(i, (i - k) % count) for i in range(count)])  7.77 us
  transfers between devices with their start and end apart: 25, of which 17 were waited for; matrix products, arithmetic and copies ran while one was open for 2% of the time, Pallas kernels for 25%

profile of v2, /device:TPU:1, one launch (start us, length us, event | category | flops | bytes accessed | tf_op | source)
XLA Modules:
  0.0 187.8 jit_solution(17768295354477236847)
XLA Ops:
  0.0 1.6 copy-done.10
  3.0 4.2 %collective-permute-start.3 = (f32[1,16,64,128]{3,2,1,0:T(8,128)S(1)}, f32[1,16,64,128]{3,2,1,0:T(8,128)S(1)}, u32[]{:S(2)}, u32[]{:S(2)}) collective-permute-start(f32[1,16,64,128]{3,2,1,0:T(8,128)S(1)} %get-tuple-element.20.refs_4_.refs_2_.refs_5_.refs_9_), channel_id=1, source_target_pairs={{0,24},{4,12},{8,0},{12,20},{16,8},{20,28},{24,16},{28,4},{1,25},{... | collective-permute-start | bytes 1572872 | tf_op jit(solution)/shard_map/prepare/ppermute | solution.py:584
  8.1 1.8 collective-permute-start
  13.0 3.0 %prepare.8 = (bf16[16,128,256]{2,1,0:T(8,128)(2,1)S(1)}, f32[8,128]{1,0:T(8,128)S(1)}) custom-call(s32[224]{0:T(256)S(1)} %reshape.74.refs_0_, f32[16,128,128]{2,1,0:T(8,128)S(1)} %copy-done.17, f32[2,16,128]{2,1,0:T(8,128)S(1)} %copy-done.21, f32[8,128]{1,0:T(8,128)S(1)} %collective-permute-done.1.refs_3_), custom_call_target="tpu_custom_call" | custom-call | flops 1 | bytes 1 | tf_op jit(solution)/shard_map/prepare/pallas_call | solution.py:38
  17.7 2.1 %collective-permute-done.2.refs_0_ = f32[1,16,64,128]{3,2,1,0:T(8,128)S(1)} collective-permute-done((f32[1,16,64,128]{3,2,1,0:T(8,128)}, f32[1,16,64,128]{3,2,1,0:T(8,128)S(1)}, u32[]{:S(2)}, u32[]{:S(2)}) %collective-permute-start.2) | collective-permute-done | bytes 524320 | tf_op jit(solution)/shard_map/prepare/ppermute | solution.py:69
  22.8 4.2 %all-to-all-start = ((f32[8,8,128]{2,1,0:T(8,128)}), f32[8,8,128]{2,1,0:T(8,128)S(1)}, u32[]{:S(2)}, u32[]{:S(2)}) async-start(f32[8,8,128]{2,1,0:T(8,128)} %broadcast_in_dim.43), calls=%async_computation | async-start | bytes 65536 | tf_op jit(solution)/shard_map/prepare/all_to_all | solution.py:620
  27.7 9.4 %all-to-all-done = f32[8,8,128]{2,1,0:T(8,128)S(1)} async-done(((f32[8,8,128]{2,1,0:T(8,128)}), f32[8,8,128]{2,1,0:T(8,128)S(1)}, u32[]{:S(2)}, u32[]{:S(2)}) %all-to-all-start) | async-done | bytes 32800 | tf_op jit(solution)/shard_map/prepare/all_to_all | solution.py:620
  37.1 3.1 %first.3.refs_8_.refs_7_.refs_5_ = f32[1,16,64,128]{3,2,1,0:T(8,128)S(1)} custom-call(s32[448]{0:T(512)S(1)} %reshape.72.refs_0_, s32[448]{0:T(512)S(1)} %reshape.73.refs_1_, s32[1]{0:T(128)} %bitcast.x_ref.refs_0_.refs_2_, bf16[16,128,256]{2,1,0:T(8,128)(2,1)S(1)} %copy-done.1, f32[64,128]{1,0:T(8,128)S(1)} %bitcast.15, f32[1,16,64,128]{3,2,1,0:T(8,128)S(1)} %copy-done.3, ...), custom_call_target="tpu_custom_call" | custom-call | flops 1 | bytes 1 | tf_op jit(solution)/shard_map/first/pallas_call | solution.py:38
  40.2 3.1 %first.4.refs_9_.refs_5_ = f32[1,16,64,128]{3,2,1,0:T(8,128)S(1)} custom-call(s32[448]{0:T(512)S(1)} %reshape.72.refs_0_, s32[448]{0:T(512)S(1)} %reshape.73.refs_1_, s32[1]{0:T(128)} %bitcast.x_ref.refs_0_.refs_2_, bf16[16,128,256]{2,1,0:T(8,128)(2,1)S(1)} %copy-done.1, f32[64,128]{1,0:T(8,128)S(1)} %bitcast.16, ...), custom_call_target="tpu_custom_call" | custom-call | flops 1 | bytes 1 | tf_op jit(solution)/shard_map/first/pallas_call | solution.py:38
  43.3 3.3 %collective-permute-start.8 = (f32[1,16,64,128]{3,2,1,0:T(8,128)S(1)}, f32[1,16,64,128]{3,2,1,0:T(8,128)S(1)}, u32[]{:S(2)}, u32[]{:S(2)}) collective-permute-start(f32[1,16,64,128]{3,2,1,0:T(8,128)S(1)} %first.4.refs_9_.refs_5_), channel_id=1, source_target_pairs={{0,24},{4,12},{8,0},{12,20},{16,8},{20,28},{24,16},{28,4},{1,25},{... | collective-permute-start | bytes 1572872 | tf_op jit(solution)/shard_map/first/ppermute | solution.py:584
  46.6 4.9 %first.5.refs_6_ = f32[2,16,64,128]{3,2,1,0:T(8,128)S(1)} custom-call(s32[448]{0:T(512)S(1)} %reshape.72.refs_0_, s32[448]{0:T(512)S(1)} %reshape.73.refs_1_, s32[1]{0:T(128)} %bitcast.x_ref.refs_0_.refs_2_, bf16[16,128,256]{2,1,0:T(8,128)(2,1)S(1)} %copy-done.1, f32[64,128]{1,0:T(8,128)S(1)} %bitcast.17, ...), custom_call_target="tpu_custom_call" | custom-call | flops 1 | bytes 1 | tf_op jit(solution)/shard_map/first/pallas_call | solution.py:38
  53.0 1.9 %collective-permute-done.6.refs_7_ = f32[1,16,64,128]{3,2,1,0:T(8,128)S(1)} collective-permute-done((f32[1,16,64,128]{3,2,1,0:T(8,128)S(1)}, f32[1,16,64,128]{3,2,1,0:T(8,128)S(1)}, u32[]{:S(2)}, u32[]{:S(2)}) %collective-permute-start.6) | collective-permute-done | bytes 524320 | tf_op jit(solution)/shard_map/first/ppermute | solution.py:584
  54.9 4.6 %second.4 = (f32[1,16,64,128]{3,2,1,0:T(8,128)}, f32[1,16,64,128]{3,2,1,0:T(8,128)S(1)}) custom-call(s32[448]{0:T(512)S(1)} %reshape.72.refs_0_, s32[448]{0:T(512)S(1)} %reshape.73.refs_1_, s32[1]{0:T(128)} %bitcast.x_ref.refs_0_.refs_2_, bf16[16,128,256]{2,1,0:T(8,128)(2,1)S(1)} %copy-done.1, f32[64,128]{1,0:T(8,128)S(1)} %bitcast.18, ...), custom_call_target="tpu_custom_call" | custom-call | flops 1 | bytes 1 | tf_op jit(solution)/shard_map/second/pallas_call | solution.py:38
  59.6 2.6 %collective-permute-start.7 = (f32[8,128]{1,0:T(8,128)S(1)}, f32[8,128]{1,0:T(8,128)S(1)}, u32[]{:S(2)}, u32[]{:S(2)}) collective-permute-start(f32[8,128]{1,0:T(8,128)S(1)} %second.5), channel_id=1, source_target_pairs={{0,1},{1,0},{2,3},{3,2},{4,5},{5,4},{6,7},{7,6},{8,9},{9,8},{10,11... | collective-permute-start | bytes 12296 | tf_op jit(solution)/shard_map/second/ppermute | solution.py:69
  63.0 5.8 %second.6 = (f32[2,16,64,128]{3,2,1,0:T(8,128)S(1)}, f32[2,16,64,128]{3,2,1,0:T(8,128)S(1)}) custom-call(s32[448]{0:T(512)S(1)} %reshape.72.refs_0_, s32[448]{0:T(512)S(1)} %reshape.73.refs_1_, s32[1]{0:T(128)} %bitcast.x_ref.refs_0_.refs_2_, bf16[16,128,256]{2,1,0:T(8,128)(2,1)S(1)} %copy-done.1, f32[64,128]{1,0:T(8,128)S(1)} %bitcast.19, ...), custom_call_target="tpu_custom_call" | custom-call | flops 1 | bytes 1 | tf_op jit(solution)/shard_map/second/pallas_call | solution.py:38
  70.8 4.5 %second.7 = (f32[1,16,64,128]{3,2,1,0:T(8,128)}, f32[1,16,64,128]{3,2,1,0:T(8,128)S(1)}) custom-call(s32[448]{0:T(512)S(1)} %reshape.72.refs_0_, s32[448]{0:T(512)S(1)} %reshape.73.refs_1_, s32[1]{0:T(128)} %bitcast.x_ref.refs_0_.refs_2_, bf16[16,128,256]{2,1,0:T(8,128)(2,1)S(1)} %copy-done.1, f32[64,128]{1,0:T(8,128)S(1)} %bitcast.20, ...), custom_call_target="tpu_custom_call" | custom-call | flops 1 | bytes 1 | tf_op jit(solution)/shard_map/second/pallas_call | solution.py:38
  79.6 5.2 %third.5.refs_11_ = f32[2,4,1,4,64,128]{5,4,3,2,1,0:T(8,128)S(1)} custom-call(s32[448]{0:T(512)S(1)} %reshape.72.refs_0_, s32[448]{0:T(512)S(1)} %reshape.73.refs_1_, s32[1]{0:T(128)} %bitcast.x_ref.refs_0_.refs_2_, bf16[16,128,256]{2,1,0:T(8,128)(2,1)S(1)} %copy-done.1, f32[64,128]{1,0:T(8,128)S(1)} %bitcast.21, ...), custom_call_target="tpu_custom_call" | custom-call | flops 1 | bytes 1 | tf_op jit(solution)/shard_map/third/pallas_call | solution.py:38
  85.8 4.5 %all-to-all-start.2 = ((f32[8,1,4,64,128]{4,3,2,1,0:T(8,128)}), f32[8,1,4,64,128]{4,3,2,1,0:T(8,128)}, u32[]{:S(2)}, u32[]{:S(2)}) async-start(f32[8,1,4,64,128]{4,3,2,1,0:T(8,128)} %bitcast.14), calls=%async_computation.2 | async-start | bytes 2097152 | tf_op jit(solution)/shard_map/third/all_to_all | solution.py:650
  92.6 4.8 %third.6.refs_11_ = f32[2,4,1,4,64,128]{5,4,3,2,1,0:T(8,128)} custom-call(s32[448]{0:T(512)S(1)} %reshape.72.refs_0_, s32[448]{0:T(512)S(1)} %reshape.73.refs_1_, s32[1]{0:T(128)} %bitcast.x_ref.refs_0_.refs_2_, bf16[16,128,256]{2,1,0:T(8,128)(2,1)S(1)} %copy-done.1, f32[64,128]{1,0:T(8,128)S(1)} %bitcast.22, ...), custom_call_target="tpu_custom_call" | custom-call | flops 1 | bytes 1 | tf_op jit(solution)/shard_map/third/pallas_call | solution.py:271
  97.4 4.8 %third.7 = f32[2,4,1,4,64,128]{5,4,3,2,1,0:T(8,128)} custom-call(s32[448]{0:T(512)S(1)} %reshape.72.refs_0_, s32[448]{0:T(512)S(1)} %reshape.73.refs_1_, s32[1]{0:T(128)} %bitcast.x_ref.refs_0_.refs_2_, bf16[16,128,256]{2,1,0:T(8,128)(2,1)S(1)} %copy-done.1, f32[64,128]{1,0:T(8,128)S(1)} %bitcast.23, ...), custom_call_target="tpu_custom_call", output_to_operand_aliasing={{}: (11, {})} | custom-call | flops 199999995904 | bytes 1 | tf_op jit(solution)/shard_map/third/pallas_call | solution.py:271
  102.1 1.8 all-to-all-done.2
  104.0 4.3 %all-to-all-start.1 = ((f32[8,1,4,64,128]{4,3,2,1,0:T(8,128)}), f32[8,1,4,64,128]{4,3,2,1,0:T(8,128)S(1)}, u32[]{:S(2)}, u32[]{:S(2)}) async-start(f32[8,1,4,64,128]{4,3,2,1,0:T(8,128)} %bitcast.4), calls=%async_computation.1 | async-start | bytes 2097152 | tf_op jit(solution)/shard_map/third/all_to_all | solution.py:650
  108.3 13.6 %all-to-all-done.1 = f32[8,1,4,64,128]{4,3,2,1,0:T(8,128)S(1)} async-done(((f32[8,1,4,64,128]{4,3,2,1,0:T(8,128)}), f32[8,1,4,64,128]{4,3,2,1,0:T(8,128)S(1)}, u32[]{:S(2)}, u32[]{:S(2)}) %all-to-all-start.1) | async-done | bytes 1048608 | tf_op jit(solution)/shard_map/third/all_to_all | solution.py:650
  121.9 2.7 %gram.2 = f32[1280,128]{1,0:T(8,128)S(1)} custom-call(f32[2,4,1,4,64,128]{5,4,3,2,1,0:T(8,128)S(1)} %bitcast.12, f32[2,4,1,4,64,128]{5,4,3,2,1,0:T(8,128)} %bitcast.8.refs_1_.refs_2_), custom_call_target="tpu_custom_call" | custom-call | flops 1 | bytes 1 | tf_op jit(solution)/shard_map/gram/pallas_call | solution.py:38
  128.4 2.1 %collective-permute-start.15 = (f32[160,128]{1,0:T(8,128)S(1)}, f32[160,128]{1,0:T(8,128)S(1)}, u32[]{:S(2)}, u32[]{:S(2)}) collective-permute-start(f32[160,128]{1,0:T(8,128)S(1)} %get-tuple-element.38), channel_id=1, source_target_pairs={{0,6},{2,0},{4,2},{6,4},{1,7},{3,1},{5,3},{7,5},{8,14},{10,8},{12,... | collective-permute-start | bytes 245768 | tf_op jit(solution)/shard_map/gram/ppermute | solution.py:550
  131.8 1.9 %collective-permute-done.15 = f32[160,128]{1,0:T(8,128)S(1)} collective-permute-done((f32[160,128]{1,0:T(8,128)S(1)}, f32[160,128]{1,0:T(8,128)S(1)}, u32[]{:S(2)}, u32[]{:S(2)}) %collective-permute-start.15) | collective-permute-done | bytes 81952 | tf_op jit(solution)/shard_map/gram/ppermute | solution.py:550
  133.8 3.3 %collective-permute-done.16 = f32[160,128]{1,0:T(8,128)S(1)} collective-permute-done((f32[160,128]{1,0:T(8,128)S(1)}, f32[160,128]{1,0:T(8,128)S(1)}, u32[]{:S(2)}, u32[]{:S(2)}) %collective-permute-start.16) | collective-permute-done | bytes 81952 | tf_op jit(solution)/shard_map/gram/ppermute | solution.py:537
  138.5 3.6 %collective-permute-done.17 = f32[160,128]{1,0:T(8,128)S(1)} collective-permute-done((f32[160,128]{1,0:T(8,128)S(1)}, f32[160,128]{1,0:T(8,128)S(1)}, u32[]{:S(2)}, u32[]{:S(2)}) %collective-permute-start.17) | collective-permute-done | bytes 81952 | tf_op jit(solution)/shard_map/gram/ppermute | solution.py:537
  145.6 1.9 %collective-permute-done.19 = f32[160,128]{1,0:T(8,128)S(1)} collective-permute-done((f32[160,128]{1,0:T(8,128)S(1)}, f32[160,128]{1,0:T(8,128)S(1)}, u32[]{:S(2)}, u32[]{:S(2)}) %collective-permute-start.19) | collective-permute-done | bytes 81952 | tf_op jit(solution)/shard_map/gram/ppermute | solution.py:557
  149.1 5.2 %collective-permute-start.21 = (f32[640,128]{1,0:T(8,128)S(1)}, f32[640,128]{1,0:T(8,128)S(1)}, u32[]{:S(2)}, u32[]{:S(2)}) collective-permute-start(f32[640,128]{1,0:T(8,128)S(1)} %constant_dynamic-update-slice_fusion.3), channel_id=1, source_target_pairs={{0,1},{1,0},{2,3},{3,2},{4,5},{5,4},{6,7},{7,6},{8,9},{9,8},{10,11... | collective-permute-start | bytes 983048 | tf_op jit(solution)/shard_map/gram/ppermute | solution.py:557
  154.3 1.8 gram.3
  156.2 31.5 %finish.1 = f32[2,4,128,512]{3,2,1,0:T(8,128)} custom-call(f32[1280,128]{1,0:T(8,128)S(1)} %constant_dynamic-update-slice_fusion.7.refs_0_, bf16[2,4,128,512]{3,2,1,0:T(8,128)(2,1)S(1)} %get-tuple-element.33.refs_1_, bf16[2,4,128,512]{3,2,1,0:T(8,128)(2,1)S(1)} %get-tuple-element.34.refs_2_), custom_call_target="tpu_custom_call" | custom-call | flops 1 | bytes 1 | tf_op jit(solution)/shard_map/finish/pallas_call | solution.py:38
  (129 shorter events, 34.3 us)
Async XLA Ops:
  0.0 8.1 %copy-start.25 = (s32[2,7,16]{2,0,1:T(2,128)S(1)}, s32[2,7,16]{2,0,1:T(2,128)}, u32[]{:S(2)}) copy-start(s32[2,7,16]{2,0,1:T(2,128)} %param.10) | copy-start | bytes 2692
  1.6 11.4 %copy-start.17 = (f32[16,128,128]{2,1,0:T(8,128)S(1)}, f32[16,128,128]{2,1,0:T(8,128)}, u32[]{:S(2)}) copy-start(f32[16,128,128]{2,1,0:T(8,128)} %refs_1_.4) | copy-start | bytes 3145732
  3.0 14.7 %collective-permute-start.3 = (f32[1,16,64,128]{3,2,1,0:T(8,128)S(1)}, f32[1,16,64,128]{3,2,1,0:T(8,128)S(1)}, u32[]{:S(2)}, u32[]{:S(2)}) collective-permute-start(f32[1,16,64,128]{3,2,1,0:T(8,128)S(1)} %get-tuple-element.20.refs_4_.refs_2_.refs_5_.refs_9_), channel_id=1, source_target_pairs={{0,24},{4,12},{8,0},{12,20},{16,8},{20,28},{24,16},{28,4},{1,25},{... | collective-permute-start | bytes 1572872 | tf_op jit(solution)/shard_map/prepare/ppermute | solution.py:584
  7.1 12.7 %collective-permute-start.2 = (f32[1,16,64,128]{3,2,1,0:T(8,128)}, f32[1,16,64,128]{3,2,1,0:T(8,128)S(1)}, u32[]{:S(2)}, u32[]{:S(2)}) collective-permute-start(f32[1,16,64,128]{3,2,1,0:T(8,128)} %get-tuple-element.24), channel_id=1, source_target_pairs={{0,4},{4,0},{1,5},{5,1},{2,6},{6,2},{3,7},{7,3},{8,12},{12,8},{9,1... | collective-permute-start | bytes 1572872 | tf_op jit(solution)/shard_map/prepare/ppermute | solution.py:69
  7.1 5.8 %collective-permute-start.1 = (f32[8,128]{1,0:T(8,128)S(1)}, f32[8,128]{1,0:T(8,128)S(1)}, u32[]{:S(2)}, u32[]{:S(2)}) collective-permute-start(f32[8,128]{1,0:T(8,128)S(1)} %get-tuple-element.21), channel_id=1, source_target_pairs={{0,1},{1,0},{2,3},{3,2},{4,5},{5,4},{6,7},{7,6},{8,9},{9,8},{10,11... | collective-permute-start | bytes 12296 | tf_op jit(solution)/shard_map/prepare/ppermute | solution.py:69
  8.1 18.9 %collective-permute-start = (f32[2,32,128]{2,1,0:T(8,128)S(1)}, f32[2,32,128]{2,1,0:T(8,128)S(1)}, u32[]{:S(2)}, u32[]{:S(2)}) collective-permute-start(f32[2,32,128]{2,1,0:T(8,128)S(1)} %prepare.7), channel_id=1, source_target_pairs={{0,4},{4,0},{1,5},{5,1},{2,6},{6,2},{3,7},{7,3},{8,12},{12,8},{9,1... | collective-permute-start | bytes 98312 | tf_op jit(solution)/shard_map/prepare/ppermute | solution.py:69
  20.6 16.4 %copy-start.1 = (bf16[16,128,256]{2,1,0:T(8,128)(2,1)S(1)}, bf16[16,128,256]{2,1,0:T(8,128)(2,1)}, u32[]{:S(2)}) copy-start(bf16[16,128,256]{2,1,0:T(8,128)(2,1)} %copy-done) | copy-start | bytes 3145732
  20.6 16.4 %copy-start.3 = (f32[1,16,64,128]{3,2,1,0:T(8,128)S(1)}, f32[1,16,64,128]{3,2,1,0:T(8,128)}, u32[]{:S(2)}) copy-start(f32[1,16,64,128]{3,2,1,0:T(8,128)} %prepare.10.refs_1_.refs_5_.refs_8_.refs_11_.refs_9_) | copy-start | bytes 1572868
  20.6 16.4 %copy-start.13 = (f32[1,16,64,128]{3,2,1,0:T(8,128)S(1)}, f32[1,16,64,128]{3,2,1,0:T(8,128)}, u32[]{:S(2)}) copy-start(f32[1,16,64,128]{3,2,1,0:T(8,128)} %copy-done.12) | copy-start | bytes 1572868
  20.6 19.6 %collective-permute-start.4 = (f32[1,16,64,128]{3,2,1,0:T(8,128)}, f32[1,16,64,128]{3,2,1,0:T(8,128)}, u32[]{:S(2)}, u32[]{:S(2)}) collective-permute-start(f32[1,16,64,128]{3,2,1,0:T(8,128)} %prepare.10.refs_1_.refs_5_.refs_8_.refs_11_.refs_9_), channel_id=1, source_target_pairs={{0,8},{4,28},{8,16},{12,4},{16,24},{20,12},{24,0},{28,20},{1,9},{5... | collective-permute-start | bytes 1572872 | tf_op jit(solution)/shard_map/prepare/ppermute | solution.py:584
  20.7 16.4 %collective-permute-start.5 = (f32[1,16,64,128]{3,2,1,0:T(8,128)}, f32[1,16,64,128]{3,2,1,0:T(8,128)}, u32[]{:S(2)}, u32[]{:S(2)}) collective-permute-start(f32[1,16,64,128]{3,2,1,0:T(8,128)} %prepare.11), channel_id=1, source_target_pairs={{0,4},{4,0},{1,5},{5,1},{2,6},{6,2},{3,7},{7,3},{8,12},{12,8},{9,1... | collective-permute-start | bytes 1572872 | tf_op jit(solution)/shard_map/prepare/ppermute | solution.py:69
  22.8 14.2 %all-to-all-start = ((f32[8,8,128]{2,1,0:T(8,128)}), f32[8,8,128]{2,1,0:T(8,128)S(1)}, u32[]{:S(2)}, u32[]{:S(2)}) async-start(f32[8,8,128]{2,1,0:T(8,128)} %broadcast_in_dim.43), calls=%async_computation | async-start | bytes 65536 | tf_op jit(solution)/shard_map/prepare/all_to_all | solution.py:620
  40.1 14.8 %collective-permute-start.6 = (f32[1,16,64,128]{3,2,1,0:T(8,128)S(1)}, f32[1,16,64,128]{3,2,1,0:T(8,128)S(1)}, u32[]{:S(2)}, u32[]{:S(2)}) collective-permute-start(f32[1,16,64,128]{3,2,1,0:T(8,128)S(1)} %first.3.refs_8_.refs_7_.refs_5_), channel_id=1, source_target_pairs={{0,8},{4,28},{8,16},{12,4},{16,24},{20,12},{24,0},{28,20},{1,9},{5... | collective-permute-start | bytes 1572872 | tf_op jit(solution)/shard_map/first/ppermute | solution.py:584
  43.3 27.5 %collective-permute-start.8 = (f32[1,16,64,128]{3,2,1,0:T(8,128)S(1)}, f32[1,16,64,128]{3,2,1,0:T(8,128)S(1)}, u32[]{:S(2)}, u32[]{:S(2)}) collective-permute-start(f32[1,16,64,128]{3,2,1,0:T(8,128)S(1)} %first.4.refs_9_.refs_5_), channel_id=1, source_target_pairs={{0,24},{4,12},{8,0},{12,20},{16,8},{20,28},{24,16},{28,4},{1,25},{... | collective-permute-start | bytes 1572872 | tf_op jit(solution)/shard_map/first/ppermute | solution.py:584
  59.6 11.2 %copy-start.5 = (f32[2,16,64,128]{3,2,1,0:T(8,128)S(1)}, f32[2,16,64,128]{3,2,1,0:T(8,128)}, u32[]{:S(2)}) copy-start(f32[2,16,64,128]{3,2,1,0:T(8,128)} %copy-done.4) | copy-start | bytes 3145732
  59.6 11.2 %copy-start.14 = (f32[1,16,64,128]{3,2,1,0:T(8,128)S(1)}, f32[1,16,64,128]{3,2,1,0:T(8,128)}, u32[]{:S(2)}) copy-start(f32[1,16,64,128]{3,2,1,0:T(8,128)} %copy-done.12) | copy-start | bytes 1572868
  59.6 3.4 %collective-permute-start.7 = (f32[8,128]{1,0:T(8,128)S(1)}, f32[8,128]{1,0:T(8,128)S(1)}, u32[]{:S(2)}, u32[]{:S(2)}) collective-permute-start(f32[8,128]{1,0:T(8,128)S(1)} %second.5), channel_id=1, source_target_pairs={{0,1},{1,0},{2,3},{3,2},{4,5},{5,4},{6,7},{7,6},{8,9},{9,8},{10,11... | collective-permute-start | bytes 12296 | tf_op jit(solution)/shard_map/second/ppermute | solution.py:69
  62.2 28.1 %collective-permute-start.10 = (f32[1,16,64,128]{3,2,1,0:T(8,128)}, f32[1,16,64,128]{3,2,1,0:T(8,128)}, u32[]{:S(2)}, u32[]{:S(2)}) collective-permute-start(f32[1,16,64,128]{3,2,1,0:T(8,128)} %get-tuple-element.27.refs_0_.refs_5_), channel_id=1, source_target_pairs={{0,24},{4,12},{8,0},{12,20},{16,8},{20,28},{24,16},{28,4},{1,25},{... | collective-permute-start | bytes 1572872 | tf_op jit(solution)/shard_map/second/ppermute | solution.py:584
  76.2 21.2 %collective-permute-start.9 = (f32[1,16,64,128]{3,2,1,0:T(8,128)}, f32[1,16,64,128]{3,2,1,0:T(8,128)}, u32[]{:S(2)}, u32[]{:S(2)}) collective-permute-start(f32[1,16,64,128]{3,2,1,0:T(8,128)} %get-tuple-element.29.refs_0_.refs_7_.refs_5_), channel_id=1, source_target_pairs={{0,8},{4,28},{8,16},{12,4},{16,24},{20,12},{24,0},{28,20},{1,9},{5... | collective-permute-start | bytes 1572872 | tf_op jit(solution)/shard_map/third/ppermute | solution.py:584
  76.9 1.4 collective-permute-start.11
  85.8 18.2 %all-to-all-start.2 = ((f32[8,1,4,64,128]{4,3,2,1,0:T(8,128)}), f32[8,1,4,64,128]{4,3,2,1,0:T(8,128)}, u32[]{:S(2)}, u32[]{:S(2)}) async-start(f32[8,1,4,64,128]{4,3,2,1,0:T(8,128)} %bitcast.14), calls=%async_computation.2 | async-start | bytes 2097152 | tf_op jit(solution)/shard_map/third/all_to_all | solution.py:650
  104.0 17.9 %all-to-all-start.1 = ((f32[8,1,4,64,128]{4,3,2,1,0:T(8,128)}), f32[8,1,4,64,128]{4,3,2,1,0:T(8,128)S(1)}, u32[]{:S(2)}, u32[]{:S(2)}) async-start(f32[8,1,4,64,128]{4,3,2,1,0:T(8,128)} %bitcast.4), calls=%async_computation.1 | async-start | bytes 2097152 | tf_op jit(solution)/shard_map/third/all_to_all | solution.py:650
  124.7 2.2 %collective-permute-start.12 = (f32[640,128]{1,0:T(8,128)S(1)}, f32[640,128]{1,0:T(8,128)S(1)}, u32[]{:S(2)}, u32[]{:S(2)}) collective-permute-start(f32[640,128]{1,0:T(8,128)S(1)} %constant_dynamic-slice_fusion.3), channel_id=1, source_target_pairs={{0,1},{1,0},{2,3},{3,2},{4,5},{5,4},{6,7},{7,6},{8,9},{9,8},{10,11... | collective-permute-start | bytes 983048 | tf_op jit(solution)/shard_map/gram/ppermute | solution.py:550
  126.9 4.6 %collective-permute-start.13 = (f32[160,128]{1,0:T(8,128)S(1)}, f32[160,128]{1,0:T(8,128)S(1)}, u32[]{:S(2)}, u32[]{:S(2)}) collective-permute-start(f32[160,128]{1,0:T(8,128)S(1)} %get-tuple-element.37), channel_id=1, source_target_pairs={{0,2},{2,4},{4,6},{6,0},{1,3},{3,5},{5,7},{7,1},{8,10},{10,12},{12... | collective-permute-start | bytes 245768 | tf_op jit(solution)/shard_map/gram/ppermute | solution.py:550
  128.2 3.6 %collective-permute-start.14 = (f32[160,128]{1,0:T(8,128)S(1)}, f32[160,128]{1,0:T(8,128)S(1)}, u32[]{:S(2)}, u32[]{:S(2)}) collective-permute-start(f32[160,128]{1,0:T(8,128)S(1)} %get-tuple-element.39), channel_id=1, source_target_pairs={{0,4},{2,6},{4,0},{6,2},{1,5},{3,7},{5,1},{7,3},{8,12},{10,14},{12... | collective-permute-start | bytes 245768 | tf_op jit(solution)/shard_map/gram/ppermute | solution.py:550
  128.4 5.2 %collective-permute-start.15 = (f32[160,128]{1,0:T(8,128)S(1)}, f32[160,128]{1,0:T(8,128)S(1)}, u32[]{:S(2)}, u32[]{:S(2)}) collective-permute-start(f32[160,128]{1,0:T(8,128)S(1)} %get-tuple-element.38), channel_id=1, source_target_pairs={{0,6},{2,0},{4,2},{6,4},{1,7},{3,1},{5,3},{7,5},{8,14},{10,8},{12,... | collective-permute-start | bytes 245768 | tf_op jit(solution)/shard_map/gram/ppermute | solution.py:550
  133.7 3.4 %collective-permute-start.16 = (f32[160,128]{1,0:T(8,128)S(1)}, f32[160,128]{1,0:T(8,128)S(1)}, u32[]{:S(2)}, u32[]{:S(2)}) collective-permute-start(f32[160,128]{1,0:T(8,128)S(1)} %add_add_fusion), channel_id=1, source_target_pairs={{0,8},{8,0},{16,24},{24,16},{1,9},{9,1},{17,25},{25,17},{2,10},{10... | collective-permute-start | bytes 245768 | tf_op jit(solution)/shard_map/gram/ppermute | solution.py:537
  137.1 5.1 %collective-permute-start.17 = (f32[160,128]{1,0:T(8,128)S(1)}, f32[160,128]{1,0:T(8,128)S(1)}, u32[]{:S(2)}, u32[]{:S(2)}) collective-permute-start(f32[160,128]{1,0:T(8,128)S(1)} %add.142), channel_id=1, source_target_pairs={{0,16},{8,24},{16,0},{24,8},{1,17},{9,25},{17,1},{25,9},{2,18},{10... | collective-permute-start | bytes 245768 | tf_op jit(solution)/shard_map/gram/ppermute | solution.py:537
  142.2 3.3 %collective-permute-start.18 = (f32[160,128]{1,0:T(8,128)S(1)}, f32[160,128]{1,0:T(8,128)S(1)}, u32[]{:S(2)}, u32[]{:S(2)}) collective-permute-start(f32[160,128]{1,0:T(8,128)S(1)} %get-tuple-element.36), channel_id=1, source_target_pairs={{0,6},{2,0},{4,2},{6,4},{1,7},{3,1},{5,3},{7,5},{8,14},{10,8},{12,... | collective-permute-start | bytes 245768 | tf_op jit(solution)/shard_map/gram/ppermute | solution.py:557
  143.4 4.1 %collective-permute-start.19 = (f32[160,128]{1,0:T(8,128)S(1)}, f32[160,128]{1,0:T(8,128)S(1)}, u32[]{:S(2)}, u32[]{:S(2)}) collective-permute-start(f32[160,128]{1,0:T(8,128)S(1)} %get-tuple-element.36), channel_id=1, source_target_pairs={{0,4},{2,6},{4,0},{6,2},{1,5},{3,7},{5,1},{7,3},{8,12},{10,14},{12... | collective-permute-start | bytes 245768 | tf_op jit(solution)/shard_map/gram/ppermute | solution.py:557
  144.8 4.3 %collective-permute-start.20 = (f32[160,128]{1,0:T(8,128)S(1)}, f32[160,128]{1,0:T(8,128)S(1)}, u32[]{:S(2)}, u32[]{:S(2)}) collective-permute-start(f32[160,128]{1,0:T(8,128)S(1)} %get-tuple-element.36), channel_id=1, source_target_pairs={{0,2},{2,4},{4,6},{6,0},{1,3},{3,5},{5,7},{7,1},{8,10},{10,12},{12... | collective-permute-start | bytes 245768 | tf_op jit(solution)/shard_map/gram/ppermute | solution.py:557
  149.1 7.1 %collective-permute-start.21 = (f32[640,128]{1,0:T(8,128)S(1)}, f32[640,128]{1,0:T(8,128)S(1)}, u32[]{:S(2)}, u32[]{:S(2)}) collective-permute-start(f32[640,128]{1,0:T(8,128)S(1)} %constant_dynamic-update-slice_fusion.3), channel_id=1, source_target_pairs={{0,1},{1,0},{2,3},{3,2},{4,5},{5,4},{6,7},{7,6},{8,9},{9,8},{10,11... | collective-permute-start | bytes 983048 | tf_op jit(solution)/shard_map/gram/ppermute | solution.py:557
  (21 other events, 59.8 us)

commit v3 on v2

--- a/solution.py
+++ b/solution.py
@@ -14,7 +14,8 @@
 f32 = jnp.float32
 bf16 = jnp.bfloat16
 pivots = 4
-vmem_limit = 48 * 1024 * 1024
+strip = 64
+vmem_limit = 12 * 1024 * 1024
 small = pl.CostEstimate(flops=1, bytes_accessed=1, transcendentals=0)
 large = pl.CostEstimate(flops=2 * 10**11, bytes_accessed=1, transcendentals=0)
 NT = (((1,), (1,)), ((), ()))
@@ -336,47 +337,29 @@
             low[natural, s] = b
 
 
-def mat_mul(a, b):
-    rows, inner, cols = len(a), len(b), len(b[0])
-    out = []
-    for i in range(rows):
-        line = []
-        for j in range(cols):
-            total = a[i][0] * b[0][j]
-            for k in range(1, inner):
-                total = total + a[i][k] * b[k][j]
-            line.append(total)
-        out.append(line)
-    return out
-
-
-def flip(a):
-    return [list(line) for line in zip(*a, strict=True)]
-
-
-def inverse_small(a):
-    size = len(a)
-    if size == 1:
-        return [[1.0 / a[0][0]]]
-    if size == 2:
-        one = 1.0 / (a[0][0] * a[1][1] - a[0][1] * a[0][1])
-        off = -(a[0][1] * one)
-        return [[a[1][1] * one, off], [off, a[0][0] * one]]
-    h = size // 2
-    corner = [line[:h] for line in a[:h]]
-    side = [line[h:] for line in a[:h]]
-    rest = [line[h:] for line in a[h:]]
-    ci = inverse_small(corner)
-    c = mat_mul(ci, side)
-    update = mat_mul(flip(side), c)
-    schur = [[rest[i][j] - update[i][j] for j in range(size - h)] for i in range(size - h)]
-    si = inverse_small(schur)
-    off = [[-v for v in line] for line in mat_mul(c, si)]
-    add = mat_mul(off, flip(c))
-    first = [[ci[i][j] - add[i][j] for j in range(h)] for i in range(h)]
-    return [first[i] + off[i] for i in range(h)] + [
-        flip(off)[i] + si[i] for i in range(size - h)
-    ]
+def adjugate_4(a):
+    def minor(i, j, m, n):
+        return a[i][m] * a[j][n] - a[j][m] * a[i][n]
+
+    pairs = [(0, 1), (0, 2), (0, 3), (1, 2), (1, 3), (2, 3)]
+    s = [minor(0, 1, m, n) for m, n in pairs]
+    c = [minor(2, 3, m, n) for m, n in pairs]
+    det = (s[0] * c[5] - s[1] * c[4]) + (s[2] * c[3] + s[3] * c[2]) - (s[4] * c[1] - s[5] * c[0])
+    b = [[None] * 4 for _ in range(4)]
+    b[0][0] = a[1][1] * c[5] - a[1][2] * c[4] + a[1][3] * c[3]
+    b[0][1] = a[0][2] * c[4] - a[0][1] * c[5] - a[0][3] * c[3]
+    b[0][2] = a[3][1] * s[5] - a[3][2] * s[4] + a[3][3] * s[3]
+    b[0][3] = a[2][2] * s[4] - a[2][1] * s[5] - a[2][3] * s[3]
+    b[1][1] = a[0][0] * c[5] - a[0][2] * c[2] + a[0][3] * c[1]
+    b[1][2] = a[3][2] * s[2] - a[3][0] * s[5] - a[3][3] * s[1]
+    b[1][3] = a[2][0] * s[5] - a[2][2] * s[2] + a[2][3] * s[1]
+    b[2][2] = a[3][0] * s[4] - a[3][1] * s[2] + a[3][3] * s[0]
+    b[2][3] = a[2][1] * s[2] - a[2][0] * s[4] - a[2][3] * s[0]
+    b[3][3] = a[2][0] * s[3] - a[2][1] * s[1] + a[2][2] * s[0]
+    for i in range(4):
+        for j in range(i):
+            b[i][j] = b[j][i]
+    return b, det
 
 
 def lower_inverse_small(a):
@@ -404,53 +387,104 @@
     return inv
 
 
+def spread_lane(value, lane):
+    return jnp.take_along_axis(
+        value, jnp.full(value.shape, lane, jnp.int32), axis=1, mode="promise_in_bounds"
+    )
+
+
+def spread_row(value, row):
+    return jnp.broadcast_to(value[row : row + 1, :], value.shape)
+
+
 def lower_inverse(block_ref, out_ref):
     size = block_ref.shape[0]
-    lanes = lax.broadcasted_iota(jnp.int32, (8, size), 1)
-    subs = lax.broadcasted_iota(jnp.int32, (8, size), 0)
+    shape = (8, size)
+    lanes = lax.broadcasted_iota(jnp.int32, shape, 1)
+    subs = lax.broadcasted_iota(jnp.int32, shape, 0)
     rows = [block_ref[8 * g : 8 * g + 8, :] for g in range(size // 8)]
-    shape = (8, size)
-    for start in range(0, size, pivots):
-        group, offset = divmod(start, 8)
-        inside = (lanes >= start) & (lanes < start + pivots)
-        here = rows[group]
-        columns = {}
-        for g in range(group, size // 8):
-            columns[g] = [
-                jnp.broadcast_to(rows[g][:, start + k : start + k + 1], shape)
+    for first in range(0, size, strip):
+        past = (first + strip) // 8
+        for start in range(first, first + strip, pivots):
+            group, offset = divmod(start, 8)
+            inside = (lanes >= start) & (lanes < start + pivots)
+            here = rows[group]
+            columns = {
+                g: [spread_lane(rows[g], start + k) for k in range(pivots)]
+                for g in range(group, past)
+            }
+            if start == first:
+                corner = [
+                    [spread_row(columns[group][j], offset + i) for j in range(pivots)]
+                    for i in range(pivots)
+                ]
+            lines = [
+                jnp.where(
+                    inside,
+                    jnp.where(lanes == start + k, 1.0, 0.0),
+                    spread_row(here, offset + k),
+                )
                 for k in range(pivots)
             ]
-        corner = [
-            [
-                jnp.broadcast_to(columns[group][j][offset + i : offset + i + 1, :], shape)
-                for j in range(pivots)
+            adj, det = adjugate_4(corner)
+            share = 1.0 / det
+            weights = [
+                ((adj[k][0] * lines[0] + adj[k][1] * lines[1]) + (adj[k][2] * lines[2] + adj[k][3] * lines[3]))
+                * share
+                for k in range(pivots)
             ]
-            for i in range(pivots)
-        ]
-        lines = [
-            jnp.where(
-                inside,
-                jnp.where(lanes == start + k, 1.0, 0.0),
-                jnp.broadcast_to(here[offset + k : offset + k + 1, :], shape),
+            after = start + pivots
+            next_corner = None
+            if after < first + strip:
+                ng, noff = divmod(after, 8)
+                side = [
+                    [spread_row(columns[ng][k], noff + i) for k in range(pivots)]
+                    for i in range(pivots)
+                ]
+                ahead = [spread_lane(rows[ng], after + j) for j in range(pivots)]
+                part = [
+                    [
+                        (adj[k][0] * side[j][0] + adj[k][1] * side[j][1])
+                        + (adj[k][2] * side[j][2] + adj[k][3] * side[j][3])
+                        for j in range(pivots)
+                    ]
+                    for k in range(pivots)
+                ]
+                next_corner = [[None] * pivots for _ in range(pivots)]
+                for i in range(pivots):
+                    for j in range(i + 1):
+                        taken = (side[i][0] * part[0][j] + side[i][1] * part[1][j]) + (
+                            side[i][2] * part[2][j] + side[i][3] * part[3][j]
+                        )
+                        next_corner[i][j] = spread_row(ahead[j], noff + i) - taken * share
+                        next_corner[j][i] = next_corner[i][j]
+            for g in range(group, past):
+                c = columns[g]
+                change = (c[0] * weights[0] + c[1] * weights[1]) + (c[2] * weights[2] + c[3] * weights[3])
+                updated = jnp.where(inside, 0.0, rows[g]) - change
+                if g == group:
+                    updated = jnp.where(subs >= offset + pivots, updated, rows[g])
+                rows[g] = updated
+            low = lower_inverse_small(corner)
+            for r in range(pivots):
+                line = functools.reduce(jnp.add, [low[r][k] * lines[k] for k in range(r + 1)])
+                rows[group] = jnp.where(subs == offset + r, line, rows[group])
+            corner = next_corner
+        mine = (lanes >= first) & (lanes < first + strip)
+        for g in range(first // 8, past):
+            rows[g] = jnp.where(mine & (lanes > subs + 8 * g), 0.0, rows[g])
+            out_ref[8 * g : 8 * g + 8, :] = jnp.where(lanes <= subs + 8 * g, rows[g], 0.0)
+        if past < size // 8:
+            panel = jnp.concatenate(rows[first // 8 : past], axis=0)
+            high, low_part = halves(panel)
+            wide = jnp.concatenate([high, low_part, high], axis=0)
+            tall = jnp.concatenate([high, high, low_part], axis=0).astype(f32)
+            tall = jnp.concatenate([tall, jnp.zeros((-3 * strip % size, size), f32)], axis=0).T
+            change = jnp.dot(
+                tall[first + strip :, : 3 * strip].astype(bf16), wide, preferred_element_type=f32
             )
-            for k in range(pivots)
-        ]
-        inv = inverse_small(corner)
-        weights = [functools.reduce(jnp.add, [inv[k][m] * lines[m] for m in range(pivots)]) for k in range(pivots)]
-        for g in range(group, size // 8):
-            change = functools.reduce(
-                jnp.add, [columns[g][k] * weights[k] for k in range(pivots)]
-            )
-            updated = jnp.where(inside, 0.0, rows[g]) - change
-            if g == group:
-                updated = jnp.where(subs >= offset + pivots, updated, rows[g])
-            rows[g] = updated
-        low = lower_inverse_small(corner)
-        for r in range(pivots):
-            line = functools.reduce(jnp.add, [low[r][k] * lines[k] for k in range(r + 1)])
-            rows[group] = jnp.where(subs == offset + r, line, rows[group])
-    for g in range(size // 8):
-        out_ref[8 * g : 8 * g + 8, :] = jnp.where(lanes <= subs + 8 * g, rows[g], 0.0)
+            for n, g in enumerate(range(past, size // 8)):
+                rows[g] = jnp.where(mine, 0.0, rows[g]) - change[8 * n : 8 * n + 8, :]
 
 
 def three(left, right):
@@ -466,10 +500,21 @@
 def finish_body(gram_ref, high_ref, low_ref, out_ref, work, diag, lower, panel, inv):
     size = work.shape[0]
     tile = diag.shape[0]
+    eye = lax.broadcasted_iota(jnp.int32, (tile, tile), 0) == lax.broadcasted_iota(
+        jnp.int32, (tile, tile), 1
+    )
+    down, across = [], []
+    place = -tile
+    for i in range(0, size, tile):
+        place += i + tile
+        kept = jnp.where(eye, gram_ref[place : place + tile, :], 0.0)
+        down.append(lax.rsqrt(jnp.sum(kept, axis=1, keepdims=True)))
+        across.append(lax.rsqrt(jnp.sum(kept, axis=0, keepdims=True)))
+    scales = jnp.concatenate(across, axis=1)
     place = 0
     for i in range(0, size, tile):
         for j in range(0, i + 1, tile):
-            block = gram_ref[place : place + tile, :]
+            block = gram_ref[place : place + tile, :] * down[i // tile] * across[j // tile]
             place += tile
             work[i : i + tile, j : j + tile] = block
             if i != j:
@@ -486,7 +531,7 @@
             inside, jnp.where(cols - at == local, 1.0, 0.0), work[pl.ds(at, tile), :]
         )
         panel[...] = three(lower[...], line)
-        kept = jnp.where(cols < at + tile, panel[...], 0.0)
+        kept = jnp.where(cols < at + tile, panel[...] * scales, 0.0)
         high, low = halves(kept)
         inv[pl.ds(at, tile), :size] = high
         inv[pl.ds(at, tile), size:] = low

time: 189 us -> 170 us (0.90)
  Pallas kernels: 81.7 us -> 63.6 us
  local copies, waits for them, and re-layouts: 16.1 us -> 12.4 us
  waiting for transfers between devices: 46.7 us -> 50.1 us
    pallas_call x15, Pallas kernels: 70.8 us -> 54.4 us  [call(): pl.pallas_call(kernel, out_shape=out_shape, in_specs=[*specs, *[pl.BlockS...]
    unnamed x59 -> x47, local copies, waits for them, and re-layouts: 13.1 us -> 9.79 us
    all_to_all x2, waiting for transfers between devices: 15.5 us -> 18.5 us  [regroup(): return lax.all_to_all(flat, axes, 0, 0, tiled=True).reshape(value.shape)]
where the time goes in v3:
time: 170 us; the launch traced here: 169 us
  Pallas kernels  63.6 us (37%)
  waiting for transfers between devices  50.1 us (29%)
  starting transfers between devices  42.7 us (25%)
  local copies, waits for them, and re-layouts  12.4 us (7%)
    pallas_call x15, Pallas kernels, call(): pl.pallas_call(kernel, out_shape=out_shape, in_specs=[*specs, *[pl.BlockS...  54.4 us
    all_to_all x2, waiting for transfers between devices, regroup(): return lax.all_to_all(flat, axes, 0, 0, tiled=True).reshape(value.shape)  18.5 us
    unnamed x47, local copies, waits for them, and re-layouts  9.79 us
    all_to_all x1, waiting for transfers between devices, per_device(): ends = jnp.max(lax.all_to_all(ends, ('z', 'x'), 0, 0, tiled=True), axis=0)  9.35 us
    all_to_all x2, starting transfers between devices, regroup(): return lax.all_to_all(flat, axes, 0, 0, tiled=True).reshape(value.shape)  8.93 us
    ppermute x6, starting transfers between devices, z_move(): return lax.ppermute(value, ('z', 'x'), pairs)  8.18 us
    pallas_call x2, Pallas kernels, step(): pl.pallas_call(kernel, out_shape=out, grid_spec=pltpu.PrefetchScalarGridS...  7.8 us
    ppermute x4, starting transfers between devices, group_sum(): lax.ppermute(total, axes, [(i, (i - k) % count) for i in range(count)])  7.79 us
  transfers between devices with their start and end apart: 25, of which 17 were waited for; matrix products, arithmetic and copies ran while one was open for 2% of the time, Pallas kernels for 25%

profile of v3, /device:TPU:1, one launch (start us, length us, event | category | flops | bytes accessed | tf_op | source)
XLA Modules:
  0.0 169.5 jit_solution(2094508055448080753)
XLA Ops:
  0.0 1.6 copy-done.4
  2.9 4.2 %collective-permute-start.3 = (f32[1,16,64,128]{3,2,1,0:T(8,128)S(1)}, f32[1,16,64,128]{3,2,1,0:T(8,128)S(1)}, u32[]{:S(2)}, u32[]{:S(2)}) collective-permute-start(f32[1,16,64,128]{3,2,1,0:T(8,128)S(1)} %get-tuple-element.20.refs_4_.refs_2_.refs_5_.refs_9_), channel_id=1, source_target_pairs={{0,24},{4,12},{8,0},{12,20},{16,8},{20,28},{24,16},{28,4},{1,25},{... | collective-permute-start | bytes 1572872 | tf_op jit(solution)/shard_map/prepare/ppermute | solution.py:629
  8.1 1.8 %collective-permute-start = (f32[2,32,128]{2,1,0:T(8,128)S(1)}, f32[2,32,128]{2,1,0:T(8,128)S(1)}, u32[]{:S(2)}, u32[]{:S(2)}) collective-permute-start(f32[2,32,128]{2,1,0:T(8,128)S(1)} %prepare.7), channel_id=1, source_target_pairs={{0,4},{4,0},{1,5},{5,1},{2,6},{6,2},{3,7},{7,3},{8,12},{12,8},{9,1... | collective-permute-start | bytes 98312 | tf_op jit(solution)/shard_map/prepare/ppermute | solution.py:70
  12.9 3.0 %prepare.8 = (bf16[16,128,256]{2,1,0:T(8,128)(2,1)S(1)}, f32[8,128]{1,0:T(8,128)S(1)}) custom-call(s32[224]{0:T(256)S(1)} %reshape.74.refs_0_, f32[16,128,128]{2,1,0:T(8,128)S(1)} %copy-done.12, f32[2,16,128]{2,1,0:T(8,128)S(1)} %copy-done.16, f32[8,128]{1,0:T(8,128)S(1)} %collective-permute-done.1.refs_3_), custom_call_target="tpu_custom_call" | custom-call | flops 1 | bytes 1 | tf_op jit(solution)/shard_map/prepare/pallas_call | solution.py:39
  17.7 2.1 %collective-permute-done.2.refs_0_ = f32[1,16,64,128]{3,2,1,0:T(8,128)S(1)} collective-permute-done((f32[1,16,64,128]{3,2,1,0:T(8,128)}, f32[1,16,64,128]{3,2,1,0:T(8,128)S(1)}, u32[]{:S(2)}, u32[]{:S(2)}) %collective-permute-start.2) | collective-permute-done | bytes 524320 | tf_op jit(solution)/shard_map/prepare/ppermute | solution.py:70
  22.8 4.2 %all-to-all-start = ((f32[8,8,128]{2,1,0:T(8,128)}), f32[8,8,128]{2,1,0:T(8,128)S(1)}, u32[]{:S(2)}, u32[]{:S(2)}) async-start(f32[8,8,128]{2,1,0:T(8,128)} %broadcast_in_dim.43), calls=%async_computation | async-start | bytes 65536 | tf_op jit(solution)/shard_map/prepare/all_to_all | solution.py:665
  27.6 9.3 %all-to-all-done = f32[8,8,128]{2,1,0:T(8,128)S(1)} async-done(((f32[8,8,128]{2,1,0:T(8,128)}), f32[8,8,128]{2,1,0:T(8,128)S(1)}, u32[]{:S(2)}, u32[]{:S(2)}) %all-to-all-start) | async-done | bytes 32800 | tf_op jit(solution)/shard_map/prepare/all_to_all | solution.py:665
  37.0 3.1 %first.3.refs_8_.refs_7_.refs_5_ = f32[1,16,64,128]{3,2,1,0:T(8,128)S(1)} custom-call(s32[448]{0:T(512)S(1)} %reshape.72.refs_0_, s32[448]{0:T(512)S(1)} %reshape.73.refs_1_, s32[1]{0:T(128)} %bitcast.x_ref.refs_0_.refs_2_, bf16[16,128,256]{2,1,0:T(8,128)(2,1)S(1)} %copy-done.1, f32[64,128]{1,0:T(8,128)S(1)} %bitcast.15, f32[1,16,64,128]{3,2,1,0:T(8,128)S(1)} %copy-done.3, ...), custom_call_target="tpu_custom_call" | custom-call | flops 1 | bytes 1 | tf_op jit(solution)/shard_map/first/pallas_call | solution.py:39
  40.2 3.1 %first.4.refs_9_.refs_5_ = f32[1,16,64,128]{3,2,1,0:T(8,128)S(1)} custom-call(s32[448]{0:T(512)S(1)} %reshape.72.refs_0_, s32[448]{0:T(512)S(1)} %reshape.73.refs_1_, s32[1]{0:T(128)} %bitcast.x_ref.refs_0_.refs_2_, bf16[16,128,256]{2,1,0:T(8,128)(2,1)S(1)} %copy-done.1, f32[64,128]{1,0:T(8,128)S(1)} %bitcast.16, ...), custom_call_target="tpu_custom_call" | custom-call | flops 1 | bytes 1 | tf_op jit(solution)/shard_map/first/pallas_call | solution.py:39
  43.3 3.3 %collective-permute-start.8 = (f32[1,16,64,128]{3,2,1,0:T(8,128)S(1)}, f32[1,16,64,128]{3,2,1,0:T(8,128)S(1)}, u32[]{:S(2)}, u32[]{:S(2)}) collective-permute-start(f32[1,16,64,128]{3,2,1,0:T(8,128)S(1)} %first.4.refs_9_.refs_5_), channel_id=1, source_target_pairs={{0,24},{4,12},{8,0},{12,20},{16,8},{20,28},{24,16},{28,4},{1,25},{... | collective-permute-start | bytes 1572872 | tf_op jit(solution)/shard_map/first/ppermute | solution.py:629
  46.6 4.9 %first.5.refs_6_ = f32[2,16,64,128]{3,2,1,0:T(8,128)S(1)} custom-call(s32[448]{0:T(512)S(1)} %reshape.72.refs_0_, s32[448]{0:T(512)S(1)} %reshape.73.refs_1_, s32[1]{0:T(128)} %bitcast.x_ref.refs_0_.refs_2_, bf16[16,128,256]{2,1,0:T(8,128)(2,1)S(1)} %copy-done.1, f32[64,128]{1,0:T(8,128)S(1)} %bitcast.17, ...), custom_call_target="tpu_custom_call" | custom-call | flops 1 | bytes 1 | tf_op jit(solution)/shard_map/first/pallas_call | solution.py:39
  52.6 2.3 %collective-permute-done.6.refs_7_ = f32[1,16,64,128]{3,2,1,0:T(8,128)S(1)} collective-permute-done((f32[1,16,64,128]{3,2,1,0:T(8,128)S(1)}, f32[1,16,64,128]{3,2,1,0:T(8,128)S(1)}, u32[]{:S(2)}, u32[]{:S(2)}) %collective-permute-start.6) | collective-permute-done | bytes 524320 | tf_op jit(solution)/shard_map/first/ppermute | solution.py:629
  54.9 4.3 %second.4 = (f32[1,16,64,128]{3,2,1,0:T(8,128)}, f32[1,16,64,128]{3,2,1,0:T(8,128)S(1)}) custom-call(s32[448]{0:T(512)S(1)} %reshape.72.refs_0_, s32[448]{0:T(512)S(1)} %reshape.73.refs_1_, s32[1]{0:T(128)} %bitcast.x_ref.refs_0_.refs_2_, bf16[16,128,256]{2,1,0:T(8,128)(2,1)S(1)} %copy-done.1, f32[64,128]{1,0:T(8,128)S(1)} %bitcast.18, ...), custom_call_target="tpu_custom_call" | custom-call | flops 1 | bytes 1 | tf_op jit(solution)/shard_map/second/pallas_call | solution.py:39
  59.2 2.6 %collective-permute-start.7 = (f32[8,128]{1,0:T(8,128)S(1)}, f32[8,128]{1,0:T(8,128)S(1)}, u32[]{:S(2)}, u32[]{:S(2)}) collective-permute-start(f32[8,128]{1,0:T(8,128)S(1)} %second.5), channel_id=1, source_target_pairs={{0,1},{1,0},{2,3},{3,2},{4,5},{5,4},{6,7},{7,6},{8,9},{9,8},{10,11... | collective-permute-start | bytes 12296 | tf_op jit(solution)/shard_map/second/ppermute | solution.py:70
  62.6 4.8 %second.6 = (f32[2,16,64,128]{3,2,1,0:T(8,128)S(1)}, f32[2,16,64,128]{3,2,1,0:T(8,128)S(1)}) custom-call(s32[448]{0:T(512)S(1)} %reshape.72.refs_0_, s32[448]{0:T(512)S(1)} %reshape.73.refs_1_, s32[1]{0:T(128)} %bitcast.x_ref.refs_0_.refs_2_, bf16[16,128,256]{2,1,0:T(8,128)(2,1)S(1)} %copy-done.1, f32[64,128]{1,0:T(8,128)S(1)} %bitcast.19, ...), custom_call_target="tpu_custom_call" | custom-call | flops 1 | bytes 1 | tf_op jit(solution)/shard_map/second/pallas_call | solution.py:39
  68.5 3.0 %second.7 = (f32[1,16,64,128]{3,2,1,0:T(8,128)S(1)}, f32[1,16,64,128]{3,2,1,0:T(8,128)S(1)}) custom-call(s32[448]{0:T(512)S(1)} %reshape.72.refs_0_, s32[448]{0:T(512)S(1)} %reshape.73.refs_1_, s32[1]{0:T(128)} %bitcast.x_ref.refs_0_.refs_2_, bf16[16,128,256]{2,1,0:T(8,128)(2,1)S(1)} %copy-done.1, f32[64,128]{1,0:T(8,128)S(1)} %bitcast.20, ...), custom_call_target="tpu_custom_call" | custom-call | flops 1 | bytes 1 | tf_op jit(solution)/shard_map/second/pallas_call | solution.py:39
  75.7 6.0 %third.5.refs_11_ = f32[2,4,1,4,64,128]{5,4,3,2,1,0:T(8,128)} custom-call(s32[448]{0:T(512)S(1)} %reshape.72.refs_0_, s32[448]{0:T(512)S(1)} %reshape.73.refs_1_, s32[1]{0:T(128)} %bitcast.x_ref.refs_0_.refs_2_, bf16[16,128,256]{2,1,0:T(8,128)(2,1)S(1)} %copy-done.1, f32[64,128]{1,0:T(8,128)S(1)} %bitcast.21, ...), custom_call_target="tpu_custom_call" | custom-call | flops 1 | bytes 1 | tf_op jit(solution)/shard_map/third/pallas_call | solution.py:39
  81.7 4.6 %all-to-all-start.2 = ((f32[8,1,4,64,128]{4,3,2,1,0:T(8,128)}), f32[8,1,4,64,128]{4,3,2,1,0:T(8,128)}, u32[]{:S(2)}, u32[]{:S(2)}) async-start(f32[8,1,4,64,128]{4,3,2,1,0:T(8,128)} %bitcast.7), calls=%async_computation.2 | async-start | bytes 2097152 | tf_op jit(solution)/shard_map/third/all_to_all | solution.py:695
  86.3 3.8 %third.6.refs_11_ = f32[2,4,1,4,64,128]{5,4,3,2,1,0:T(8,128)S(1)} custom-call(s32[448]{0:T(512)S(1)} %reshape.72.refs_0_, s32[448]{0:T(512)S(1)} %reshape.73.refs_1_, s32[1]{0:T(128)} %bitcast.x_ref.refs_0_.refs_2_, bf16[16,128,256]{2,1,0:T(8,128)(2,1)S(1)} %copy-done.1, f32[64,128]{1,0:T(8,128)S(1)} %bitcast.22, ...), custom_call_target="tpu_custom_call" | custom-call | flops 1 | bytes 1 | tf_op jit(solution)/shard_map/third/pallas_call | solution.py:272
  90.2 4.0 %third.7 = f32[2,4,1,4,64,128]{5,4,3,2,1,0:T(8,128)S(1)} custom-call(s32[448]{0:T(512)S(1)} %reshape.72.refs_0_, s32[448]{0:T(512)S(1)} %reshape.73.refs_1_, s32[1]{0:T(128)} %bitcast.x_ref.refs_0_.refs_2_, bf16[16,128,256]{2,1,0:T(8,128)(2,1)S(1)} %copy-done.1, f32[64,128]{1,0:T(8,128)S(1)} %bitcast.23, ...), custom_call_target="tpu_custom_call", output_to_operand_aliasing={{}: (11, {})} | custom-call | flops 199999995904 | bytes 1 | tf_op jit(solution)/shard_map/third/pallas_call | solution.py:272
  95.1 4.9 %all-to-all-done.2 = f32[8,1,4,64,128]{4,3,2,1,0:T(8,128)} async-done(((f32[8,1,4,64,128]{4,3,2,1,0:T(8,128)}), f32[8,1,4,64,128]{4,3,2,1,0:T(8,128)}, u32[]{:S(2)}, u32[]{:S(2)}) %all-to-all-start.2) | async-done | bytes 1048608 | tf_op jit(solution)/shard_map/third/all_to_all | solution.py:695
  100.0 4.3 %all-to-all-start.1 = ((f32[8,1,4,64,128]{4,3,2,1,0:T(8,128)}), f32[8,1,4,64,128]{4,3,2,1,0:T(8,128)S(1)}, u32[]{:S(2)}, u32[]{:S(2)}) async-start(f32[8,1,4,64,128]{4,3,2,1,0:T(8,128)} %bitcast.14), calls=%async_computation.1 | async-start | bytes 2097152 | tf_op jit(solution)/shard_map/third/all_to_all | solution.py:695
  104.4 13.6 %all-to-all-done.1 = f32[8,1,4,64,128]{4,3,2,1,0:T(8,128)S(1)} async-done(((f32[8,1,4,64,128]{4,3,2,1,0:T(8,128)}), f32[8,1,4,64,128]{4,3,2,1,0:T(8,128)S(1)}, u32[]{:S(2)}, u32[]{:S(2)}) %all-to-all-start.1) | async-done | bytes 1048608 | tf_op jit(solution)/shard_map/third/all_to_all | solution.py:695
  118.0 2.7 %gram.2 = f32[1280,128]{1,0:T(8,128)S(1)} custom-call(f32[2,4,1,4,64,128]{5,4,3,2,1,0:T(8,128)S(1)} %bitcast.12, f32[2,4,1,4,64,128]{5,4,3,2,1,0:T(8,128)} %bitcast.8.refs_1_.refs_2_), custom_call_target="tpu_custom_call" | custom-call | flops 1 | bytes 1 | tf_op jit(solution)/shard_map/gram/pallas_call | solution.py:39
  124.5 2.1 %collective-permute-start.15 = (f32[160,128]{1,0:T(8,128)S(1)}, f32[160,128]{1,0:T(8,128)S(1)}, u32[]{:S(2)}, u32[]{:S(2)}) collective-permute-start(f32[160,128]{1,0:T(8,128)S(1)} %get-tuple-element.38), channel_id=1, source_target_pairs={{0,6},{2,0},{4,2},{6,4},{1,7},{3,1},{5,3},{7,5},{8,14},{10,8},{12,... | collective-permute-start | bytes 245768 | tf_op jit(solution)/shard_map/gram/ppermute | solution.py:595
  127.8 1.9 %collective-permute-done.15 = f32[160,128]{1,0:T(8,128)S(1)} collective-permute-done((f32[160,128]{1,0:T(8,128)S(1)}, f32[160,128]{1,0:T(8,128)S(1)}, u32[]{:S(2)}, u32[]{:S(2)}) %collective-permute-start.15) | collective-permute-done | bytes 81952 | tf_op jit(solution)/shard_map/gram/ppermute | solution.py:595
  129.8 3.3 %collective-permute-done.16 = f32[160,128]{1,0:T(8,128)S(1)} collective-permute-done((f32[160,128]{1,0:T(8,128)S(1)}, f32[160,128]{1,0:T(8,128)S(1)}, u32[]{:S(2)}, u32[]{:S(2)}) %collective-permute-start.16) | collective-permute-done | bytes 81952 | tf_op jit(solution)/shard_map/gram/ppermute | solution.py:582
  134.6 3.6 %collective-permute-done.17 = f32[160,128]{1,0:T(8,128)S(1)} collective-permute-done((f32[160,128]{1,0:T(8,128)S(1)}, f32[160,128]{1,0:T(8,128)S(1)}, u32[]{:S(2)}, u32[]{:S(2)}) %collective-permute-start.17) | collective-permute-done | bytes 81952 | tf_op jit(solution)/shard_map/gram/ppermute | solution.py:582
  141.6 1.9 %collective-permute-done.19 = f32[160,128]{1,0:T(8,128)S(1)} collective-permute-done((f32[160,128]{1,0:T(8,128)S(1)}, f32[160,128]{1,0:T(8,128)S(1)}, u32[]{:S(2)}, u32[]{:S(2)}) %collective-permute-start.19) | collective-permute-done | bytes 81952 | tf_op jit(solution)/shard_map/gram/ppermute | solution.py:602
  145.1 5.2 %collective-permute-start.21 = (f32[640,128]{1,0:T(8,128)S(1)}, f32[640,128]{1,0:T(8,128)S(1)}, u32[]{:S(2)}, u32[]{:S(2)}) collective-permute-start(f32[640,128]{1,0:T(8,128)S(1)} %constant_dynamic-update-slice_fusion.3), channel_id=1, source_target_pairs={{0,1},{1,0},{2,3},{3,2},{4,5},{5,4},{6,7},{7,6},{8,9},{9,8},{10,11... | collective-permute-start | bytes 983048 | tf_op jit(solution)/shard_map/gram/ppermute | solution.py:602
  150.3 1.8 %gram.3 = (bf16[2,4,128,512]{3,2,1,0:T(8,128)(2,1)S(1)}, bf16[2,4,128,512]{3,2,1,0:T(8,128)(2,1)S(1)}) custom-call(s32[1]{0:T(128)} %bitcast.x_ref.refs_0_.refs_2_, f32[2,4,1,4,64,128]{5,4,3,2,1,0:T(8,128)S(1)} %bitcast.13, f32[2,4,1,4,64,128]{5,4,3,2,1,0:T(8,128)} %bitcast.8.refs_1_.refs_2_), custom_call_target="tpu_custom_call" | custom-call | flops 1 | bytes 1 | tf_op jit(solution)/shard_map/gram/pallas_call | solution.py:39
  152.3 17.2 %finish.1 = f32[2,4,128,512]{3,2,1,0:T(8,128)} custom-call(f32[1280,128]{1,0:T(8,128)S(1)} %constant_dynamic-update-slice_fusion.7.refs_0_, bf16[2,4,128,512]{3,2,1,0:T(8,128)(2,1)S(1)} %get-tuple-element.33.refs_1_, bf16[2,4,128,512]{3,2,1,0:T(8,128)(2,1)S(1)} %get-tuple-element.34.refs_2_), custom_call_target="tpu_custom_call" | custom-call | flops 1 | bytes 1 | tf_op jit(solution)/shard_map/finish/pallas_call | solution.py:39
  (117 shorter events, 30.5 us)
Async XLA Ops:
  0.0 8.1 %copy-start.19 = (s32[2,7,16]{2,0,1:T(2,128)S(1)}, s32[2,7,16]{2,0,1:T(2,128)}, u32[]{:S(2)}) copy-start(s32[2,7,16]{2,0,1:T(2,128)} %param.10) | copy-start | bytes 2692
  1.6 6.5 %copy-start.16 = (f32[2,16,128]{2,1,0:T(8,128)S(1)}, f32[2,16,128]{2,1,0:T(8,128)}, u32[]{:S(2)}) copy-start(f32[2,16,128]{2,1,0:T(8,128)} %refs_2_.2) | copy-start | bytes 49156
  1.6 11.3 %copy-start.12 = (f32[16,128,128]{2,1,0:T(8,128)S(1)}, f32[16,128,128]{2,1,0:T(8,128)}, u32[]{:S(2)}) copy-start(f32[16,128,128]{2,1,0:T(8,128)} %refs_1_.4) | copy-start | bytes 3145732
  2.9 14.7 %collective-permute-start.3 = (f32[1,16,64,128]{3,2,1,0:T(8,128)S(1)}, f32[1,16,64,128]{3,2,1,0:T(8,128)S(1)}, u32[]{:S(2)}, u32[]{:S(2)}) collective-permute-start(f32[1,16,64,128]{3,2,1,0:T(8,128)S(1)} %get-tuple-element.20.refs_4_.refs_2_.refs_5_.refs_9_), channel_id=1, source_target_pairs={{0,24},{4,12},{8,0},{12,20},{16,8},{20,28},{24,16},{28,4},{1,25},{... | collective-permute-start | bytes 1572872 | tf_op jit(solution)/shard_map/prepare/ppermute | solution.py:629
  7.1 12.7 %collective-permute-start.2 = (f32[1,16,64,128]{3,2,1,0:T(8,128)}, f32[1,16,64,128]{3,2,1,0:T(8,128)S(1)}, u32[]{:S(2)}, u32[]{:S(2)}) collective-permute-start(f32[1,16,64,128]{3,2,1,0:T(8,128)} %get-tuple-element.24), channel_id=1, source_target_pairs={{0,4},{4,0},{1,5},{5,1},{2,6},{6,2},{3,7},{7,3},{8,12},{12,8},{9,1... | collective-permute-start | bytes 1572872 | tf_op jit(solution)/shard_map/prepare/ppermute | solution.py:70
  7.1 5.8 %collective-permute-start.1 = (f32[8,128]{1,0:T(8,128)S(1)}, f32[8,128]{1,0:T(8,128)S(1)}, u32[]{:S(2)}, u32[]{:S(2)}) collective-permute-start(f32[8,128]{1,0:T(8,128)S(1)} %get-tuple-element.21), channel_id=1, source_target_pairs={{0,1},{1,0},{2,3},{3,2},{4,5},{5,4},{6,7},{7,6},{8,9},{9,8},{10,11... | collective-permute-start | bytes 12296 | tf_op jit(solution)/shard_map/prepare/ppermute | solution.py:70
  8.1 18.9 %collective-permute-start = (f32[2,32,128]{2,1,0:T(8,128)S(1)}, f32[2,32,128]{2,1,0:T(8,128)S(1)}, u32[]{:S(2)}, u32[]{:S(2)}) collective-permute-start(f32[2,32,128]{2,1,0:T(8,128)S(1)} %prepare.7), channel_id=1, source_target_pairs={{0,4},{4,0},{1,5},{5,1},{2,6},{6,2},{3,7},{7,3},{8,12},{12,8},{9,1... | collective-permute-start | bytes 98312 | tf_op jit(solution)/shard_map/prepare/ppermute | solution.py:70
  20.6 16.4 %copy-start.1 = (bf16[16,128,256]{2,1,0:T(8,128)(2,1)S(1)}, bf16[16,128,256]{2,1,0:T(8,128)(2,1)}, u32[]{:S(2)}) copy-start(bf16[16,128,256]{2,1,0:T(8,128)(2,1)} %copy-done) | copy-start | bytes 3145732
  20.6 16.4 %copy-start.3 = (f32[1,16,64,128]{3,2,1,0:T(8,128)S(1)}, f32[1,16,64,128]{3,2,1,0:T(8,128)}, u32[]{:S(2)}) copy-start(f32[1,16,64,128]{3,2,1,0:T(8,128)} %prepare.10.refs_1_.refs_5_.refs_8_.refs_11_.refs_9_) | copy-start | bytes 1572868
  20.6 16.4 %copy-start.7 = (f32[1,16,64,128]{3,2,1,0:T(8,128)S(1)}, f32[1,16,64,128]{3,2,1,0:T(8,128)}, u32[]{:S(2)}) copy-start(f32[1,16,64,128]{3,2,1,0:T(8,128)} %copy-done.6) | copy-start | bytes 1572868
  20.6 19.6 %collective-permute-start.4 = (f32[1,16,64,128]{3,2,1,0:T(8,128)}, f32[1,16,64,128]{3,2,1,0:T(8,128)}, u32[]{:S(2)}, u32[]{:S(2)}) collective-permute-start(f32[1,16,64,128]{3,2,1,0:T(8,128)} %prepare.10.refs_1_.refs_5_.refs_8_.refs_11_.refs_9_), channel_id=1, source_target_pairs={{0,8},{4,28},{8,16},{12,4},{16,24},{20,12},{24,0},{28,20},{1,9},{5... | collective-permute-start | bytes 1572872 | tf_op jit(solution)/shard_map/prepare/ppermute | solution.py:629
  20.6 16.4 %collective-permute-start.5 = (f32[1,16,64,128]{3,2,1,0:T(8,128)}, f32[1,16,64,128]{3,2,1,0:T(8,128)}, u32[]{:S(2)}, u32[]{:S(2)}) collective-permute-start(f32[1,16,64,128]{3,2,1,0:T(8,128)} %prepare.11), channel_id=1, source_target_pairs={{0,4},{4,0},{1,5},{5,1},{2,6},{6,2},{3,7},{7,3},{8,12},{12,8},{9,1... | collective-permute-start | bytes 1572872 | tf_op jit(solution)/shard_map/prepare/ppermute | solution.py:70
  22.8 14.2 %all-to-all-start = ((f32[8,8,128]{2,1,0:T(8,128)}), f32[8,8,128]{2,1,0:T(8,128)S(1)}, u32[]{:S(2)}, u32[]{:S(2)}) async-start(f32[8,8,128]{2,1,0:T(8,128)} %broadcast_in_dim.43), calls=%async_computation | async-start | bytes 65536 | tf_op jit(solution)/shard_map/prepare/all_to_all | solution.py:665
  40.1 14.8 %collective-permute-start.6 = (f32[1,16,64,128]{3,2,1,0:T(8,128)S(1)}, f32[1,16,64,128]{3,2,1,0:T(8,128)S(1)}, u32[]{:S(2)}, u32[]{:S(2)}) collective-permute-start(f32[1,16,64,128]{3,2,1,0:T(8,128)S(1)} %first.3.refs_8_.refs_7_.refs_5_), channel_id=1, source_target_pairs={{0,8},{4,28},{8,16},{12,4},{16,24},{20,12},{24,0},{28,20},{1,9},{5... | collective-permute-start | bytes 1572872 | tf_op jit(solution)/shard_map/first/ppermute | solution.py:629
  43.3 25.2 %collective-permute-start.8 = (f32[1,16,64,128]{3,2,1,0:T(8,128)S(1)}, f32[1,16,64,128]{3,2,1,0:T(8,128)S(1)}, u32[]{:S(2)}, u32[]{:S(2)}) collective-permute-start(f32[1,16,64,128]{3,2,1,0:T(8,128)S(1)} %first.4.refs_9_.refs_5_), channel_id=1, source_target_pairs={{0,24},{4,12},{8,0},{12,20},{16,8},{20,28},{24,16},{28,4},{1,25},{... | collective-permute-start | bytes 1572872 | tf_op jit(solution)/shard_map/first/ppermute | solution.py:629
  59.2 9.2 %copy-start.8 = (f32[1,16,64,128]{3,2,1,0:T(8,128)S(1)}, f32[1,16,64,128]{3,2,1,0:T(8,128)}, u32[]{:S(2)}) copy-start(f32[1,16,64,128]{3,2,1,0:T(8,128)} %copy-done.6) | copy-start | bytes 1572868
  59.2 3.4 %collective-permute-start.7 = (f32[8,128]{1,0:T(8,128)S(1)}, f32[8,128]{1,0:T(8,128)S(1)}, u32[]{:S(2)}, u32[]{:S(2)}) collective-permute-start(f32[8,128]{1,0:T(8,128)S(1)} %second.5), channel_id=1, source_target_pairs={{0,1},{1,0},{2,3},{3,2},{4,5},{5,4},{6,7},{7,6},{8,9},{9,8},{10,11... | collective-permute-start | bytes 12296 | tf_op jit(solution)/shard_map/second/ppermute | solution.py:70
  61.8 24.5 %collective-permute-start.10 = (f32[1,16,64,128]{3,2,1,0:T(8,128)}, f32[1,16,64,128]{3,2,1,0:T(8,128)}, u32[]{:S(2)}, u32[]{:S(2)}) collective-permute-start(f32[1,16,64,128]{3,2,1,0:T(8,128)} %get-tuple-element.27.refs_0_.refs_5_), channel_id=1, source_target_pairs={{0,24},{4,12},{8,0},{12,20},{16,8},{20,28},{24,16},{28,4},{1,25},{... | collective-permute-start | bytes 1572872 | tf_op jit(solution)/shard_map/second/ppermute | solution.py:629
  72.3 17.9 %collective-permute-start.9 = (f32[1,16,64,128]{3,2,1,0:T(8,128)S(1)}, f32[1,16,64,128]{3,2,1,0:T(8,128)}, u32[]{:S(2)}, u32[]{:S(2)}) collective-permute-start(f32[1,16,64,128]{3,2,1,0:T(8,128)S(1)} %get-tuple-element.29.refs_0_.refs_7_.refs_5_), channel_id=1, source_target_pairs={{0,8},{4,28},{8,16},{12,4},{16,24},{20,12},{24,0},{28,20},{1,9},{5... | collective-permute-start | bytes 1572872 | tf_op jit(solution)/shard_map/third/ppermute | solution.py:629
  72.9 1.4 collective-permute-start.11
  81.7 18.3 %all-to-all-start.2 = ((f32[8,1,4,64,128]{4,3,2,1,0:T(8,128)}), f32[8,1,4,64,128]{4,3,2,1,0:T(8,128)}, u32[]{:S(2)}, u32[]{:S(2)}) async-start(f32[8,1,4,64,128]{4,3,2,1,0:T(8,128)} %bitcast.7), calls=%async_computation.2 | async-start | bytes 2097152 | tf_op jit(solution)/shard_map/third/all_to_all | solution.py:695
  100.0 17.9 %all-to-all-start.1 = ((f32[8,1,4,64,128]{4,3,2,1,0:T(8,128)}), f32[8,1,4,64,128]{4,3,2,1,0:T(8,128)S(1)}, u32[]{:S(2)}, u32[]{:S(2)}) async-start(f32[8,1,4,64,128]{4,3,2,1,0:T(8,128)} %bitcast.14), calls=%async_computation.1 | async-start | bytes 2097152 | tf_op jit(solution)/shard_map/third/all_to_all | solution.py:695
  120.7 2.2 %collective-permute-start.12 = (f32[640,128]{1,0:T(8,128)S(1)}, f32[640,128]{1,0:T(8,128)S(1)}, u32[]{:S(2)}, u32[]{:S(2)}) collective-permute-start(f32[640,128]{1,0:T(8,128)S(1)} %constant_dynamic-slice_fusion.3), channel_id=1, source_target_pairs={{0,1},{1,0},{2,3},{3,2},{4,5},{5,4},{6,7},{7,6},{8,9},{9,8},{10,11... | collective-permute-start | bytes 983048 | tf_op jit(solution)/shard_map/gram/ppermute | solution.py:595
  123.0 4.6 %collective-permute-start.13 = (f32[160,128]{1,0:T(8,128)S(1)}, f32[160,128]{1,0:T(8,128)S(1)}, u32[]{:S(2)}, u32[]{:S(2)}) collective-permute-start(f32[160,128]{1,0:T(8,128)S(1)} %get-tuple-element.37), channel_id=1, source_target_pairs={{0,2},{2,4},{4,6},{6,0},{1,3},{3,5},{5,7},{7,1},{8,10},{10,12},{12... | collective-permute-start | bytes 245768 | tf_op jit(solution)/shard_map/gram/ppermute | solution.py:595
  124.2 3.6 %collective-permute-start.14 = (f32[160,128]{1,0:T(8,128)S(1)}, f32[160,128]{1,0:T(8,128)S(1)}, u32[]{:S(2)}, u32[]{:S(2)}) collective-permute-start(f32[160,128]{1,0:T(8,128)S(1)} %get-tuple-element.39), channel_id=1, source_target_pairs={{0,4},{2,6},{4,0},{6,2},{1,5},{3,7},{5,1},{7,3},{8,12},{10,14},{12... | collective-permute-start | bytes 245768 | tf_op jit(solution)/shard_map/gram/ppermute | solution.py:595
  124.5 5.2 %collective-permute-start.15 = (f32[160,128]{1,0:T(8,128)S(1)}, f32[160,128]{1,0:T(8,128)S(1)}, u32[]{:S(2)}, u32[]{:S(2)}) collective-permute-start(f32[160,128]{1,0:T(8,128)S(1)} %get-tuple-element.38), channel_id=1, source_target_pairs={{0,6},{2,0},{4,2},{6,4},{1,7},{3,1},{5,3},{7,5},{8,14},{10,8},{12,... | collective-permute-start | bytes 245768 | tf_op jit(solution)/shard_map/gram/ppermute | solution.py:595
  129.7 3.4 %collective-permute-start.16 = (f32[160,128]{1,0:T(8,128)S(1)}, f32[160,128]{1,0:T(8,128)S(1)}, u32[]{:S(2)}, u32[]{:S(2)}) collective-permute-start(f32[160,128]{1,0:T(8,128)S(1)} %add_add_fusion), channel_id=1, source_target_pairs={{0,8},{8,0},{16,24},{24,16},{1,9},{9,1},{17,25},{25,17},{2,10},{10... | collective-permute-start | bytes 245768 | tf_op jit(solution)/shard_map/gram/ppermute | solution.py:582
  133.1 5.1 %collective-permute-start.17 = (f32[160,128]{1,0:T(8,128)S(1)}, f32[160,128]{1,0:T(8,128)S(1)}, u32[]{:S(2)}, u32[]{:S(2)}) collective-permute-start(f32[160,128]{1,0:T(8,128)S(1)} %add.142), channel_id=1, source_target_pairs={{0,16},{8,24},{16,0},{24,8},{1,17},{9,25},{17,1},{25,9},{2,18},{10... | collective-permute-start | bytes 245768 | tf_op jit(solution)/shard_map/gram/ppermute | solution.py:582
  138.3 3.3 %collective-permute-start.18 = (f32[160,128]{1,0:T(8,128)S(1)}, f32[160,128]{1,0:T(8,128)S(1)}, u32[]{:S(2)}, u32[]{:S(2)}) collective-permute-start(f32[160,128]{1,0:T(8,128)S(1)} %get-tuple-element.36), channel_id=1, source_target_pairs={{0,6},{2,0},{4,2},{6,4},{1,7},{3,1},{5,3},{7,5},{8,14},{10,8},{12,... | collective-permute-start | bytes 245768 | tf_op jit(solution)/shard_map/gram/ppermute | solution.py:602
  139.4 4.1 %collective-permute-start.19 = (f32[160,128]{1,0:T(8,128)S(1)}, f32[160,128]{1,0:T(8,128)S(1)}, u32[]{:S(2)}, u32[]{:S(2)}) collective-permute-start(f32[160,128]{1,0:T(8,128)S(1)} %get-tuple-element.36), channel_id=1, source_target_pairs={{0,4},{2,6},{4,0},{6,2},{1,5},{3,7},{5,1},{7,3},{8,12},{10,14},{12... | collective-permute-start | bytes 245768 | tf_op jit(solution)/shard_map/gram/ppermute | solution.py:602
  140.8 4.3 %collective-permute-start.20 = (f32[160,128]{1,0:T(8,128)S(1)}, f32[160,128]{1,0:T(8,128)S(1)}, u32[]{:S(2)}, u32[]{:S(2)}) collective-permute-start(f32[160,128]{1,0:T(8,128)S(1)} %get-tuple-element.36), channel_id=1, source_target_pairs={{0,2},{2,4},{4,6},{6,0},{1,3},{3,5},{5,7},{7,1},{8,10},{10,12},{12... | collective-permute-start | bytes 245768 | tf_op jit(solution)/shard_map/gram/ppermute | solution.py:602
  145.1 7.1 %collective-permute-start.21 = (f32[640,128]{1,0:T(8,128)S(1)}, f32[640,128]{1,0:T(8,128)S(1)}, u32[]{:S(2)}, u32[]{:S(2)}) collective-permute-start(f32[640,128]{1,0:T(8,128)S(1)} %constant_dynamic-update-slice_fusion.3), channel_id=1, source_target_pairs={{0,1},{1,0},{2,3},{3,2},{4,5},{5,4},{6,7},{7,6},{8,9},{9,8},{10,11... | collective-permute-start | bytes 983048 | tf_op jit(solution)/shard_map/gram/ppermute | solution.py:602
  (15 other events, 34.4 us)

commit v4 on v3

--- a/solution.py
+++ b/solution.py
@@ -246,7 +246,7 @@
                 out_ref[n, s] = result
             return carry
 
-        lax.fori_loop(0, sites, block, 0, unroll=4)
+        lax.fori_loop(0, sites, block, 0, unroll=16)
 
 
 def step(consts, pieces, order, layers_out, total, more=(), last_shape=None, number=1, after=(), cost=small, into=None):
@@ -292,14 +292,15 @@
     return [ref[a, b, layer, s] for b in range(ref.shape[1]) for a in range(2)]
 
 
-def gram_body(edge_ref, inner_ref, gram_ref, high, low):
-    _, _, inner_layers, share, half, orb = inner_ref.shape
+def gram_body(piece_ref, *refs):
+    *given, gram_ref, high, low = refs
+    _, states, layers, share, half, orb = piece_ref.shape
     col = 0
-    for chain in range(inner_layers + 1):
+    for layer in range(layers):
         for s in range(share):
-            for n, part in enumerate(all_states(edge_ref, inner_ref, chain, s)):
+            for n in range(2 * states):
                 at = (slice(n * half, (n + 1) * half), slice(col, col + orb))
-                high[at], low[at] = halves(part)
+                high[at], low[at] = halves(piece_ref[n % 2, n // 2, layer, s])
             col += orb
     count = high.shape[0]
     tile = gram_ref.shape[1]
@@ -308,8 +309,8 @@
     blocks = {}
     for i in range(0, count, wide):
         for j in range(0, i + 1, wide):
-            a = [r[i : i + wide, :] for r in (high, high, low)]
-            b = [r[j : j + wide, :] for r in (high, low, high)]
+            a = [r[i : i + wide, :] for r in (high, high, low, low)]
+            b = [r[j : j + wide, :] for r in (high, low, high, low)]
             blocks[i, j] = lax.dot_general(
                 jnp.concatenate(a, axis=1),
                 jnp.concatenate(b, axis=1),
@@ -319,9 +320,10 @@
     for i in range(0, count, tile):
         for j in range(0, i + 1, tile):
             block = blocks[i // wide * wide, j // wide * wide]
-            gram_ref[place : place + tile, :] = block[
-                i % wide : i % wide + tile, j % wide : j % wide + tile
-            ]
+            block = block[i % wide : i % wide + tile, j % wide : j % wide + tile]
+            for ref in given:
+                block = block + ref[place : place + tile, :]
+            gram_ref[place : place + tile, :] = block
             place += tile
 
 
@@ -710,18 +712,18 @@
         )
     start_in = jnp.concatenate([mine_i, theirs], axis=0)
     with jax.named_scope("second"):
+        in2, in1s = step(
+            consts, [one1, in1, four1], [[1], inside, [total]], inside, total,
+            [ends, mine_b, start_in, partner_b], number=2,
+        )
         one2, one1s = step(
             consts, [one1, in1, near1], [[1], inside, [0]], [1], total,
-            [ends, mine_b, start_in, near], number=2,
+            [ends, mine_b, start_in, near], number=2, after=(in2,),
         )
         far2 = z_move(one2, True)
-        in2, in1s = step(
-            consts, [one1, in1, four1], [[1], inside, [total]], inside, total,
-            [ends, mine_b, start_in, partner_b], number=2, after=(sent_after(one2),),
-        )
         four2, four1 = step(
             consts, [four1, in1, far1], [[total], inside, [total + 1]], [total], total,
-            [ends, partner_b, start_in, far], number=2, after=(in2,),
+            [ends, partner_b, start_in, far], number=2, after=(sent_after(one2),),
         )
     in1 = in1s
     with jax.named_scope("third"):
@@ -737,23 +739,28 @@
             consts, [four2, in2, far2], [[total], inside, [total + 1]], [total], total,
             [ends, four1, degree], edge_shape, number=3, after=(in3_local,),
         )
-        out3 = step(
+        out3_local = step(
             consts, [one2, in2, near2], [[1], inside, [0]], [1], total,
             [ends, one1s, degree], edge_shape, number=3, cost=large, into=four3,
         )
-        out3 = regroup(out3, group)
+        out3 = regroup(out3_local, group)
     pieces = (out3, in3)
     width = 2 * states * half
-    depth_rows = layers * share * orb
     tiles = width // orb
     with jax.named_scope("gram"):
-        gram = call(
-            gram_body,
-            pieces,
-            [vmem()] * 2,
-            jax.ShapeDtypeStruct((tiles * (tiles + 1) // 2 * orb, orb), f32),
-            [pltpu.VMEM((width, depth_rows), bf16)] * 2,
-        )
+        def gram_of(piece, given, after):
+            depth_rows = piece.shape[2] * share * orb
+            return call(
+                gram_body,
+                (piece, *given),
+                [vmem()] * (1 + len(given)),
+                jax.ShapeDtypeStruct((tiles * (tiles + 1) // 2 * orb, orb), f32),
+                [pltpu.VMEM((width, depth_rows), bf16)] * 2,
+                after,
+            )
+
+        gram = gram_of(in3, (), (sent_after(out3_local),))
+        gram = gram_of(out3, (gram,), ())
         high, low = call(
             rows_body,
             (x_arr, *pieces),

time: 170 us -> 164 us (0.965)
  Pallas kernels: 63.6 us -> 59.7 us
  local copies, waits for them, and re-layouts: 12.4 us -> 10.5 us
  waiting for transfers between devices: 50.1 us -> 48.3 us
    ppermute x6, waiting for transfers between devices: 3.15 us -> 7.97 us  [z_move(): return lax.ppermute(value, ('z', 'x'), pairs)]
    pallas_call x15 -> x17, Pallas kernels: 54.4 us -> 49.9 us  [call(): pl.pallas_call(kernel, out_shape=out_shape, in_specs=[*specs, *[pl.BlockS...]
    all_to_all x2, waiting for transfers between devices: 18.5 us -> 14.2 us  [regroup(): return lax.all_to_all(flat, axes, 0, 0, tiled=True).reshape(value.shape)]
    ppermute x2, waiting for transfers between devices: 6.91 us -> 4.39 us  [group_sum(): lax.ppermute(value, axes, [(i, i ^ hop) for i in range(count)])]
    unnamed x47 -> x45, local copies, waits for them, and re-layouts: 9.79 us -> 7.88 us
    ppermute x6 -> x7, starting transfers between devices: 7.43 us -> 8.07 us  [swap(): return lax.ppermute(value, axis, [(0, 1), (1, 0)])]
    ppermute x6 -> x7, waiting for transfers between devices: 3.66 us -> 3.83 us  [swap(): return lax.ppermute(value, axis, [(0, 1), (1, 0)])]
  transfers between devices with their start and end apart: 25 -> 26, of which waited for: 17 -> 19; matrix products, arithmetic and copies ran while one was open for 2% -> 2% of each run, Pallas kernels for 25% -> 25%
where the time goes in v4:
time: 164 us; the launch traced here: 163 us
  Pallas kernels  59.7 us (36%)
  waiting for transfers between devices  48.3 us (29%)
  starting transfers between devices  44.3 us (27%)
  local copies, waits for them, and re-layouts  10.5 us (6%)
    pallas_call x17, Pallas kernels, call(): pl.pallas_call(kernel, out_shape=out_shape, in_specs=[*specs, *[pl.BlockS...  49.9 us
    all_to_all x2, waiting for transfers between devices, regroup(): return lax.all_to_all(flat, axes, 0, 0, tiled=True).reshape(value.shape)  14.2 us
    all_to_all x1, waiting for transfers between devices, per_device(): ends = jnp.max(lax.all_to_all(ends, ('z', 'x'), 0, 0, tiled=True), axis=0)  9.35 us
    all_to_all x2, starting transfers between devices, regroup(): return lax.all_to_all(flat, axes, 0, 0, tiled=True).reshape(value.shape)  8.94 us
    pallas_call x2, Pallas kernels, step(): pl.pallas_call(kernel, out_shape=out, grid_spec=pltpu.PrefetchScalarGridS...  8.46 us
    ppermute x7, starting transfers between devices, swap(): return lax.ppermute(value, axis, [(0, 1), (1, 0)])  8.07 us
    ppermute x6, waiting for transfers between devices, z_move(): return lax.ppermute(value, ('z', 'x'), pairs)  7.97 us
    unnamed x45, local copies, waits for them, and re-layouts  7.88 us
  transfers between devices with their start and end apart: 26, of which 19 were waited for; matrix products, arithmetic and copies ran while one was open for 2% of the time, Pallas kernels for 25%

profile of v4, /device:TPU:1, one launch (start us, length us, event | category | flops | bytes accessed | tf_op | source)
XLA Modules:
  0.0 163.4 jit_solution(1759549691540125801)
XLA Ops:
  2.9 4.2 %collective-permute-start.3 = (f32[1,16,64,128]{3,2,1,0:T(8,128)S(1)}, f32[1,16,64,128]{3,2,1,0:T(8,128)S(1)}, u32[]{:S(2)}, u32[]{:S(2)}) collective-permute-start(f32[1,16,64,128]{3,2,1,0:T(8,128)S(1)} %get-tuple-element.20.refs_4_.refs_2_.refs_5_.refs_9_), channel_id=1, source_target_pairs={{0,24},{4,12},{8,0},{12,20},{16,8},{20,28},{24,16},{28,4},{1,25},{... | collective-permute-start | bytes 1572872 | tf_op jit(solution)/shard_map/prepare/ppermute | solution.py:631
  8.1 1.8 %collective-permute-start = (f32[2,32,128]{2,1,0:T(8,128)S(1)}, f32[2,32,128]{2,1,0:T(8,128)S(1)}, u32[]{:S(2)}, u32[]{:S(2)}) collective-permute-start(f32[2,32,128]{2,1,0:T(8,128)S(1)} %prepare.7), channel_id=1, source_target_pairs={{0,4},{4,0},{1,5},{5,1},{2,6},{6,2},{3,7},{7,3},{8,12},{12,8},{9,1... | collective-permute-start | bytes 98312 | tf_op jit(solution)/shard_map/prepare/ppermute | solution.py:70
  12.9 3.0 %prepare.8 = (bf16[16,128,256]{2,1,0:T(8,128)(2,1)S(1)}, f32[8,128]{1,0:T(8,128)S(1)}) custom-call(s32[224]{0:T(256)S(1)} %reshape.74.refs_0_, f32[16,128,128]{2,1,0:T(8,128)S(1)} %copy-done.11, f32[2,16,128]{2,1,0:T(8,128)S(1)} %copy-done.15, f32[8,128]{1,0:T(8,128)S(1)} %collective-permute-done.1.refs_3_), custom_call_target="tpu_custom_call" | custom-call | flops 1 | bytes 1 | tf_op jit(solution)/shard_map/prepare/pallas_call | solution.py:39
  17.7 2.1 %collective-permute-done.2.refs_0_ = f32[1,16,64,128]{3,2,1,0:T(8,128)S(1)} collective-permute-done((f32[1,16,64,128]{3,2,1,0:T(8,128)}, f32[1,16,64,128]{3,2,1,0:T(8,128)S(1)}, u32[]{:S(2)}, u32[]{:S(2)}) %collective-permute-start.2) | collective-permute-done | bytes 524320 | tf_op jit(solution)/shard_map/prepare/ppermute | solution.py:70
  22.8 4.2 %all-to-all-start = ((f32[8,8,128]{2,1,0:T(8,128)}), f32[8,8,128]{2,1,0:T(8,128)S(1)}, u32[]{:S(2)}, u32[]{:S(2)}) async-start(f32[8,8,128]{2,1,0:T(8,128)} %broadcast_in_dim.43), calls=%async_computation | async-start | bytes 65536 | tf_op jit(solution)/shard_map/prepare/all_to_all | solution.py:667
  27.6 9.3 %all-to-all-done = f32[8,8,128]{2,1,0:T(8,128)S(1)} async-done(((f32[8,8,128]{2,1,0:T(8,128)}), f32[8,8,128]{2,1,0:T(8,128)S(1)}, u32[]{:S(2)}, u32[]{:S(2)}) %all-to-all-start) | async-done | bytes 32800 | tf_op jit(solution)/shard_map/prepare/all_to_all | solution.py:667
  37.0 2.6 %first.3.refs_8_.refs_7_.refs_5_ = f32[1,16,64,128]{3,2,1,0:T(8,128)S(1)} custom-call(s32[448]{0:T(512)S(1)} %reshape.72.refs_0_, s32[448]{0:T(512)S(1)} %reshape.73.refs_1_, s32[1]{0:T(128)} %bitcast.x_ref.refs_0_.refs_2_, bf16[16,128,256]{2,1,0:T(8,128)(2,1)S(1)} %copy-done.1, f32[64,128]{1,0:T(8,128)S(1)} %bitcast.14, f32[1,16,64,128]{3,2,1,0:T(8,128)S(1)} %copy-done.3, ...), custom_call_target="tpu_custom_call" | custom-call | flops 1 | bytes 1 | tf_op jit(solution)/shard_map/first/pallas_call | solution.py:39
  39.7 2.6 %first.4.refs_9_.refs_5_ = f32[1,16,64,128]{3,2,1,0:T(8,128)S(1)} custom-call(s32[448]{0:T(512)S(1)} %reshape.72.refs_0_, s32[448]{0:T(512)S(1)} %reshape.73.refs_1_, s32[1]{0:T(128)} %bitcast.x_ref.refs_0_.refs_2_, bf16[16,128,256]{2,1,0:T(8,128)(2,1)S(1)} %copy-done.1, f32[64,128]{1,0:T(8,128)S(1)} %bitcast.15, ...), custom_call_target="tpu_custom_call" | custom-call | flops 1 | bytes 1 | tf_op jit(solution)/shard_map/first/pallas_call | solution.py:39
  42.2 3.3 %collective-permute-start.7 = (f32[1,16,64,128]{3,2,1,0:T(8,128)S(1)}, f32[1,16,64,128]{3,2,1,0:T(8,128)S(1)}, u32[]{:S(2)}, u32[]{:S(2)}) collective-permute-start(f32[1,16,64,128]{3,2,1,0:T(8,128)S(1)} %first.4.refs_9_.refs_5_), channel_id=1, source_target_pairs={{0,24},{4,12},{8,0},{12,20},{16,8},{20,28},{24,16},{28,4},{1,25},{... | collective-permute-start | bytes 1572872 | tf_op jit(solution)/shard_map/first/ppermute | solution.py:631
  46.6 3.7 %first.5.refs_6_ = f32[2,16,64,128]{3,2,1,0:T(8,128)S(1)} custom-call(s32[448]{0:T(512)S(1)} %reshape.72.refs_0_, s32[448]{0:T(512)S(1)} %reshape.73.refs_1_, s32[1]{0:T(128)} %bitcast.x_ref.refs_0_.refs_2_, bf16[16,128,256]{2,1,0:T(8,128)(2,1)S(1)} %copy-done.1, f32[64,128]{1,0:T(8,128)S(1)} %bitcast.16, ...), custom_call_target="tpu_custom_call" | custom-call | flops 1 | bytes 1 | tf_op jit(solution)/shard_map/first/pallas_call | solution.py:39
  50.4 3.8 %second.4 = (f32[2,16,64,128]{3,2,1,0:T(8,128)S(1)}, f32[2,16,64,128]{3,2,1,0:T(8,128)S(1)}) custom-call(s32[448]{0:T(512)S(1)} %reshape.72.refs_0_, s32[448]{0:T(512)S(1)} %reshape.73.refs_1_, s32[1]{0:T(128)} %bitcast.x_ref.refs_0_.refs_2_, bf16[16,128,256]{2,1,0:T(8,128)(2,1)S(1)} %copy-done.1, f32[64,128]{1,0:T(8,128)S(1)} %bitcast.17, ...), custom_call_target="tpu_custom_call" | custom-call | flops 1 | bytes 1 | tf_op jit(solution)/shard_map/second/pallas_call | solution.py:39
  54.4 4.0 %second.5 = (f32[1,16,64,128]{3,2,1,0:T(8,128)}, f32[1,16,64,128]{3,2,1,0:T(8,128)S(1)}) custom-call(s32[448]{0:T(512)S(1)} %reshape.72.refs_0_, s32[448]{0:T(512)S(1)} %reshape.73.refs_1_, s32[1]{0:T(128)} %bitcast.x_ref.refs_0_.refs_2_, bf16[16,128,256]{2,1,0:T(8,128)(2,1)S(1)} %copy-done.1, f32[64,128]{1,0:T(8,128)S(1)} %bitcast.18, ...), custom_call_target="tpu_custom_call" | custom-call | flops 1 | bytes 1 | tf_op jit(solution)/shard_map/second/pallas_call | solution.py:39
  58.4 2.5 %collective-permute-start.8 = (f32[8,128]{1,0:T(8,128)S(1)}, f32[8,128]{1,0:T(8,128)S(1)}, u32[]{:S(2)}, u32[]{:S(2)}) collective-permute-start(f32[8,128]{1,0:T(8,128)S(1)} %second.6), channel_id=1, source_target_pairs={{0,1},{1,0},{2,3},{3,2},{4,5},{5,4},{6,7},{7,6},{8,9},{9,8},{10,11... | collective-permute-start | bytes 12296 | tf_op jit(solution)/shard_map/second/ppermute | solution.py:70
  60.9 5.7 %collective-permute-done.7.refs_7_ = f32[1,16,64,128]{3,2,1,0:T(8,128)S(1)} collective-permute-done((f32[1,16,64,128]{3,2,1,0:T(8,128)S(1)}, f32[1,16,64,128]{3,2,1,0:T(8,128)S(1)}, u32[]{:S(2)}, u32[]{:S(2)}) %collective-permute-start.7) | collective-permute-done | bytes 524320 | tf_op jit(solution)/shard_map/first/ppermute | solution.py:631
  66.6 2.5 %second.7 = (f32[1,16,64,128]{3,2,1,0:T(8,128)S(1)}, f32[1,16,64,128]{3,2,1,0:T(8,128)S(1)}) custom-call(s32[448]{0:T(512)S(1)} %reshape.72.refs_0_, s32[448]{0:T(512)S(1)} %reshape.73.refs_1_, s32[1]{0:T(128)} %bitcast.x_ref.refs_0_.refs_2_, bf16[16,128,256]{2,1,0:T(8,128)(2,1)S(1)} %copy-done.1, f32[64,128]{1,0:T(8,128)S(1)} %bitcast.19, ...), custom_call_target="tpu_custom_call" | custom-call | flops 1 | bytes 1 | tf_op jit(solution)/shard_map/second/pallas_call | solution.py:39
  73.2 4.9 %third.5.refs_11_ = f32[2,4,1,4,64,128]{5,4,3,2,1,0:T(8,128)} custom-call(s32[448]{0:T(512)S(1)} %reshape.72.refs_0_, s32[448]{0:T(512)S(1)} %reshape.73.refs_1_, s32[1]{0:T(128)} %bitcast.x_ref.refs_0_.refs_2_, bf16[16,128,256]{2,1,0:T(8,128)(2,1)S(1)} %copy-done.1, f32[64,128]{1,0:T(8,128)S(1)} %bitcast.20, ...), custom_call_target="tpu_custom_call" | custom-call | flops 1 | bytes 1 | tf_op jit(solution)/shard_map/third/pallas_call | solution.py:39
  78.1 4.6 %all-to-all-start.2 = ((f32[8,1,4,64,128]{4,3,2,1,0:T(8,128)}), f32[8,1,4,64,128]{4,3,2,1,0:T(8,128)}, u32[]{:S(2)}, u32[]{:S(2)}) async-start(f32[8,1,4,64,128]{4,3,2,1,0:T(8,128)} %bitcast.7), calls=%async_computation.2 | async-start | bytes 2097152 | tf_op jit(solution)/shard_map/third/all_to_all | solution.py:697
  82.8 4.1 %third.6.refs_11_ = f32[2,4,1,4,64,128]{5,4,3,2,1,0:T(8,128)} custom-call(s32[448]{0:T(512)S(1)} %reshape.72.refs_0_, s32[448]{0:T(512)S(1)} %reshape.73.refs_1_, s32[1]{0:T(128)} %bitcast.x_ref.refs_0_.refs_2_, bf16[16,128,256]{2,1,0:T(8,128)(2,1)S(1)} %copy-done.1, f32[64,128]{1,0:T(8,128)S(1)} %bitcast.21, ...), custom_call_target="tpu_custom_call" | custom-call | flops 1 | bytes 1 | tf_op jit(solution)/shard_map/third/pallas_call | solution.py:272
  88.2 4.3 %third.7.refs_0_ = f32[2,4,1,4,64,128]{5,4,3,2,1,0:T(8,128)} custom-call(s32[448]{0:T(512)S(1)} %reshape.72.refs_0_, s32[448]{0:T(512)S(1)} %reshape.73.refs_1_, s32[1]{0:T(128)} %bitcast.x_ref.refs_0_.refs_2_, bf16[16,128,256]{2,1,0:T(8,128)(2,1)S(1)} %copy-done.1, f32[64,128]{1,0:T(8,128)S(1)} %bitcast.22, ...), custom_call_target="tpu_custom_call", output_to_operand_aliasing={{}: (11, {})} | custom-call | flops 199999995904 | bytes 1 | tf_op jit(solution)/shard_map/third/pallas_call | solution.py:272
  92.5 4.0 %all-to-all-done.2 = f32[8,1,4,64,128]{4,3,2,1,0:T(8,128)} async-done(((f32[8,1,4,64,128]{4,3,2,1,0:T(8,128)}), f32[8,1,4,64,128]{4,3,2,1,0:T(8,128)}, u32[]{:S(2)}, u32[]{:S(2)}) %all-to-all-start.2) | async-done | bytes 1048608 | tf_op jit(solution)/shard_map/third/all_to_all | solution.py:697
  96.5 4.3 %all-to-all-start.1 = ((f32[8,1,4,64,128]{4,3,2,1,0:T(8,128)}), f32[8,1,4,64,128]{4,3,2,1,0:T(8,128)S(1)}, u32[]{:S(2)}, u32[]{:S(2)}) async-start(f32[8,1,4,64,128]{4,3,2,1,0:T(8,128)} %bitcast.4), calls=%async_computation.1 | async-start | bytes 2097152 | tf_op jit(solution)/shard_map/third/all_to_all | solution.py:697
  102.0 2.2 %gram.5.refs_1_ = f32[1280,128]{1,0:T(8,128)S(1)} custom-call(f32[2,4,1,4,64,128]{5,4,3,2,1,0:T(8,128)} %bitcast.8.refs_0_.refs_2_, f32[8,128]{1,0:T(8,128)S(1)} %collective-permute-done.12.refs_1_), custom_call_target="tpu_custom_call" | custom-call | flops 1 | bytes 1 | tf_op jit(solution)/shard_map/gram/pallas_call | solution.py:39
  104.2 10.2 %all-to-all-done.1 = f32[8,1,4,64,128]{4,3,2,1,0:T(8,128)S(1)} async-done(((f32[8,1,4,64,128]{4,3,2,1,0:T(8,128)}), f32[8,1,4,64,128]{4,3,2,1,0:T(8,128)S(1)}, u32[]{:S(2)}, u32[]{:S(2)}) %all-to-all-start.1) | async-done | bytes 1048608 | tf_op jit(solution)/shard_map/third/all_to_all | solution.py:697
  119.3 2.1 %collective-permute-start.16 = (f32[160,128]{1,0:T(8,128)S(1)}, f32[160,128]{1,0:T(8,128)S(1)}, u32[]{:S(2)}, u32[]{:S(2)}) collective-permute-start(f32[160,128]{1,0:T(8,128)S(1)} %get-tuple-element.38), channel_id=1, source_target_pairs={{0,6},{2,0},{4,2},{6,4},{1,7},{3,1},{5,3},{7,5},{8,14},{10,8},{12,... | collective-permute-start | bytes 245768 | tf_op jit(solution)/shard_map/gram/ppermute | solution.py:597
  122.6 1.9 %collective-permute-done.16 = f32[160,128]{1,0:T(8,128)S(1)} collective-permute-done((f32[160,128]{1,0:T(8,128)S(1)}, f32[160,128]{1,0:T(8,128)S(1)}, u32[]{:S(2)}, u32[]{:S(2)}) %collective-permute-start.16) | collective-permute-done | bytes 81952 | tf_op jit(solution)/shard_map/gram/ppermute | solution.py:597
  125.8 2.0 %collective-permute-done.17 = f32[160,128]{1,0:T(8,128)S(1)} collective-permute-done((f32[160,128]{1,0:T(8,128)S(1)}, f32[160,128]{1,0:T(8,128)S(1)}, u32[]{:S(2)}, u32[]{:S(2)}) %collective-permute-start.17) | collective-permute-done | bytes 81952 | tf_op jit(solution)/shard_map/gram/ppermute | solution.py:584
  127.9 1.9 %collective-permute-start.18 = (f32[160,128]{1,0:T(8,128)S(1)}, f32[160,128]{1,0:T(8,128)S(1)}, u32[]{:S(2)}, u32[]{:S(2)}) collective-permute-start(f32[160,128]{1,0:T(8,128)S(1)} %add.142), channel_id=1, source_target_pairs={{0,16},{8,24},{16,0},{24,8},{1,17},{9,25},{17,1},{25,9},{2,18},{10... | collective-permute-start | bytes 245768 | tf_op jit(solution)/shard_map/gram/ppermute | solution.py:584
  129.8 2.4 %collective-permute-done.18 = f32[160,128]{1,0:T(8,128)S(1)} collective-permute-done((f32[160,128]{1,0:T(8,128)S(1)}, f32[160,128]{1,0:T(8,128)S(1)}, u32[]{:S(2)}, u32[]{:S(2)}) %collective-permute-start.18) | collective-permute-done | bytes 81952 | tf_op jit(solution)/shard_map/gram/ppermute | solution.py:584
  135.5 1.9 %collective-permute-done.20 = f32[160,128]{1,0:T(8,128)S(1)} collective-permute-done((f32[160,128]{1,0:T(8,128)S(1)}, f32[160,128]{1,0:T(8,128)S(1)}, u32[]{:S(2)}, u32[]{:S(2)}) %collective-permute-start.20) | collective-permute-done | bytes 81952 | tf_op jit(solution)/shard_map/gram/ppermute | solution.py:604
  139.0 5.2 %collective-permute-start.22 = (f32[640,128]{1,0:T(8,128)S(1)}, f32[640,128]{1,0:T(8,128)S(1)}, u32[]{:S(2)}, u32[]{:S(2)}) collective-permute-start(f32[640,128]{1,0:T(8,128)S(1)} %constant_dynamic-update-slice_fusion.3), channel_id=1, source_target_pairs={{0,1},{1,0},{2,3},{3,2},{4,5},{5,4},{6,7},{7,6},{8,9},{9,8},{10,11... | collective-permute-start | bytes 983048 | tf_op jit(solution)/shard_map/gram/ppermute | solution.py:604
  144.2 1.8 %gram.7 = (bf16[2,4,128,512]{3,2,1,0:T(8,128)(2,1)S(1)}, bf16[2,4,128,512]{3,2,1,0:T(8,128)(2,1)S(1)}) custom-call(s32[1]{0:T(128)} %bitcast.x_ref.refs_0_.refs_2_, f32[2,4,1,4,64,128]{5,4,3,2,1,0:T(8,128)S(1)} %bitcast.13, f32[2,4,1,4,64,128]{5,4,3,2,1,0:T(8,128)} %bitcast.8.refs_0_.refs_2_), custom_call_target="tpu_custom_call" | custom-call | flops 1 | bytes 1 | tf_op jit(solution)/shard_map/gram/pallas_call | solution.py:39
  146.2 17.2 %finish.1 = f32[2,4,128,512]{3,2,1,0:T(8,128)} custom-call(f32[1280,128]{1,0:T(8,128)S(1)} %constant_dynamic-update-slice_fusion.7.refs_0_, bf16[2,4,128,512]{3,2,1,0:T(8,128)(2,1)S(1)} %get-tuple-element.33.refs_1_, bf16[2,4,128,512]{3,2,1,0:T(8,128)(2,1)S(1)} %get-tuple-element.34.refs_2_), custom_call_target="tpu_custom_call" | custom-call | flops 1 | bytes 1 | tf_op jit(solution)/shard_map/finish/pallas_call | solution.py:39
  (119 shorter events, 32.7 us)
Async XLA Ops:
  1.6 11.3 %copy-start.11 = (f32[16,128,128]{2,1,0:T(8,128)S(1)}, f32[16,128,128]{2,1,0:T(8,128)}, u32[]{:S(2)}) copy-start(f32[16,128,128]{2,1,0:T(8,128)} %refs_1_.4) | copy-start | bytes 3145732
  2.9 14.7 %collective-permute-start.3 = (f32[1,16,64,128]{3,2,1,0:T(8,128)S(1)}, f32[1,16,64,128]{3,2,1,0:T(8,128)S(1)}, u32[]{:S(2)}, u32[]{:S(2)}) collective-permute-start(f32[1,16,64,128]{3,2,1,0:T(8,128)S(1)} %get-tuple-element.20.refs_4_.refs_2_.refs_5_.refs_9_), channel_id=1, source_target_pairs={{0,24},{4,12},{8,0},{12,20},{16,8},{20,28},{24,16},{28,4},{1,25},{... | collective-permute-start | bytes 1572872 | tf_op jit(solution)/shard_map/prepare/ppermute | solution.py:631
  7.1 12.7 %collective-permute-start.2 = (f32[1,16,64,128]{3,2,1,0:T(8,128)}, f32[1,16,64,128]{3,2,1,0:T(8,128)S(1)}, u32[]{:S(2)}, u32[]{:S(2)}) collective-permute-start(f32[1,16,64,128]{3,2,1,0:T(8,128)} %get-tuple-element.24), channel_id=1, source_target_pairs={{0,4},{4,0},{1,5},{5,1},{2,6},{6,2},{3,7},{7,3},{8,12},{12,8},{9,1... | collective-permute-start | bytes 1572872 | tf_op jit(solution)/shard_map/prepare/ppermute | solution.py:70
  7.1 5.8 %collective-permute-start.1 = (f32[8,128]{1,0:T(8,128)S(1)}, f32[8,128]{1,0:T(8,128)S(1)}, u32[]{:S(2)}, u32[]{:S(2)}) collective-permute-start(f32[8,128]{1,0:T(8,128)S(1)} %get-tuple-element.21), channel_id=1, source_target_pairs={{0,1},{1,0},{2,3},{3,2},{4,5},{5,4},{6,7},{7,6},{8,9},{9,8},{10,11... | collective-permute-start | bytes 12296 | tf_op jit(solution)/shard_map/prepare/ppermute | solution.py:70
  8.1 18.9 %collective-permute-start = (f32[2,32,128]{2,1,0:T(8,128)S(1)}, f32[2,32,128]{2,1,0:T(8,128)S(1)}, u32[]{:S(2)}, u32[]{:S(2)}) collective-permute-start(f32[2,32,128]{2,1,0:T(8,128)S(1)} %prepare.7), channel_id=1, source_target_pairs={{0,4},{4,0},{1,5},{5,1},{2,6},{6,2},{3,7},{7,3},{8,12},{12,8},{9,1... | collective-permute-start | bytes 98312 | tf_op jit(solution)/shard_map/prepare/ppermute | solution.py:70
  20.6 16.4 %copy-start.1 = (bf16[16,128,256]{2,1,0:T(8,128)(2,1)S(1)}, bf16[16,128,256]{2,1,0:T(8,128)(2,1)}, u32[]{:S(2)}) copy-start(bf16[16,128,256]{2,1,0:T(8,128)(2,1)} %copy-done) | copy-start | bytes 3145732
  20.6 16.4 %copy-start.3 = (f32[1,16,64,128]{3,2,1,0:T(8,128)S(1)}, f32[1,16,64,128]{3,2,1,0:T(8,128)}, u32[]{:S(2)}) copy-start(f32[1,16,64,128]{3,2,1,0:T(8,128)} %prepare.10.refs_1_.refs_5_.refs_8_.refs_11_.refs_9_) | copy-start | bytes 1572868
  20.6 16.4 %copy-start.7 = (f32[1,16,64,128]{3,2,1,0:T(8,128)S(1)}, f32[1,16,64,128]{3,2,1,0:T(8,128)}, u32[]{:S(2)}) copy-start(f32[1,16,64,128]{3,2,1,0:T(8,128)} %copy-done.6) | copy-start | bytes 1572868
  20.6 19.1 %collective-permute-start.4 = (f32[1,16,64,128]{3,2,1,0:T(8,128)}, f32[1,16,64,128]{3,2,1,0:T(8,128)}, u32[]{:S(2)}, u32[]{:S(2)}) collective-permute-start(f32[1,16,64,128]{3,2,1,0:T(8,128)} %prepare.10.refs_1_.refs_5_.refs_8_.refs_11_.refs_9_), channel_id=1, source_target_pairs={{0,8},{4,28},{8,16},{12,4},{16,24},{20,12},{24,0},{28,20},{1,9},{5... | collective-permute-start | bytes 1572872 | tf_op jit(solution)/shard_map/prepare/ppermute | solution.py:631
  20.6 16.4 %collective-permute-start.5 = (f32[1,16,64,128]{3,2,1,0:T(8,128)}, f32[1,16,64,128]{3,2,1,0:T(8,128)}, u32[]{:S(2)}, u32[]{:S(2)}) collective-permute-start(f32[1,16,64,128]{3,2,1,0:T(8,128)} %prepare.11), channel_id=1, source_target_pairs={{0,4},{4,0},{1,5},{5,1},{2,6},{6,2},{3,7},{7,3},{8,12},{12,8},{9,1... | collective-permute-start | bytes 1572872 | tf_op jit(solution)/shard_map/prepare/ppermute | solution.py:70
  22.8 14.2 %all-to-all-start = ((f32[8,8,128]{2,1,0:T(8,128)}), f32[8,8,128]{2,1,0:T(8,128)S(1)}, u32[]{:S(2)}, u32[]{:S(2)}) async-start(f32[8,8,128]{2,1,0:T(8,128)} %broadcast_in_dim.43), calls=%async_computation | async-start | bytes 65536 | tf_op jit(solution)/shard_map/prepare/all_to_all | solution.py:667
  39.6 14.8 %collective-permute-start.6 = (f32[1,16,64,128]{3,2,1,0:T(8,128)S(1)}, f32[1,16,64,128]{3,2,1,0:T(8,128)S(1)}, u32[]{:S(2)}, u32[]{:S(2)}) collective-permute-start(f32[1,16,64,128]{3,2,1,0:T(8,128)S(1)} %first.3.refs_8_.refs_7_.refs_5_), channel_id=1, source_target_pairs={{0,8},{4,28},{8,16},{12,4},{16,24},{20,12},{24,0},{28,20},{1,9},{5... | collective-permute-start | bytes 1572872 | tf_op jit(solution)/shard_map/first/ppermute | solution.py:631
  42.2 24.4 %collective-permute-start.7 = (f32[1,16,64,128]{3,2,1,0:T(8,128)S(1)}, f32[1,16,64,128]{3,2,1,0:T(8,128)S(1)}, u32[]{:S(2)}, u32[]{:S(2)}) collective-permute-start(f32[1,16,64,128]{3,2,1,0:T(8,128)S(1)} %first.4.refs_9_.refs_5_), channel_id=1, source_target_pairs={{0,24},{4,12},{8,0},{12,20},{16,8},{20,28},{24,16},{28,4},{1,25},{... | collective-permute-start | bytes 1572872 | tf_op jit(solution)/shard_map/first/ppermute | solution.py:631
  54.4 12.2 %copy-start.8 = (f32[1,16,64,128]{3,2,1,0:T(8,128)S(1)}, f32[1,16,64,128]{3,2,1,0:T(8,128)}, u32[]{:S(2)}) copy-start(f32[1,16,64,128]{3,2,1,0:T(8,128)} %copy-done.6) | copy-start | bytes 1572868
  58.4 12.7 %copy-start.20 = (s32[128]{0:T(128)S(1)}, s32[128]{0:T(128)}, u32[]{:S(2)}) copy-start(s32[128]{0:T(128)} %param.11) | copy-start | bytes 1540
  58.4 8.2 %collective-permute-start.8 = (f32[8,128]{1,0:T(8,128)S(1)}, f32[8,128]{1,0:T(8,128)S(1)}, u32[]{:S(2)}, u32[]{:S(2)}) collective-permute-start(f32[8,128]{1,0:T(8,128)S(1)} %second.6), channel_id=1, source_target_pairs={{0,1},{1,0},{2,3},{3,2},{4,5},{5,4},{6,7},{7,6},{8,9},{9,8},{10,11... | collective-permute-start | bytes 12296 | tf_op jit(solution)/shard_map/second/ppermute | solution.py:70
  60.9 21.8 %collective-permute-start.10 = (f32[1,16,64,128]{3,2,1,0:T(8,128)}, f32[1,16,64,128]{3,2,1,0:T(8,128)}, u32[]{:S(2)}, u32[]{:S(2)}) collective-permute-start(f32[1,16,64,128]{3,2,1,0:T(8,128)} %get-tuple-element.28.refs_0_.refs_5_), channel_id=1, source_target_pairs={{0,24},{4,12},{8,0},{12,20},{16,8},{20,28},{24,16},{28,4},{1,25},{... | collective-permute-start | bytes 1572872 | tf_op jit(solution)/shard_map/second/ppermute | solution.py:631
  70.0 18.2 %collective-permute-start.9 = (f32[1,16,64,128]{3,2,1,0:T(8,128)S(1)}, f32[1,16,64,128]{3,2,1,0:T(8,128)}, u32[]{:S(2)}, u32[]{:S(2)}) collective-permute-start(f32[1,16,64,128]{3,2,1,0:T(8,128)S(1)} %get-tuple-element.29.refs_0_.refs_7_.refs_5_), channel_id=1, source_target_pairs={{0,8},{4,28},{8,16},{12,4},{16,24},{20,12},{24,0},{28,20},{1,9},{5... | collective-permute-start | bytes 1572872 | tf_op jit(solution)/shard_map/third/ppermute | solution.py:631
  70.0 2.0 %collective-permute-start.11 = (f32[8,128]{1,0:T(8,128)S(1)}, f32[8,128]{1,0:T(8,128)S(1)}, u32[]{:S(2)}, u32[]{:S(2)}) collective-permute-start(f32[8,128]{1,0:T(8,128)S(1)} %third.4), channel_id=1, source_target_pairs={{0,1},{1,0},{2,3},{3,2},{4,5},{5,4},{6,7},{7,6},{8,9},{9,8},{10,11... | collective-permute-start | bytes 12296 | tf_op jit(solution)/shard_map/third/ppermute | solution.py:70
  78.1 18.3 %all-to-all-start.2 = ((f32[8,1,4,64,128]{4,3,2,1,0:T(8,128)}), f32[8,1,4,64,128]{4,3,2,1,0:T(8,128)}, u32[]{:S(2)}, u32[]{:S(2)}) async-start(f32[8,1,4,64,128]{4,3,2,1,0:T(8,128)} %bitcast.7), calls=%async_computation.2 | async-start | bytes 2097152 | tf_op jit(solution)/shard_map/third/all_to_all | solution.py:697
  96.5 17.9 %all-to-all-start.1 = ((f32[8,1,4,64,128]{4,3,2,1,0:T(8,128)}), f32[8,1,4,64,128]{4,3,2,1,0:T(8,128)S(1)}, u32[]{:S(2)}, u32[]{:S(2)}) async-start(f32[8,1,4,64,128]{4,3,2,1,0:T(8,128)} %bitcast.4), calls=%async_computation.1 | async-start | bytes 2097152 | tf_op jit(solution)/shard_map/third/all_to_all | solution.py:697
  100.8 1.2 collective-permute-start.12
  115.5 2.2 %collective-permute-start.13 = (f32[640,128]{1,0:T(8,128)S(1)}, f32[640,128]{1,0:T(8,128)S(1)}, u32[]{:S(2)}, u32[]{:S(2)}) collective-permute-start(f32[640,128]{1,0:T(8,128)S(1)} %constant_dynamic-slice_fusion.3), channel_id=1, source_target_pairs={{0,1},{1,0},{2,3},{3,2},{4,5},{5,4},{6,7},{7,6},{8,9},{9,8},{10,11... | collective-permute-start | bytes 983048 | tf_op jit(solution)/shard_map/gram/ppermute | solution.py:597
  117.7 4.6 %collective-permute-start.14 = (f32[160,128]{1,0:T(8,128)S(1)}, f32[160,128]{1,0:T(8,128)S(1)}, u32[]{:S(2)}, u32[]{:S(2)}) collective-permute-start(f32[160,128]{1,0:T(8,128)S(1)} %get-tuple-element.37), channel_id=1, source_target_pairs={{0,2},{2,4},{4,6},{6,0},{1,3},{3,5},{5,7},{7,1},{8,10},{10,12},{12... | collective-permute-start | bytes 245768 | tf_op jit(solution)/shard_map/gram/ppermute | solution.py:597
  119.0 3.6 %collective-permute-start.15 = (f32[160,128]{1,0:T(8,128)S(1)}, f32[160,128]{1,0:T(8,128)S(1)}, u32[]{:S(2)}, u32[]{:S(2)}) collective-permute-start(f32[160,128]{1,0:T(8,128)S(1)} %get-tuple-element.39), channel_id=1, source_target_pairs={{0,4},{2,6},{4,0},{6,2},{1,5},{3,7},{5,1},{7,3},{8,12},{10,14},{12... | collective-permute-start | bytes 245768 | tf_op jit(solution)/shard_map/gram/ppermute | solution.py:597
  119.3 5.2 %collective-permute-start.16 = (f32[160,128]{1,0:T(8,128)S(1)}, f32[160,128]{1,0:T(8,128)S(1)}, u32[]{:S(2)}, u32[]{:S(2)}) collective-permute-start(f32[160,128]{1,0:T(8,128)S(1)} %get-tuple-element.38), channel_id=1, source_target_pairs={{0,6},{2,0},{4,2},{6,4},{1,7},{3,1},{5,3},{7,5},{8,14},{10,8},{12,... | collective-permute-start | bytes 245768 | tf_op jit(solution)/shard_map/gram/ppermute | solution.py:597
  124.5 3.4 %collective-permute-start.17 = (f32[160,128]{1,0:T(8,128)S(1)}, f32[160,128]{1,0:T(8,128)S(1)}, u32[]{:S(2)}, u32[]{:S(2)}) collective-permute-start(f32[160,128]{1,0:T(8,128)S(1)} %add_add_fusion), channel_id=1, source_target_pairs={{0,8},{8,0},{16,24},{24,16},{1,9},{9,1},{17,25},{25,17},{2,10},{10... | collective-permute-start | bytes 245768 | tf_op jit(solution)/shard_map/gram/ppermute | solution.py:584
  127.9 4.3 %collective-permute-start.18 = (f32[160,128]{1,0:T(8,128)S(1)}, f32[160,128]{1,0:T(8,128)S(1)}, u32[]{:S(2)}, u32[]{:S(2)}) collective-permute-start(f32[160,128]{1,0:T(8,128)S(1)} %add.142), channel_id=1, source_target_pairs={{0,16},{8,24},{16,0},{24,8},{1,17},{9,25},{17,1},{25,9},{2,18},{10... | collective-permute-start | bytes 245768 | tf_op jit(solution)/shard_map/gram/ppermute | solution.py:584
  132.2 3.3 %collective-permute-start.19 = (f32[160,128]{1,0:T(8,128)S(1)}, f32[160,128]{1,0:T(8,128)S(1)}, u32[]{:S(2)}, u32[]{:S(2)}) collective-permute-start(f32[160,128]{1,0:T(8,128)S(1)} %get-tuple-element.36), channel_id=1, source_target_pairs={{0,6},{2,0},{4,2},{6,4},{1,7},{3,1},{5,3},{7,5},{8,14},{10,8},{12,... | collective-permute-start | bytes 245768 | tf_op jit(solution)/shard_map/gram/ppermute | solution.py:604
  133.3 4.1 %collective-permute-start.20 = (f32[160,128]{1,0:T(8,128)S(1)}, f32[160,128]{1,0:T(8,128)S(1)}, u32[]{:S(2)}, u32[]{:S(2)}) collective-permute-start(f32[160,128]{1,0:T(8,128)S(1)} %get-tuple-element.36), channel_id=1, source_target_pairs={{0,4},{2,6},{4,0},{6,2},{1,5},{3,7},{5,1},{7,3},{8,12},{10,14},{12... | collective-permute-start | bytes 245768 | tf_op jit(solution)/shard_map/gram/ppermute | solution.py:604
  134.7 4.3 %collective-permute-start.21 = (f32[160,128]{1,0:T(8,128)S(1)}, f32[160,128]{1,0:T(8,128)S(1)}, u32[]{:S(2)}, u32[]{:S(2)}) collective-permute-start(f32[160,128]{1,0:T(8,128)S(1)} %get-tuple-element.36), channel_id=1, source_target_pairs={{0,2},{2,4},{4,6},{6,0},{1,3},{3,5},{5,7},{7,1},{8,10},{10,12},{12... | collective-permute-start | bytes 245768 | tf_op jit(solution)/shard_map/gram/ppermute | solution.py:604
  139.0 7.1 %collective-permute-start.22 = (f32[640,128]{1,0:T(8,128)S(1)}, f32[640,128]{1,0:T(8,128)S(1)}, u32[]{:S(2)}, u32[]{:S(2)}) collective-permute-start(f32[640,128]{1,0:T(8,128)S(1)} %constant_dynamic-update-slice_fusion.3), channel_id=1, source_target_pairs={{0,1},{1,0},{2,3},{3,2},{4,5},{5,4},{6,7},{7,6},{8,9},{9,8},{10,11... | collective-permute-start | bytes 983048 | tf_op jit(solution)/shard_map/gram/ppermute | solution.py:604
  (15 other events, 55.9 us)

commit v5 on v4

--- a/solution.py
+++ b/solution.py
@@ -85,7 +85,7 @@
             other[j, s] = jnp.where(x == 0, high, low)
             return carry
 
-        lax.fori_loop(0, sites, one, 0, unroll=4)
+        lax.fori_loop(0, sites, one, 0, unroll=16)
 
 
 def turn_first(x_arr, states):
@@ -210,7 +210,7 @@
             split[layer * sites + s, half:, :] = low_part
             return carry
 
-        lax.fori_loop(0, sites, one, 0, unroll=4)
+        lax.fori_loop(0, sites, one, 0, unroll=16)
 
     for n, layer in enumerate(layers_out):
 

time: 164 us -> 164 us (level)
  Pallas kernels: 59.7 us -> 57.7 us
  transfers between devices with their start and end apart: 26 -> 26, of which waited for: 19 -> 19; matrix products, arithmetic and copies ran while one was open for 2% -> 2% of each run, Pallas kernels for 25% -> 24%
where the time goes in v5:
time: 164 us; the launch traced here: 163 us
  Pallas kernels  57.7 us (35%)
  waiting for transfers between devices  49.2 us (30%)
  starting transfers between devices  44.6 us (27%)
  local copies, waits for them, and re-layouts  10.5 us (6%)
    pallas_call x17, Pallas kernels, call(): pl.pallas_call(kernel, out_shape=out_shape, in_specs=[*specs, *[pl.BlockS...  48.6 us
    all_to_all x2, waiting for transfers between devices, regroup(): return lax.all_to_all(flat, axes, 0, 0, tiled=True).reshape(value.shape)  14 us
    all_to_all x1, waiting for transfers between devices, per_device(): ends = jnp.max(lax.all_to_all(ends, ('z', 'x'), 0, 0, tiled=True), axis=0)  9.35 us
    ppermute x6, waiting for transfers between devices, z_move(): return lax.ppermute(value, ('z', 'x'), pairs)  9.08 us
    all_to_all x2, starting transfers between devices, regroup(): return lax.all_to_all(flat, axes, 0, 0, tiled=True).reshape(value.shape)  8.92 us
    ppermute x7, starting transfers between devices, swap(): return lax.ppermute(value, axis, [(0, 1), (1, 0)])  8.22 us
    pallas_call x2, Pallas kernels, step(): pl.pallas_call(kernel, out_shape=out, grid_spec=pltpu.PrefetchScalarGridS...  8.07 us
    unnamed x45, local copies, waits for them, and re-layouts  7.88 us
  transfers between devices with their start and end apart: 26, of which 19 were waited for; matrix products, arithmetic and copies ran while one was open for 2% of the time, Pallas kernels for 24%

profile of v5, /device:TPU:1, one launch (start us, length us, event | category | flops | bytes accessed | tf_op | source)
XLA Modules:
  0.0 162.8 jit_solution(13802493762080178065)
XLA Ops:
  2.7 4.2 %collective-permute-start.3 = (f32[1,16,64,128]{3,2,1,0:T(8,128)S(1)}, f32[1,16,64,128]{3,2,1,0:T(8,128)S(1)}, u32[]{:S(2)}, u32[]{:S(2)}) collective-permute-start(f32[1,16,64,128]{3,2,1,0:T(8,128)S(1)} %get-tuple-element.20.refs_4_.refs_2_.refs_5_.refs_9_), channel_id=1, source_target_pairs={{0,24},{4,12},{8,0},{12,20},{16,8},{20,28},{24,16},{28,4},{1,25},{... | collective-permute-start | bytes 1572872 | tf_op jit(solution)/shard_map/prepare/ppermute | solution.py:631
  12.5 3.0 %prepare.8 = (bf16[16,128,256]{2,1,0:T(8,128)(2,1)S(1)}, f32[8,128]{1,0:T(8,128)S(1)}) custom-call(s32[224]{0:T(256)S(1)} %reshape.74.refs_0_, f32[16,128,128]{2,1,0:T(8,128)S(1)} %copy-done.11, f32[2,16,128]{2,1,0:T(8,128)S(1)} %copy-done.15, f32[8,128]{1,0:T(8,128)S(1)} %collective-permute-done.1.refs_3_), custom_call_target="tpu_custom_call" | custom-call | flops 1 | bytes 1 | tf_op jit(solution)/shard_map/prepare/pallas_call | solution.py:39
  17.5 2.1 %collective-permute-done.2.refs_0_ = f32[1,16,64,128]{3,2,1,0:T(8,128)S(1)} collective-permute-done((f32[1,16,64,128]{3,2,1,0:T(8,128)}, f32[1,16,64,128]{3,2,1,0:T(8,128)S(1)}, u32[]{:S(2)}, u32[]{:S(2)}) %collective-permute-start.2) | collective-permute-done | bytes 524320 | tf_op jit(solution)/shard_map/prepare/ppermute | solution.py:70
  22.6 4.2 %all-to-all-start = ((f32[8,8,128]{2,1,0:T(8,128)}), f32[8,8,128]{2,1,0:T(8,128)S(1)}, u32[]{:S(2)}, u32[]{:S(2)}) async-start(f32[8,8,128]{2,1,0:T(8,128)} %broadcast_in_dim.43), calls=%async_computation | async-start | bytes 65536 | tf_op jit(solution)/shard_map/prepare/all_to_all | solution.py:667
  27.4 9.3 %all-to-all-done = f32[8,8,128]{2,1,0:T(8,128)S(1)} async-done(((f32[8,8,128]{2,1,0:T(8,128)}), f32[8,8,128]{2,1,0:T(8,128)S(1)}, u32[]{:S(2)}, u32[]{:S(2)}) %all-to-all-start) | async-done | bytes 32800 | tf_op jit(solution)/shard_map/prepare/all_to_all | solution.py:667
  36.8 2.5 %first.3.refs_8_.refs_7_.refs_5_ = f32[1,16,64,128]{3,2,1,0:T(8,128)S(1)} custom-call(s32[448]{0:T(512)S(1)} %reshape.72.refs_0_, s32[448]{0:T(512)S(1)} %reshape.73.refs_1_, s32[1]{0:T(128)} %bitcast.x_ref.refs_0_.refs_2_, bf16[16,128,256]{2,1,0:T(8,128)(2,1)S(1)} %copy-done.1, f32[64,128]{1,0:T(8,128)S(1)} %bitcast.14, f32[1,16,64,128]{3,2,1,0:T(8,128)S(1)} %copy-done.3, ...), custom_call_target="tpu_custom_call" | custom-call | flops 1 | bytes 1 | tf_op jit(solution)/shard_map/first/pallas_call | solution.py:39
  39.4 2.5 %first.4.refs_9_.refs_5_ = f32[1,16,64,128]{3,2,1,0:T(8,128)S(1)} custom-call(s32[448]{0:T(512)S(1)} %reshape.72.refs_0_, s32[448]{0:T(512)S(1)} %reshape.73.refs_1_, s32[1]{0:T(128)} %bitcast.x_ref.refs_0_.refs_2_, bf16[16,128,256]{2,1,0:T(8,128)(2,1)S(1)} %copy-done.1, f32[64,128]{1,0:T(8,128)S(1)} %bitcast.15, ...), custom_call_target="tpu_custom_call" | custom-call | flops 1 | bytes 1 | tf_op jit(solution)/shard_map/first/pallas_call | solution.py:39
  41.8 3.5 %collective-permute-start.7 = (f32[1,16,64,128]{3,2,1,0:T(8,128)S(1)}, f32[1,16,64,128]{3,2,1,0:T(8,128)S(1)}, u32[]{:S(2)}, u32[]{:S(2)}) collective-permute-start(f32[1,16,64,128]{3,2,1,0:T(8,128)S(1)} %first.4.refs_9_.refs_5_), channel_id=1, source_target_pairs={{0,24},{4,12},{8,0},{12,20},{16,8},{20,28},{24,16},{28,4},{1,25},{... | collective-permute-start | bytes 1572872 | tf_op jit(solution)/shard_map/first/ppermute | solution.py:631
  46.4 3.6 %first.5.refs_6_ = f32[2,16,64,128]{3,2,1,0:T(8,128)S(1)} custom-call(s32[448]{0:T(512)S(1)} %reshape.72.refs_0_, s32[448]{0:T(512)S(1)} %reshape.73.refs_1_, s32[1]{0:T(128)} %bitcast.x_ref.refs_0_.refs_2_, bf16[16,128,256]{2,1,0:T(8,128)(2,1)S(1)} %copy-done.1, f32[64,128]{1,0:T(8,128)S(1)} %bitcast.16, ...), custom_call_target="tpu_custom_call" | custom-call | flops 1 | bytes 1 | tf_op jit(solution)/shard_map/first/pallas_call | solution.py:39
  50.1 3.6 %second.4 = (f32[2,16,64,128]{3,2,1,0:T(8,128)S(1)}, f32[2,16,64,128]{3,2,1,0:T(8,128)S(1)}) custom-call(s32[448]{0:T(512)S(1)} %reshape.72.refs_0_, s32[448]{0:T(512)S(1)} %reshape.73.refs_1_, s32[1]{0:T(128)} %bitcast.x_ref.refs_0_.refs_2_, bf16[16,128,256]{2,1,0:T(8,128)(2,1)S(1)} %copy-done.1, f32[64,128]{1,0:T(8,128)S(1)} %bitcast.17, ...), custom_call_target="tpu_custom_call" | custom-call | flops 1 | bytes 1 | tf_op jit(solution)/shard_map/second/pallas_call | solution.py:39
  54.1 3.7 %second.5 = (f32[1,16,64,128]{3,2,1,0:T(8,128)}, f32[1,16,64,128]{3,2,1,0:T(8,128)S(1)}) custom-call(s32[448]{0:T(512)S(1)} %reshape.72.refs_0_, s32[448]{0:T(512)S(1)} %reshape.73.refs_1_, s32[1]{0:T(128)} %bitcast.x_ref.refs_0_.refs_2_, bf16[16,128,256]{2,1,0:T(8,128)(2,1)S(1)} %copy-done.1, f32[64,128]{1,0:T(8,128)S(1)} %bitcast.18, ...), custom_call_target="tpu_custom_call" | custom-call | flops 1 | bytes 1 | tf_op jit(solution)/shard_map/second/pallas_call | solution.py:39
  57.8 2.6 %collective-permute-start.8 = (f32[8,128]{1,0:T(8,128)S(1)}, f32[8,128]{1,0:T(8,128)S(1)}, u32[]{:S(2)}, u32[]{:S(2)}) collective-permute-start(f32[8,128]{1,0:T(8,128)S(1)} %second.6), channel_id=1, source_target_pairs={{0,1},{1,0},{2,3},{3,2},{4,5},{5,4},{6,7},{7,6},{8,9},{9,8},{10,11... | collective-permute-start | bytes 12296 | tf_op jit(solution)/shard_map/second/ppermute | solution.py:70
  60.4 5.9 %collective-permute-done.7.refs_7_ = f32[1,16,64,128]{3,2,1,0:T(8,128)S(1)} collective-permute-done((f32[1,16,64,128]{3,2,1,0:T(8,128)S(1)}, f32[1,16,64,128]{3,2,1,0:T(8,128)S(1)}, u32[]{:S(2)}, u32[]{:S(2)}) %collective-permute-start.7) | collective-permute-done | bytes 524320 | tf_op jit(solution)/shard_map/first/ppermute | solution.py:631
  66.3 2.4 %second.7 = (f32[1,16,64,128]{3,2,1,0:T(8,128)S(1)}, f32[1,16,64,128]{3,2,1,0:T(8,128)S(1)}) custom-call(s32[448]{0:T(512)S(1)} %reshape.72.refs_0_, s32[448]{0:T(512)S(1)} %reshape.73.refs_1_, s32[1]{0:T(128)} %bitcast.x_ref.refs_0_.refs_2_, bf16[16,128,256]{2,1,0:T(8,128)(2,1)S(1)} %copy-done.1, f32[64,128]{1,0:T(8,128)S(1)} %bitcast.19, ...), custom_call_target="tpu_custom_call" | custom-call | flops 1 | bytes 1 | tf_op jit(solution)/shard_map/second/pallas_call | solution.py:39
  72.8 4.7 %third.5.refs_11_ = f32[2,4,1,4,64,128]{5,4,3,2,1,0:T(8,128)} custom-call(s32[448]{0:T(512)S(1)} %reshape.72.refs_0_, s32[448]{0:T(512)S(1)} %reshape.73.refs_1_, s32[1]{0:T(128)} %bitcast.x_ref.refs_0_.refs_2_, bf16[16,128,256]{2,1,0:T(8,128)(2,1)S(1)} %copy-done.1, f32[64,128]{1,0:T(8,128)S(1)} %bitcast.20, ...), custom_call_target="tpu_custom_call" | custom-call | flops 1 | bytes 1 | tf_op jit(solution)/shard_map/third/pallas_call | solution.py:39
  77.5 4.6 %all-to-all-start.2 = ((f32[8,1,4,64,128]{4,3,2,1,0:T(8,128)}), f32[8,1,4,64,128]{4,3,2,1,0:T(8,128)}, u32[]{:S(2)}, u32[]{:S(2)}) async-start(f32[8,1,4,64,128]{4,3,2,1,0:T(8,128)} %bitcast.7), calls=%async_computation.2 | async-start | bytes 2097152 | tf_op jit(solution)/shard_map/third/all_to_all | solution.py:697
  82.1 4.0 %third.6.refs_11_ = f32[2,4,1,4,64,128]{5,4,3,2,1,0:T(8,128)} custom-call(s32[448]{0:T(512)S(1)} %reshape.72.refs_0_, s32[448]{0:T(512)S(1)} %reshape.73.refs_1_, s32[1]{0:T(128)} %bitcast.x_ref.refs_0_.refs_2_, bf16[16,128,256]{2,1,0:T(8,128)(2,1)S(1)} %copy-done.1, f32[64,128]{1,0:T(8,128)S(1)} %bitcast.21, ...), custom_call_target="tpu_custom_call" | custom-call | flops 1 | bytes 1 | tf_op jit(solution)/shard_map/third/pallas_call | solution.py:272
  86.1 1.8 %collective-permute-done.9.refs_7_ = f32[1,16,64,128]{3,2,1,0:T(8,128)} collective-permute-done((f32[1,16,64,128]{3,2,1,0:T(8,128)S(1)}, f32[1,16,64,128]{3,2,1,0:T(8,128)}, u32[]{:S(2)}, u32[]{:S(2)}) %collective-permute-start.9) | collective-permute-done | bytes 524320 | tf_op jit(solution)/shard_map/third/ppermute | solution.py:631
  87.9 4.1 %third.7.refs_0_ = f32[2,4,1,4,64,128]{5,4,3,2,1,0:T(8,128)} custom-call(s32[448]{0:T(512)S(1)} %reshape.72.refs_0_, s32[448]{0:T(512)S(1)} %reshape.73.refs_1_, s32[1]{0:T(128)} %bitcast.x_ref.refs_0_.refs_2_, bf16[16,128,256]{2,1,0:T(8,128)(2,1)S(1)} %copy-done.1, f32[64,128]{1,0:T(8,128)S(1)} %bitcast.22, ...), custom_call_target="tpu_custom_call", output_to_operand_aliasing={{}: (11, {})} | custom-call | flops 199999995904 | bytes 1 | tf_op jit(solution)/shard_map/third/pallas_call | solution.py:272
  92.0 3.8 %all-to-all-done.2 = f32[8,1,4,64,128]{4,3,2,1,0:T(8,128)} async-done(((f32[8,1,4,64,128]{4,3,2,1,0:T(8,128)}), f32[8,1,4,64,128]{4,3,2,1,0:T(8,128)}, u32[]{:S(2)}, u32[]{:S(2)}) %all-to-all-start.2) | async-done | bytes 1048608 | tf_op jit(solution)/shard_map/third/all_to_all | solution.py:697
  95.8 4.3 %all-to-all-start.1 = ((f32[8,1,4,64,128]{4,3,2,1,0:T(8,128)}), f32[8,1,4,64,128]{4,3,2,1,0:T(8,128)S(1)}, u32[]{:S(2)}, u32[]{:S(2)}) async-start(f32[8,1,4,64,128]{4,3,2,1,0:T(8,128)} %bitcast.4), calls=%async_computation.1 | async-start | bytes 2097152 | tf_op jit(solution)/shard_map/third/all_to_all | solution.py:697
  101.3 2.2 %gram.5.refs_1_ = f32[1280,128]{1,0:T(8,128)S(1)} custom-call(f32[2,4,1,4,64,128]{5,4,3,2,1,0:T(8,128)} %bitcast.8.refs_0_.refs_2_, f32[8,128]{1,0:T(8,128)S(1)} %collective-permute-done.12.refs_1_), custom_call_target="tpu_custom_call" | custom-call | flops 1 | bytes 1 | tf_op jit(solution)/shard_map/gram/pallas_call | solution.py:39
  103.6 10.2 %all-to-all-done.1 = f32[8,1,4,64,128]{4,3,2,1,0:T(8,128)S(1)} async-done(((f32[8,1,4,64,128]{4,3,2,1,0:T(8,128)}), f32[8,1,4,64,128]{4,3,2,1,0:T(8,128)S(1)}, u32[]{:S(2)}, u32[]{:S(2)}) %all-to-all-start.1) | async-done | bytes 1048608 | tf_op jit(solution)/shard_map/third/all_to_all | solution.py:697
  118.6 2.1 %collective-permute-start.16 = (f32[160,128]{1,0:T(8,128)S(1)}, f32[160,128]{1,0:T(8,128)S(1)}, u32[]{:S(2)}, u32[]{:S(2)}) collective-permute-start(f32[160,128]{1,0:T(8,128)S(1)} %get-tuple-element.38), channel_id=1, source_target_pairs={{0,6},{2,0},{4,2},{6,4},{1,7},{3,1},{5,3},{7,5},{8,14},{10,8},{12,... | collective-permute-start | bytes 245768 | tf_op jit(solution)/shard_map/gram/ppermute | solution.py:597
  121.9 1.9 %collective-permute-done.16 = f32[160,128]{1,0:T(8,128)S(1)} collective-permute-done((f32[160,128]{1,0:T(8,128)S(1)}, f32[160,128]{1,0:T(8,128)S(1)}, u32[]{:S(2)}, u32[]{:S(2)}) %collective-permute-start.16) | collective-permute-done | bytes 81952 | tf_op jit(solution)/shard_map/gram/ppermute | solution.py:597
  125.2 2.0 %collective-permute-done.17 = f32[160,128]{1,0:T(8,128)S(1)} collective-permute-done((f32[160,128]{1,0:T(8,128)S(1)}, f32[160,128]{1,0:T(8,128)S(1)}, u32[]{:S(2)}, u32[]{:S(2)}) %collective-permute-start.17) | collective-permute-done | bytes 81952 | tf_op jit(solution)/shard_map/gram/ppermute | solution.py:584
  127.2 1.9 %collective-permute-start.18 = (f32[160,128]{1,0:T(8,128)S(1)}, f32[160,128]{1,0:T(8,128)S(1)}, u32[]{:S(2)}, u32[]{:S(2)}) collective-permute-start(f32[160,128]{1,0:T(8,128)S(1)} %add.142), channel_id=1, source_target_pairs={{0,16},{8,24},{16,0},{24,8},{1,17},{9,25},{17,1},{25,9},{2,18},{10... | collective-permute-start | bytes 245768 | tf_op jit(solution)/shard_map/gram/ppermute | solution.py:584
  129.1 2.4 %collective-permute-done.18 = f32[160,128]{1,0:T(8,128)S(1)} collective-permute-done((f32[160,128]{1,0:T(8,128)S(1)}, f32[160,128]{1,0:T(8,128)S(1)}, u32[]{:S(2)}, u32[]{:S(2)}) %collective-permute-start.18) | collective-permute-done | bytes 81952 | tf_op jit(solution)/shard_map/gram/ppermute | solution.py:584
  134.9 1.9 %collective-permute-done.20 = f32[160,128]{1,0:T(8,128)S(1)} collective-permute-done((f32[160,128]{1,0:T(8,128)S(1)}, f32[160,128]{1,0:T(8,128)S(1)}, u32[]{:S(2)}, u32[]{:S(2)}) %collective-permute-start.20) | collective-permute-done | bytes 81952 | tf_op jit(solution)/shard_map/gram/ppermute | solution.py:604
  138.4 5.2 %collective-permute-start.22 = (f32[640,128]{1,0:T(8,128)S(1)}, f32[640,128]{1,0:T(8,128)S(1)}, u32[]{:S(2)}, u32[]{:S(2)}) collective-permute-start(f32[640,128]{1,0:T(8,128)S(1)} %constant_dynamic-update-slice_fusion.3), channel_id=1, source_target_pairs={{0,1},{1,0},{2,3},{3,2},{4,5},{5,4},{6,7},{7,6},{8,9},{9,8},{10,11... | collective-permute-start | bytes 983048 | tf_op jit(solution)/shard_map/gram/ppermute | solution.py:604
  143.6 1.8 %gram.7 = (bf16[2,4,128,512]{3,2,1,0:T(8,128)(2,1)S(1)}, bf16[2,4,128,512]{3,2,1,0:T(8,128)(2,1)S(1)}) custom-call(s32[1]{0:T(128)} %bitcast.x_ref.refs_0_.refs_2_, f32[2,4,1,4,64,128]{5,4,3,2,1,0:T(8,128)S(1)} %bitcast.13, f32[2,4,1,4,64,128]{5,4,3,2,1,0:T(8,128)} %bitcast.8.refs_0_.refs_2_), custom_call_target="tpu_custom_call" | custom-call | flops 1 | bytes 1 | tf_op jit(solution)/shard_map/gram/pallas_call | solution.py:39
  145.6 17.2 %finish.1 = f32[2,4,128,512]{3,2,1,0:T(8,128)} custom-call(f32[1280,128]{1,0:T(8,128)S(1)} %constant_dynamic-update-slice_fusion.7.refs_0_, bf16[2,4,128,512]{3,2,1,0:T(8,128)(2,1)S(1)} %get-tuple-element.33.refs_1_, bf16[2,4,128,512]{3,2,1,0:T(8,128)(2,1)S(1)} %get-tuple-element.34.refs_2_), custom_call_target="tpu_custom_call" | custom-call | flops 1 | bytes 1 | tf_op jit(solution)/shard_map/finish/pallas_call | solution.py:39
  (119 shorter events, 33.2 us)
Async XLA Ops:
  2.7 14.7 %collective-permute-start.3 = (f32[1,16,64,128]{3,2,1,0:T(8,128)S(1)}, f32[1,16,64,128]{3,2,1,0:T(8,128)S(1)}, u32[]{:S(2)}, u32[]{:S(2)}) collective-permute-start(f32[1,16,64,128]{3,2,1,0:T(8,128)S(1)} %get-tuple-element.20.refs_4_.refs_2_.refs_5_.refs_9_), channel_id=1, source_target_pairs={{0,24},{4,12},{8,0},{12,20},{16,8},{20,28},{24,16},{28,4},{1,25},{... | collective-permute-start | bytes 1572872 | tf_op jit(solution)/shard_map/prepare/ppermute | solution.py:631
  6.9 12.7 %collective-permute-start.2 = (f32[1,16,64,128]{3,2,1,0:T(8,128)}, f32[1,16,64,128]{3,2,1,0:T(8,128)S(1)}, u32[]{:S(2)}, u32[]{:S(2)}) collective-permute-start(f32[1,16,64,128]{3,2,1,0:T(8,128)} %get-tuple-element.24), channel_id=1, source_target_pairs={{0,4},{4,0},{1,5},{5,1},{2,6},{6,2},{3,7},{7,3},{8,12},{12,8},{9,1... | collective-permute-start | bytes 1572872 | tf_op jit(solution)/shard_map/prepare/ppermute | solution.py:70
  6.9 5.6 %collective-permute-start.1 = (f32[8,128]{1,0:T(8,128)S(1)}, f32[8,128]{1,0:T(8,128)S(1)}, u32[]{:S(2)}, u32[]{:S(2)}) collective-permute-start(f32[8,128]{1,0:T(8,128)S(1)} %get-tuple-element.21), channel_id=1, source_target_pairs={{0,1},{1,0},{2,3},{3,2},{4,5},{5,4},{6,7},{7,6},{8,9},{9,8},{10,11... | collective-permute-start | bytes 12296 | tf_op jit(solution)/shard_map/prepare/ppermute | solution.py:70
  7.9 18.9 %collective-permute-start = (f32[2,32,128]{2,1,0:T(8,128)S(1)}, f32[2,32,128]{2,1,0:T(8,128)S(1)}, u32[]{:S(2)}, u32[]{:S(2)}) collective-permute-start(f32[2,32,128]{2,1,0:T(8,128)S(1)} %prepare.7), channel_id=1, source_target_pairs={{0,4},{4,0},{1,5},{5,1},{2,6},{6,2},{3,7},{7,3},{8,12},{12,8},{9,1... | collective-permute-start | bytes 98312 | tf_op jit(solution)/shard_map/prepare/ppermute | solution.py:70
  20.4 16.4 %copy-start.1 = (bf16[16,128,256]{2,1,0:T(8,128)(2,1)S(1)}, bf16[16,128,256]{2,1,0:T(8,128)(2,1)}, u32[]{:S(2)}) copy-start(bf16[16,128,256]{2,1,0:T(8,128)(2,1)} %copy-done) | copy-start | bytes 3145732
  20.4 16.4 %copy-start.3 = (f32[1,16,64,128]{3,2,1,0:T(8,128)S(1)}, f32[1,16,64,128]{3,2,1,0:T(8,128)}, u32[]{:S(2)}) copy-start(f32[1,16,64,128]{3,2,1,0:T(8,128)} %prepare.10.refs_1_.refs_5_.refs_8_.refs_11_.refs_9_) | copy-start | bytes 1572868
  20.4 16.4 %copy-start.7 = (f32[1,16,64,128]{3,2,1,0:T(8,128)S(1)}, f32[1,16,64,128]{3,2,1,0:T(8,128)}, u32[]{:S(2)}) copy-start(f32[1,16,64,128]{3,2,1,0:T(8,128)} %copy-done.6) | copy-start | bytes 1572868
  20.4 19.0 %collective-permute-start.4 = (f32[1,16,64,128]{3,2,1,0:T(8,128)}, f32[1,16,64,128]{3,2,1,0:T(8,128)}, u32[]{:S(2)}, u32[]{:S(2)}) collective-permute-start(f32[1,16,64,128]{3,2,1,0:T(8,128)} %prepare.10.refs_1_.refs_5_.refs_8_.refs_11_.refs_9_), channel_id=1, source_target_pairs={{0,8},{4,28},{8,16},{12,4},{16,24},{20,12},{24,0},{28,20},{1,9},{5... | collective-permute-start | bytes 1572872 | tf_op jit(solution)/shard_map/prepare/ppermute | solution.py:631
  20.4 16.4 %collective-permute-start.5 = (f32[1,16,64,128]{3,2,1,0:T(8,128)}, f32[1,16,64,128]{3,2,1,0:T(8,128)}, u32[]{:S(2)}, u32[]{:S(2)}) collective-permute-start(f32[1,16,64,128]{3,2,1,0:T(8,128)} %prepare.11), channel_id=1, source_target_pairs={{0,4},{4,0},{1,5},{5,1},{2,6},{6,2},{3,7},{7,3},{8,12},{12,8},{9,1... | collective-permute-start | bytes 1572872 | tf_op jit(solution)/shard_map/prepare/ppermute | solution.py:70
  22.6 14.2 %all-to-all-start = ((f32[8,8,128]{2,1,0:T(8,128)}), f32[8,8,128]{2,1,0:T(8,128)S(1)}, u32[]{:S(2)}, u32[]{:S(2)}) async-start(f32[8,8,128]{2,1,0:T(8,128)} %broadcast_in_dim.43), calls=%async_computation | async-start | bytes 65536 | tf_op jit(solution)/shard_map/prepare/all_to_all | solution.py:667
  39.3 14.8 %collective-permute-start.6 = (f32[1,16,64,128]{3,2,1,0:T(8,128)S(1)}, f32[1,16,64,128]{3,2,1,0:T(8,128)S(1)}, u32[]{:S(2)}, u32[]{:S(2)}) collective-permute-start(f32[1,16,64,128]{3,2,1,0:T(8,128)S(1)} %first.3.refs_8_.refs_7_.refs_5_), channel_id=1, source_target_pairs={{0,8},{4,28},{8,16},{12,4},{16,24},{20,12},{24,0},{28,20},{1,9},{5... | collective-permute-start | bytes 1572872 | tf_op jit(solution)/shard_map/first/ppermute | solution.py:631
  41.8 24.5 %collective-permute-start.7 = (f32[1,16,64,128]{3,2,1,0:T(8,128)S(1)}, f32[1,16,64,128]{3,2,1,0:T(8,128)S(1)}, u32[]{:S(2)}, u32[]{:S(2)}) collective-permute-start(f32[1,16,64,128]{3,2,1,0:T(8,128)S(1)} %first.4.refs_9_.refs_5_), channel_id=1, source_target_pairs={{0,24},{4,12},{8,0},{12,20},{16,8},{20,28},{24,16},{28,4},{1,25},{... | collective-permute-start | bytes 1572872 | tf_op jit(solution)/shard_map/first/ppermute | solution.py:631
  54.1 12.2 %copy-start.8 = (f32[1,16,64,128]{3,2,1,0:T(8,128)S(1)}, f32[1,16,64,128]{3,2,1,0:T(8,128)}, u32[]{:S(2)}) copy-start(f32[1,16,64,128]{3,2,1,0:T(8,128)} %copy-done.6) | copy-start | bytes 1572868
  57.8 10.9 %copy-start.16 = (f32[1,16,64,128]{3,2,1,0:T(8,128)}, f32[1,16,64,128]{3,2,1,0:T(8,128)S(1)}, u32[]{:S(2)}) copy-start(f32[1,16,64,128]{3,2,1,0:T(8,128)S(1)} %get-tuple-element.30.refs_9_) | copy-start | bytes 1572868
  57.8 12.9 %copy-start.20 = (s32[128]{0:T(128)S(1)}, s32[128]{0:T(128)}, u32[]{:S(2)}) copy-start(s32[128]{0:T(128)} %param.11) | copy-start | bytes 1540
  57.8 8.5 %collective-permute-start.8 = (f32[8,128]{1,0:T(8,128)S(1)}, f32[8,128]{1,0:T(8,128)S(1)}, u32[]{:S(2)}, u32[]{:S(2)}) collective-permute-start(f32[8,128]{1,0:T(8,128)S(1)} %second.6), channel_id=1, source_target_pairs={{0,1},{1,0},{2,3},{3,2},{4,5},{5,4},{6,7},{7,6},{8,9},{9,8},{10,11... | collective-permute-start | bytes 12296 | tf_op jit(solution)/shard_map/second/ppermute | solution.py:70
  60.4 21.7 %collective-permute-start.10 = (f32[1,16,64,128]{3,2,1,0:T(8,128)}, f32[1,16,64,128]{3,2,1,0:T(8,128)}, u32[]{:S(2)}, u32[]{:S(2)}) collective-permute-start(f32[1,16,64,128]{3,2,1,0:T(8,128)} %get-tuple-element.28.refs_0_.refs_5_), channel_id=1, source_target_pairs={{0,24},{4,12},{8,0},{12,20},{16,8},{20,28},{24,16},{28,4},{1,25},{... | collective-permute-start | bytes 1572872 | tf_op jit(solution)/shard_map/second/ppermute | solution.py:631
  69.5 18.4 %collective-permute-start.9 = (f32[1,16,64,128]{3,2,1,0:T(8,128)S(1)}, f32[1,16,64,128]{3,2,1,0:T(8,128)}, u32[]{:S(2)}, u32[]{:S(2)}) collective-permute-start(f32[1,16,64,128]{3,2,1,0:T(8,128)S(1)} %get-tuple-element.29.refs_0_.refs_7_.refs_5_), channel_id=1, source_target_pairs={{0,8},{4,28},{8,16},{12,4},{16,24},{20,12},{24,0},{28,20},{1,9},{5... | collective-permute-start | bytes 1572872 | tf_op jit(solution)/shard_map/third/ppermute | solution.py:631
  69.5 2.0 %collective-permute-start.11 = (f32[8,128]{1,0:T(8,128)S(1)}, f32[8,128]{1,0:T(8,128)S(1)}, u32[]{:S(2)}, u32[]{:S(2)}) collective-permute-start(f32[8,128]{1,0:T(8,128)S(1)} %third.4), channel_id=1, source_target_pairs={{0,1},{1,0},{2,3},{3,2},{4,5},{5,4},{6,7},{7,6},{8,9},{9,8},{10,11... | collective-permute-start | bytes 12296 | tf_op jit(solution)/shard_map/third/ppermute | solution.py:70
  77.5 18.3 %all-to-all-start.2 = ((f32[8,1,4,64,128]{4,3,2,1,0:T(8,128)}), f32[8,1,4,64,128]{4,3,2,1,0:T(8,128)}, u32[]{:S(2)}, u32[]{:S(2)}) async-start(f32[8,1,4,64,128]{4,3,2,1,0:T(8,128)} %bitcast.7), calls=%async_computation.2 | async-start | bytes 2097152 | tf_op jit(solution)/shard_map/third/all_to_all | solution.py:697
  95.8 17.9 %all-to-all-start.1 = ((f32[8,1,4,64,128]{4,3,2,1,0:T(8,128)}), f32[8,1,4,64,128]{4,3,2,1,0:T(8,128)S(1)}, u32[]{:S(2)}, u32[]{:S(2)}) async-start(f32[8,1,4,64,128]{4,3,2,1,0:T(8,128)} %bitcast.4), calls=%async_computation.1 | async-start | bytes 2097152 | tf_op jit(solution)/shard_map/third/all_to_all | solution.py:697
  100.1 1.2 collective-permute-start.12
  114.8 2.2 %collective-permute-start.13 = (f32[640,128]{1,0:T(8,128)S(1)}, f32[640,128]{1,0:T(8,128)S(1)}, u32[]{:S(2)}, u32[]{:S(2)}) collective-permute-start(f32[640,128]{1,0:T(8,128)S(1)} %constant_dynamic-slice_fusion.3), channel_id=1, source_target_pairs={{0,1},{1,0},{2,3},{3,2},{4,5},{5,4},{6,7},{7,6},{8,9},{9,8},{10,11... | collective-permute-start | bytes 983048 | tf_op jit(solution)/shard_map/gram/ppermute | solution.py:597
  117.1 4.6 %collective-permute-start.14 = (f32[160,128]{1,0:T(8,128)S(1)}, f32[160,128]{1,0:T(8,128)S(1)}, u32[]{:S(2)}, u32[]{:S(2)}) collective-permute-start(f32[160,128]{1,0:T(8,128)S(1)} %get-tuple-element.37), channel_id=1, source_target_pairs={{0,2},{2,4},{4,6},{6,0},{1,3},{3,5},{5,7},{7,1},{8,10},{10,12},{12... | collective-permute-start | bytes 245768 | tf_op jit(solution)/shard_map/gram/ppermute | solution.py:597
  118.4 3.6 %collective-permute-start.15 = (f32[160,128]{1,0:T(8,128)S(1)}, f32[160,128]{1,0:T(8,128)S(1)}, u32[]{:S(2)}, u32[]{:S(2)}) collective-permute-start(f32[160,128]{1,0:T(8,128)S(1)} %get-tuple-element.39), channel_id=1, source_target_pairs={{0,4},{2,6},{4,0},{6,2},{1,5},{3,7},{5,1},{7,3},{8,12},{10,14},{12... | collective-permute-start | bytes 245768 | tf_op jit(solution)/shard_map/gram/ppermute | solution.py:597
  118.6 5.2 %collective-permute-start.16 = (f32[160,128]{1,0:T(8,128)S(1)}, f32[160,128]{1,0:T(8,128)S(1)}, u32[]{:S(2)}, u32[]{:S(2)}) collective-permute-start(f32[160,128]{1,0:T(8,128)S(1)} %get-tuple-element.38), channel_id=1, source_target_pairs={{0,6},{2,0},{4,2},{6,4},{1,7},{3,1},{5,3},{7,5},{8,14},{10,8},{12,... | collective-permute-start | bytes 245768 | tf_op jit(solution)/shard_map/gram/ppermute | solution.py:597
  123.9 3.4 %collective-permute-start.17 = (f32[160,128]{1,0:T(8,128)S(1)}, f32[160,128]{1,0:T(8,128)S(1)}, u32[]{:S(2)}, u32[]{:S(2)}) collective-permute-start(f32[160,128]{1,0:T(8,128)S(1)} %add_add_fusion), channel_id=1, source_target_pairs={{0,8},{8,0},{16,24},{24,16},{1,9},{9,1},{17,25},{25,17},{2,10},{10... | collective-permute-start | bytes 245768 | tf_op jit(solution)/shard_map/gram/ppermute | solution.py:584
  127.2 4.3 %collective-permute-start.18 = (f32[160,128]{1,0:T(8,128)S(1)}, f32[160,128]{1,0:T(8,128)S(1)}, u32[]{:S(2)}, u32[]{:S(2)}) collective-permute-start(f32[160,128]{1,0:T(8,128)S(1)} %add.142), channel_id=1, source_target_pairs={{0,16},{8,24},{16,0},{24,8},{1,17},{9,25},{17,1},{25,9},{2,18},{10... | collective-permute-start | bytes 245768 | tf_op jit(solution)/shard_map/gram/ppermute | solution.py:584
  131.5 3.3 %collective-permute-start.19 = (f32[160,128]{1,0:T(8,128)S(1)}, f32[160,128]{1,0:T(8,128)S(1)}, u32[]{:S(2)}, u32[]{:S(2)}) collective-permute-start(f32[160,128]{1,0:T(8,128)S(1)} %get-tuple-element.36), channel_id=1, source_target_pairs={{0,6},{2,0},{4,2},{6,4},{1,7},{3,1},{5,3},{7,5},{8,14},{10,8},{12,... | collective-permute-start | bytes 245768 | tf_op jit(solution)/shard_map/gram/ppermute | solution.py:604
  132.7 4.1 %collective-permute-start.20 = (f32[160,128]{1,0:T(8,128)S(1)}, f32[160,128]{1,0:T(8,128)S(1)}, u32[]{:S(2)}, u32[]{:S(2)}) collective-permute-start(f32[160,128]{1,0:T(8,128)S(1)} %get-tuple-element.36), channel_id=1, source_target_pairs={{0,4},{2,6},{4,0},{6,2},{1,5},{3,7},{5,1},{7,3},{8,12},{10,14},{12... | collective-permute-start | bytes 245768 | tf_op jit(solution)/shard_map/gram/ppermute | solution.py:604
  134.1 4.3 %collective-permute-start.21 = (f32[160,128]{1,0:T(8,128)S(1)}, f32[160,128]{1,0:T(8,128)S(1)}, u32[]{:S(2)}, u32[]{:S(2)}) collective-permute-start(f32[160,128]{1,0:T(8,128)S(1)} %get-tuple-element.36), channel_id=1, source_target_pairs={{0,2},{2,4},{4,6},{6,0},{1,3},{3,5},{5,7},{7,1},{8,10},{10,12},{12... | collective-permute-start | bytes 245768 | tf_op jit(solution)/shard_map/gram/ppermute | solution.py:604
  138.4 7.1 %collective-permute-start.22 = (f32[640,128]{1,0:T(8,128)S(1)}, f32[640,128]{1,0:T(8,128)S(1)}, u32[]{:S(2)}, u32[]{:S(2)}) collective-permute-start(f32[640,128]{1,0:T(8,128)S(1)} %constant_dynamic-update-slice_fusion.3), channel_id=1, source_target_pairs={{0,1},{1,0},{2,3},{3,2},{4,5},{5,4},{6,7},{7,6},{8,9},{9,8},{10,11... | collective-permute-start | bytes 983048 | tf_op jit(solution)/shard_map/gram/ppermute | solution.py:604
  (15 other events, 55.7 us)

commit v6 on v5

--- a/solution.py
+++ b/solution.py
@@ -661,7 +661,7 @@
             [pltpu.VMEM((couplings.shape[0], 1, orb), f32)] * 2,
             after=(mark,),
         )
-        partner_b = hold(partner_b, far, table)
+        partner_b = hold(partner_b, far, ends)
         devices = 2 * depth
         ends = jnp.broadcast_to(ends[None], (devices, *ends.shape))
         ends = jnp.max(lax.all_to_all(ends, ("z", "x"), 0, 0, tiled=True), axis=0)

time: 164 us -> 164 us (level)
  no operation moved by 1% of the time
where the time goes in v6:
time: 164 us; the launch traced here: 163 us
  Pallas kernels  57.8 us (35%)
  waiting for transfers between devices  48.4 us (30%)
  starting transfers between devices  44.6 us (27%)
  local copies, waits for them, and re-layouts  11.3 us (7%)
    pallas_call x17, Pallas kernels, call(): pl.pallas_call(kernel, out_shape=out_shape, in_specs=[*specs, *[pl.BlockS...  48.6 us
    all_to_all x2, waiting for transfers between devices, regroup(): return lax.all_to_all(flat, axes, 0, 0, tiled=True).reshape(value.shape)  14 us
    all_to_all x1, waiting for transfers between devices, per_device(): ends = jnp.max(lax.all_to_all(ends, ('z', 'x'), 0, 0, tiled=True), axis=0)  9.35 us
    all_to_all x2, starting transfers between devices, regroup(): return lax.all_to_all(flat, axes, 0, 0, tiled=True).reshape(value.shape)  8.92 us
    unnamed x45, local copies, waits for them, and re-layouts  8.71 us
    ppermute x6, waiting for transfers between devices, z_move(): return lax.ppermute(value, ('z', 'x'), pairs)  8.26 us
    ppermute x7, starting transfers between devices, swap(): return lax.ppermute(value, axis, [(0, 1), (1, 0)])  8.18 us
    pallas_call x2, Pallas kernels, step(): pl.pallas_call(kernel, out_shape=out, grid_spec=pltpu.PrefetchScalarGridS...  8.07 us
  transfers between devices with their start and end apart: 26, of which 19 were waited for; matrix products, arithmetic and copies ran while one was open for 2% of the time, Pallas kernels for 24%

profile of v6, /device:TPU:1, one launch (start us, length us, event | category | flops | bytes accessed | tf_op | source)
XLA Modules:
  0.0 162.7 jit_solution(14078031877407807151)
XLA Ops:
  2.7 4.2 %collective-permute-start.3 = (f32[1,16,64,128]{3,2,1,0:T(8,128)S(1)}, f32[1,16,64,128]{3,2,1,0:T(8,128)S(1)}, u32[]{:S(2)}, u32[]{:S(2)}) collective-permute-start(f32[1,16,64,128]{3,2,1,0:T(8,128)S(1)} %get-tuple-element.20.refs_4_.refs_2_.refs_5_.refs_9_), channel_id=1, source_target_pairs={{0,24},{4,12},{8,0},{12,20},{16,8},{20,28},{24,16},{28,4},{1,25},{... | collective-permute-start | bytes 1572872 | tf_op jit(solution)/shard_map/prepare/ppermute | solution.py:631
  13.8 3.0 %prepare.8 = (bf16[16,128,256]{2,1,0:T(8,128)(2,1)S(1)}, f32[8,128]{1,0:T(8,128)S(1)}) custom-call(s32[224]{0:T(256)S(1)} %reshape.74.refs_0_, f32[16,128,128]{2,1,0:T(8,128)S(1)} %copy-done.9, f32[2,16,128]{2,1,0:T(8,128)S(1)} %copy-done.13, f32[8,128]{1,0:T(8,128)S(1)} %collective-permute-done.1.refs_3_), custom_call_target="tpu_custom_call" | custom-call | flops 1 | bytes 1 | tf_op jit(solution)/shard_map/prepare/pallas_call | solution.py:39
  17.5 2.1 %collective-permute-done.2.refs_0_ = f32[1,16,64,128]{3,2,1,0:T(8,128)S(1)} collective-permute-done((f32[1,16,64,128]{3,2,1,0:T(8,128)}, f32[1,16,64,128]{3,2,1,0:T(8,128)S(1)}, u32[]{:S(2)}, u32[]{:S(2)}) %collective-permute-start.2) | collective-permute-done | bytes 524320 | tf_op jit(solution)/shard_map/prepare/ppermute | solution.py:70
  22.6 4.2 %all-to-all-start = ((f32[8,8,128]{2,1,0:T(8,128)}), f32[8,8,128]{2,1,0:T(8,128)S(1)}, u32[]{:S(2)}, u32[]{:S(2)}) async-start(f32[8,8,128]{2,1,0:T(8,128)} %broadcast_in_dim.43), calls=%async_computation | async-start | bytes 65536 | tf_op jit(solution)/shard_map/prepare/all_to_all | solution.py:667
  27.4 9.4 %all-to-all-done = f32[8,8,128]{2,1,0:T(8,128)S(1)} async-done(((f32[8,8,128]{2,1,0:T(8,128)}), f32[8,8,128]{2,1,0:T(8,128)S(1)}, u32[]{:S(2)}, u32[]{:S(2)}) %all-to-all-start) | async-done | bytes 32800 | tf_op jit(solution)/shard_map/prepare/all_to_all | solution.py:667
  36.8 2.5 %first.3.refs_8_.refs_7_.refs_5_ = f32[1,16,64,128]{3,2,1,0:T(8,128)S(1)} custom-call(s32[448]{0:T(512)S(1)} %reshape.72.refs_0_, s32[448]{0:T(512)S(1)} %reshape.73.refs_1_, s32[1]{0:T(128)} %bitcast.x_ref.refs_0_.refs_2_, bf16[16,128,256]{2,1,0:T(8,128)(2,1)S(1)} %get-tuple-element.22.refs_3_, f32[64,128]{1,0:T(8,128)S(1)} %bitcast.14, ...), custom_call_target="tpu_custom_call" | custom-call | flops 1 | bytes 1 | tf_op jit(solution)/shard_map/first/pallas_call | solution.py:39
  39.4 2.5 %first.4.refs_9_.refs_5_ = f32[1,16,64,128]{3,2,1,0:T(8,128)S(1)} custom-call(s32[448]{0:T(512)S(1)} %reshape.72.refs_0_, s32[448]{0:T(512)S(1)} %reshape.73.refs_1_, s32[1]{0:T(128)} %bitcast.x_ref.refs_0_.refs_2_, bf16[16,128,256]{2,1,0:T(8,128)(2,1)S(1)} %get-tuple-element.22.refs_3_, f32[64,128]{1,0:T(8,128)S(1)} %bitcast.15, ...), custom_call_target="tpu_custom_call" | custom-call | flops 1 | bytes 1 | tf_op jit(solution)/shard_map/first/pallas_call | solution.py:39
  41.8 3.5 %collective-permute-start.7 = (f32[1,16,64,128]{3,2,1,0:T(8,128)S(1)}, f32[1,16,64,128]{3,2,1,0:T(8,128)S(1)}, u32[]{:S(2)}, u32[]{:S(2)}) collective-permute-start(f32[1,16,64,128]{3,2,1,0:T(8,128)S(1)} %first.4.refs_9_.refs_5_), channel_id=1, source_target_pairs={{0,24},{4,12},{8,0},{12,20},{16,8},{20,28},{24,16},{28,4},{1,25},{... | collective-permute-start | bytes 1572872 | tf_op jit(solution)/shard_map/first/ppermute | solution.py:631
  46.4 3.6 %first.5.refs_6_ = f32[2,16,64,128]{3,2,1,0:T(8,128)S(1)} custom-call(s32[448]{0:T(512)S(1)} %reshape.72.refs_0_, s32[448]{0:T(512)S(1)} %reshape.73.refs_1_, s32[1]{0:T(128)} %bitcast.x_ref.refs_0_.refs_2_, bf16[16,128,256]{2,1,0:T(8,128)(2,1)S(1)} %get-tuple-element.22.refs_3_, f32[64,128]{1,0:T(8,128)S(1)} %bitcast.16, ...), custom_call_target="tpu_custom_call" | custom-call | flops 1 | bytes 1 | tf_op jit(solution)/shard_map/first/pallas_call | solution.py:39
  50.1 3.6 %second.4 = (f32[2,16,64,128]{3,2,1,0:T(8,128)S(1)}, f32[2,16,64,128]{3,2,1,0:T(8,128)S(1)}) custom-call(s32[448]{0:T(512)S(1)} %reshape.72.refs_0_, s32[448]{0:T(512)S(1)} %reshape.73.refs_1_, s32[1]{0:T(128)} %bitcast.x_ref.refs_0_.refs_2_, bf16[16,128,256]{2,1,0:T(8,128)(2,1)S(1)} %get-tuple-element.22.refs_3_, f32[64,128]{1,0:T(8,128)S(1)} %bitcast.17, ...), custom_call_target="tpu_custom_call" | custom-call | flops 1 | bytes 1 | tf_op jit(solution)/shard_map/second/pallas_call | solution.py:39
  54.1 3.7 %second.5 = (f32[1,16,64,128]{3,2,1,0:T(8,128)}, f32[1,16,64,128]{3,2,1,0:T(8,128)S(1)}) custom-call(s32[448]{0:T(512)S(1)} %reshape.72.refs_0_, s32[448]{0:T(512)S(1)} %reshape.73.refs_1_, s32[1]{0:T(128)} %bitcast.x_ref.refs_0_.refs_2_, bf16[16,128,256]{2,1,0:T(8,128)(2,1)S(1)} %get-tuple-element.22.refs_3_, f32[64,128]{1,0:T(8,128)S(1)} %bitcast.18, ...), custom_call_target="tpu_custom_call" | custom-call | flops 1 | bytes 1 | tf_op jit(solution)/shard_map/second/pallas_call | solution.py:39
  57.8 2.6 %collective-permute-start.8 = (f32[8,128]{1,0:T(8,128)S(1)}, f32[8,128]{1,0:T(8,128)S(1)}, u32[]{:S(2)}, u32[]{:S(2)}) collective-permute-start(f32[8,128]{1,0:T(8,128)S(1)} %second.6), channel_id=1, source_target_pairs={{0,1},{1,0},{2,3},{3,2},{4,5},{5,4},{6,7},{7,6},{8,9},{9,8},{10,11... | collective-permute-start | bytes 12296 | tf_op jit(solution)/shard_map/second/ppermute | solution.py:70
  60.4 5.9 %collective-permute-done.7.refs_7_ = f32[1,16,64,128]{3,2,1,0:T(8,128)S(1)} collective-permute-done((f32[1,16,64,128]{3,2,1,0:T(8,128)S(1)}, f32[1,16,64,128]{3,2,1,0:T(8,128)S(1)}, u32[]{:S(2)}, u32[]{:S(2)}) %collective-permute-start.7) | collective-permute-done | bytes 524320 | tf_op jit(solution)/shard_map/first/ppermute | solution.py:631
  66.3 2.4 %second.7 = (f32[1,16,64,128]{3,2,1,0:T(8,128)S(1)}, f32[1,16,64,128]{3,2,1,0:T(8,128)S(1)}) custom-call(s32[448]{0:T(512)S(1)} %reshape.72.refs_0_, s32[448]{0:T(512)S(1)} %reshape.73.refs_1_, s32[1]{0:T(128)} %bitcast.x_ref.refs_0_.refs_2_, bf16[16,128,256]{2,1,0:T(8,128)(2,1)S(1)} %get-tuple-element.22.refs_3_, f32[64,128]{1,0:T(8,128)S(1)} %bitcast.19, ...), custom_call_target="tpu_custom_call" | custom-call | flops 1 | bytes 1 | tf_op jit(solution)/shard_map/second/pallas_call | solution.py:39
  72.8 4.7 %third.5.refs_11_ = f32[2,4,1,4,64,128]{5,4,3,2,1,0:T(8,128)} custom-call(s32[448]{0:T(512)S(1)} %reshape.72.refs_0_, s32[448]{0:T(512)S(1)} %reshape.73.refs_1_, s32[1]{0:T(128)} %bitcast.x_ref.refs_0_.refs_2_, bf16[16,128,256]{2,1,0:T(8,128)(2,1)S(1)} %get-tuple-element.22.refs_3_, f32[64,128]{1,0:T(8,128)S(1)} %bitcast.20, ...), custom_call_target="tpu_custom_call" | custom-call | flops 1 | bytes 1 | tf_op jit(solution)/shard_map/third/pallas_call | solution.py:39
  77.5 4.6 %all-to-all-start.2 = ((f32[8,1,4,64,128]{4,3,2,1,0:T(8,128)}), f32[8,1,4,64,128]{4,3,2,1,0:T(8,128)}, u32[]{:S(2)}, u32[]{:S(2)}) async-start(f32[8,1,4,64,128]{4,3,2,1,0:T(8,128)} %bitcast.7), calls=%async_computation.2 | async-start | bytes 2097152 | tf_op jit(solution)/shard_map/third/all_to_all | solution.py:697
  82.1 4.0 %third.6.refs_11_ = f32[2,4,1,4,64,128]{5,4,3,2,1,0:T(8,128)} custom-call(s32[448]{0:T(512)S(1)} %reshape.72.refs_0_, s32[448]{0:T(512)S(1)} %reshape.73.refs_1_, s32[1]{0:T(128)} %bitcast.x_ref.refs_0_.refs_2_, bf16[16,128,256]{2,1,0:T(8,128)(2,1)S(1)} %get-tuple-element.22.refs_3_, f32[64,128]{1,0:T(8,128)S(1)} %bitcast.21, ...), custom_call_target="tpu_custom_call" | custom-call | flops 1 | bytes 1 | tf_op jit(solution)/shard_map/third/pallas_call | solution.py:272
  86.1 1.8 %collective-permute-done.9.refs_7_ = f32[1,16,64,128]{3,2,1,0:T(8,128)} collective-permute-done((f32[1,16,64,128]{3,2,1,0:T(8,128)S(1)}, f32[1,16,64,128]{3,2,1,0:T(8,128)}, u32[]{:S(2)}, u32[]{:S(2)}) %collective-permute-start.9) | collective-permute-done | bytes 524320 | tf_op jit(solution)/shard_map/third/ppermute | solution.py:631
  87.9 4.1 %third.7.refs_0_ = f32[2,4,1,4,64,128]{5,4,3,2,1,0:T(8,128)} custom-call(s32[448]{0:T(512)S(1)} %reshape.72.refs_0_, s32[448]{0:T(512)S(1)} %reshape.73.refs_1_, s32[1]{0:T(128)} %bitcast.x_ref.refs_0_.refs_2_, bf16[16,128,256]{2,1,0:T(8,128)(2,1)S(1)} %get-tuple-element.22.refs_3_, f32[64,128]{1,0:T(8,128)S(1)} %bitcast.22, ...), custom_call_target="tpu_custom_call", output_to_operand_aliasing={{}: (11, {})} | custom-call | flops 199999995904 | bytes 1 | tf_op jit(solution)/shard_map/third/pallas_call | solution.py:272
  92.0 3.8 %all-to-all-done.2 = f32[8,1,4,64,128]{4,3,2,1,0:T(8,128)} async-done(((f32[8,1,4,64,128]{4,3,2,1,0:T(8,128)}), f32[8,1,4,64,128]{4,3,2,1,0:T(8,128)}, u32[]{:S(2)}, u32[]{:S(2)}) %all-to-all-start.2) | async-done | bytes 1048608 | tf_op jit(solution)/shard_map/third/all_to_all | solution.py:697
  95.8 4.3 %all-to-all-start.1 = ((f32[8,1,4,64,128]{4,3,2,1,0:T(8,128)}), f32[8,1,4,64,128]{4,3,2,1,0:T(8,128)S(1)}, u32[]{:S(2)}, u32[]{:S(2)}) async-start(f32[8,1,4,64,128]{4,3,2,1,0:T(8,128)} %bitcast.4), calls=%async_computation.1 | async-start | bytes 2097152 | tf_op jit(solution)/shard_map/third/all_to_all | solution.py:697
  101.3 2.2 %gram.5.refs_1_ = f32[1280,128]{1,0:T(8,128)S(1)} custom-call(f32[2,4,1,4,64,128]{5,4,3,2,1,0:T(8,128)} %bitcast.8.refs_0_.refs_2_, f32[8,128]{1,0:T(8,128)S(1)} %collective-permute-done.12.refs_1_), custom_call_target="tpu_custom_call" | custom-call | flops 1 | bytes 1 | tf_op jit(solution)/shard_map/gram/pallas_call | solution.py:39
  103.5 10.2 %all-to-all-done.1 = f32[8,1,4,64,128]{4,3,2,1,0:T(8,128)S(1)} async-done(((f32[8,1,4,64,128]{4,3,2,1,0:T(8,128)}), f32[8,1,4,64,128]{4,3,2,1,0:T(8,128)S(1)}, u32[]{:S(2)}, u32[]{:S(2)}) %all-to-all-start.1) | async-done | bytes 1048608 | tf_op jit(solution)/shard_map/third/all_to_all | solution.py:697
  118.6 2.1 %collective-permute-start.16 = (f32[160,128]{1,0:T(8,128)S(1)}, f32[160,128]{1,0:T(8,128)S(1)}, u32[]{:S(2)}, u32[]{:S(2)}) collective-permute-start(f32[160,128]{1,0:T(8,128)S(1)} %get-tuple-element.38), channel_id=1, source_target_pairs={{0,6},{2,0},{4,2},{6,4},{1,7},{3,1},{5,3},{7,5},{8,14},{10,8},{12,... | collective-permute-start | bytes 245768 | tf_op jit(solution)/shard_map/gram/ppermute | solution.py:597
  121.9 1.9 %collective-permute-done.16 = f32[160,128]{1,0:T(8,128)S(1)} collective-permute-done((f32[160,128]{1,0:T(8,128)S(1)}, f32[160,128]{1,0:T(8,128)S(1)}, u32[]{:S(2)}, u32[]{:S(2)}) %collective-permute-start.16) | collective-permute-done | bytes 81952 | tf_op jit(solution)/shard_map/gram/ppermute | solution.py:597
  125.2 2.0 %collective-permute-done.17 = f32[160,128]{1,0:T(8,128)S(1)} collective-permute-done((f32[160,128]{1,0:T(8,128)S(1)}, f32[160,128]{1,0:T(8,128)S(1)}, u32[]{:S(2)}, u32[]{:S(2)}) %collective-permute-start.17) | collective-permute-done | bytes 81952 | tf_op jit(solution)/shard_map/gram/ppermute | solution.py:584
  127.2 1.9 %collective-permute-start.18 = (f32[160,128]{1,0:T(8,128)S(1)}, f32[160,128]{1,0:T(8,128)S(1)}, u32[]{:S(2)}, u32[]{:S(2)}) collective-permute-start(f32[160,128]{1,0:T(8,128)S(1)} %add.142), channel_id=1, source_target_pairs={{0,16},{8,24},{16,0},{24,8},{1,17},{9,25},{17,1},{25,9},{2,18},{10... | collective-permute-start | bytes 245768 | tf_op jit(solution)/shard_map/gram/ppermute | solution.py:584
  129.1 2.4 %collective-permute-done.18 = f32[160,128]{1,0:T(8,128)S(1)} collective-permute-done((f32[160,128]{1,0:T(8,128)S(1)}, f32[160,128]{1,0:T(8,128)S(1)}, u32[]{:S(2)}, u32[]{:S(2)}) %collective-permute-start.18) | collective-permute-done | bytes 81952 | tf_op jit(solution)/shard_map/gram/ppermute | solution.py:584
  134.9 1.9 %collective-permute-done.20 = f32[160,128]{1,0:T(8,128)S(1)} collective-permute-done((f32[160,128]{1,0:T(8,128)S(1)}, f32[160,128]{1,0:T(8,128)S(1)}, u32[]{:S(2)}, u32[]{:S(2)}) %collective-permute-start.20) | collective-permute-done | bytes 81952 | tf_op jit(solution)/shard_map/gram/ppermute | solution.py:604
  138.4 5.2 %collective-permute-start.22 = (f32[640,128]{1,0:T(8,128)S(1)}, f32[640,128]{1,0:T(8,128)S(1)}, u32[]{:S(2)}, u32[]{:S(2)}) collective-permute-start(f32[640,128]{1,0:T(8,128)S(1)} %constant_dynamic-update-slice_fusion.3), channel_id=1, source_target_pairs={{0,1},{1,0},{2,3},{3,2},{4,5},{5,4},{6,7},{7,6},{8,9},{9,8},{10,11... | collective-permute-start | bytes 983048 | tf_op jit(solution)/shard_map/gram/ppermute | solution.py:604
  143.6 1.8 %gram.7 = (bf16[2,4,128,512]{3,2,1,0:T(8,128)(2,1)S(1)}, bf16[2,4,128,512]{3,2,1,0:T(8,128)(2,1)S(1)}) custom-call(s32[1]{0:T(128)} %bitcast.x_ref.refs_0_.refs_2_, f32[2,4,1,4,64,128]{5,4,3,2,1,0:T(8,128)S(1)} %bitcast.13, f32[2,4,1,4,64,128]{5,4,3,2,1,0:T(8,128)} %bitcast.8.refs_0_.refs_2_), custom_call_target="tpu_custom_call" | custom-call | flops 1 | bytes 1 | tf_op jit(solution)/shard_map/gram/pallas_call | solution.py:39
  145.6 17.2 %finish.1 = f32[2,4,128,512]{3,2,1,0:T(8,128)} custom-call(f32[1280,128]{1,0:T(8,128)S(1)} %constant_dynamic-update-slice_fusion.7.refs_0_, bf16[2,4,128,512]{3,2,1,0:T(8,128)(2,1)S(1)} %get-tuple-element.33.refs_1_, bf16[2,4,128,512]{3,2,1,0:T(8,128)(2,1)S(1)} %get-tuple-element.34.refs_2_), custom_call_target="tpu_custom_call" | custom-call | flops 1 | bytes 1 | tf_op jit(solution)/shard_map/finish/pallas_call | solution.py:39
  (119 shorter events, 33.2 us)
Async XLA Ops:
  0.0 7.9 %copy-start.18 = (s32[2,7,16]{2,0,1:T(2,128)S(1)}, s32[2,7,16]{2,0,1:T(2,128)}, u32[]{:S(2)}) copy-start(s32[2,7,16]{2,0,1:T(2,128)} %param.10) | copy-start | bytes 2692
  2.7 14.7 %collective-permute-start.3 = (f32[1,16,64,128]{3,2,1,0:T(8,128)S(1)}, f32[1,16,64,128]{3,2,1,0:T(8,128)S(1)}, u32[]{:S(2)}, u32[]{:S(2)}) collective-permute-start(f32[1,16,64,128]{3,2,1,0:T(8,128)S(1)} %get-tuple-element.20.refs_4_.refs_2_.refs_5_.refs_9_), channel_id=1, source_target_pairs={{0,24},{4,12},{8,0},{12,20},{16,8},{20,28},{24,16},{28,4},{1,25},{... | collective-permute-start | bytes 1572872 | tf_op jit(solution)/shard_map/prepare/ppermute | solution.py:631
  6.9 12.7 %collective-permute-start.2 = (f32[1,16,64,128]{3,2,1,0:T(8,128)}, f32[1,16,64,128]{3,2,1,0:T(8,128)S(1)}, u32[]{:S(2)}, u32[]{:S(2)}) collective-permute-start(f32[1,16,64,128]{3,2,1,0:T(8,128)} %get-tuple-element.24), channel_id=1, source_target_pairs={{0,4},{4,0},{1,5},{5,1},{2,6},{6,2},{3,7},{7,3},{8,12},{12,8},{9,1... | collective-permute-start | bytes 1572872 | tf_op jit(solution)/shard_map/prepare/ppermute | solution.py:70
  6.9 5.6 %collective-permute-start.1 = (f32[8,128]{1,0:T(8,128)S(1)}, f32[8,128]{1,0:T(8,128)S(1)}, u32[]{:S(2)}, u32[]{:S(2)}) collective-permute-start(f32[8,128]{1,0:T(8,128)S(1)} %get-tuple-element.21), channel_id=1, source_target_pairs={{0,1},{1,0},{2,3},{3,2},{4,5},{5,4},{6,7},{7,6},{8,9},{9,8},{10,11... | collective-permute-start | bytes 12296 | tf_op jit(solution)/shard_map/prepare/ppermute | solution.py:70
  7.9 18.9 %collective-permute-start = (f32[2,32,128]{2,1,0:T(8,128)S(1)}, f32[2,32,128]{2,1,0:T(8,128)S(1)}, u32[]{:S(2)}, u32[]{:S(2)}) collective-permute-start(f32[2,32,128]{2,1,0:T(8,128)S(1)} %prepare.7), channel_id=1, source_target_pairs={{0,4},{4,0},{1,5},{5,1},{2,6},{6,2},{3,7},{7,3},{8,12},{12,8},{9,1... | collective-permute-start | bytes 98312 | tf_op jit(solution)/shard_map/prepare/ppermute | solution.py:70
  20.4 16.4 %copy-start.1 = (f32[1,16,64,128]{3,2,1,0:T(8,128)S(1)}, f32[1,16,64,128]{3,2,1,0:T(8,128)}, u32[]{:S(2)}) copy-start(f32[1,16,64,128]{3,2,1,0:T(8,128)} %prepare.10.refs_1_.refs_5_.refs_8_.refs_11_.refs_9_) | copy-start | bytes 1572868
  20.4 16.4 %copy-start.5 = (f32[1,16,64,128]{3,2,1,0:T(8,128)S(1)}, f32[1,16,64,128]{3,2,1,0:T(8,128)}, u32[]{:S(2)}) copy-start(f32[1,16,64,128]{3,2,1,0:T(8,128)} %copy-done.4) | copy-start | bytes 1572868
  20.4 19.0 %collective-permute-start.4 = (f32[1,16,64,128]{3,2,1,0:T(8,128)}, f32[1,16,64,128]{3,2,1,0:T(8,128)}, u32[]{:S(2)}, u32[]{:S(2)}) collective-permute-start(f32[1,16,64,128]{3,2,1,0:T(8,128)} %prepare.10.refs_1_.refs_5_.refs_8_.refs_11_.refs_9_), channel_id=1, source_target_pairs={{0,8},{4,28},{8,16},{12,4},{16,24},{20,12},{24,0},{28,20},{1,9},{5... | collective-permute-start | bytes 1572872 | tf_op jit(solution)/shard_map/prepare/ppermute | solution.py:631
  20.4 16.4 %collective-permute-start.5 = (f32[1,16,64,128]{3,2,1,0:T(8,128)}, f32[1,16,64,128]{3,2,1,0:T(8,128)}, u32[]{:S(2)}, u32[]{:S(2)}) collective-permute-start(f32[1,16,64,128]{3,2,1,0:T(8,128)} %prepare.11), channel_id=1, source_target_pairs={{0,4},{4,0},{1,5},{5,1},{2,6},{6,2},{3,7},{7,3},{8,12},{12,8},{9,1... | collective-permute-start | bytes 1572872 | tf_op jit(solution)/shard_map/prepare/ppermute | solution.py:70
  22.6 14.2 %all-to-all-start = ((f32[8,8,128]{2,1,0:T(8,128)}), f32[8,8,128]{2,1,0:T(8,128)S(1)}, u32[]{:S(2)}, u32[]{:S(2)}) async-start(f32[8,8,128]{2,1,0:T(8,128)} %broadcast_in_dim.43), calls=%async_computation | async-start | bytes 65536 | tf_op jit(solution)/shard_map/prepare/all_to_all | solution.py:667
  39.3 14.8 %collective-permute-start.6 = (f32[1,16,64,128]{3,2,1,0:T(8,128)S(1)}, f32[1,16,64,128]{3,2,1,0:T(8,128)S(1)}, u32[]{:S(2)}, u32[]{:S(2)}) collective-permute-start(f32[1,16,64,128]{3,2,1,0:T(8,128)S(1)} %first.3.refs_8_.refs_7_.refs_5_), channel_id=1, source_target_pairs={{0,8},{4,28},{8,16},{12,4},{16,24},{20,12},{24,0},{28,20},{1,9},{5... | collective-permute-start | bytes 1572872 | tf_op jit(solution)/shard_map/first/ppermute | solution.py:631
  41.8 24.5 %collective-permute-start.7 = (f32[1,16,64,128]{3,2,1,0:T(8,128)S(1)}, f32[1,16,64,128]{3,2,1,0:T(8,128)S(1)}, u32[]{:S(2)}, u32[]{:S(2)}) collective-permute-start(f32[1,16,64,128]{3,2,1,0:T(8,128)S(1)} %first.4.refs_9_.refs_5_), channel_id=1, source_target_pairs={{0,24},{4,12},{8,0},{12,20},{16,8},{20,28},{24,16},{28,4},{1,25},{... | collective-permute-start | bytes 1572872 | tf_op jit(solution)/shard_map/first/ppermute | solution.py:631
  54.1 12.2 %copy-start.6 = (f32[1,16,64,128]{3,2,1,0:T(8,128)S(1)}, f32[1,16,64,128]{3,2,1,0:T(8,128)}, u32[]{:S(2)}) copy-start(f32[1,16,64,128]{3,2,1,0:T(8,128)} %copy-done.4) | copy-start | bytes 1572868
  57.8 10.9 %copy-start.16 = (f32[1,16,64,128]{3,2,1,0:T(8,128)}, f32[1,16,64,128]{3,2,1,0:T(8,128)S(1)}, u32[]{:S(2)}) copy-start(f32[1,16,64,128]{3,2,1,0:T(8,128)S(1)} %get-tuple-element.30.refs_9_) | copy-start | bytes 1572868
  57.8 12.9 %copy-start.20 = (s32[128]{0:T(128)S(1)}, s32[128]{0:T(128)}, u32[]{:S(2)}) copy-start(s32[128]{0:T(128)} %param.11) | copy-start | bytes 1540
  57.8 8.5 %collective-permute-start.8 = (f32[8,128]{1,0:T(8,128)S(1)}, f32[8,128]{1,0:T(8,128)S(1)}, u32[]{:S(2)}, u32[]{:S(2)}) collective-permute-start(f32[8,128]{1,0:T(8,128)S(1)} %second.6), channel_id=1, source_target_pairs={{0,1},{1,0},{2,3},{3,2},{4,5},{5,4},{6,7},{7,6},{8,9},{9,8},{10,11... | collective-permute-start | bytes 12296 | tf_op jit(solution)/shard_map/second/ppermute | solution.py:70
  60.4 21.7 %collective-permute-start.10 = (f32[1,16,64,128]{3,2,1,0:T(8,128)}, f32[1,16,64,128]{3,2,1,0:T(8,128)}, u32[]{:S(2)}, u32[]{:S(2)}) collective-permute-start(f32[1,16,64,128]{3,2,1,0:T(8,128)} %get-tuple-element.28.refs_0_.refs_5_), channel_id=1, source_target_pairs={{0,24},{4,12},{8,0},{12,20},{16,8},{20,28},{24,16},{28,4},{1,25},{... | collective-permute-start | bytes 1572872 | tf_op jit(solution)/shard_map/second/ppermute | solution.py:631
  69.5 18.4 %collective-permute-start.9 = (f32[1,16,64,128]{3,2,1,0:T(8,128)S(1)}, f32[1,16,64,128]{3,2,1,0:T(8,128)}, u32[]{:S(2)}, u32[]{:S(2)}) collective-permute-start(f32[1,16,64,128]{3,2,1,0:T(8,128)S(1)} %get-tuple-element.29.refs_0_.refs_7_.refs_5_), channel_id=1, source_target_pairs={{0,8},{4,28},{8,16},{12,4},{16,24},{20,12},{24,0},{28,20},{1,9},{5... | collective-permute-start | bytes 1572872 | tf_op jit(solution)/shard_map/third/ppermute | solution.py:631
  69.5 2.0 %collective-permute-start.11 = (f32[8,128]{1,0:T(8,128)S(1)}, f32[8,128]{1,0:T(8,128)S(1)}, u32[]{:S(2)}, u32[]{:S(2)}) collective-permute-start(f32[8,128]{1,0:T(8,128)S(1)} %third.4), channel_id=1, source_target_pairs={{0,1},{1,0},{2,3},{3,2},{4,5},{5,4},{6,7},{7,6},{8,9},{9,8},{10,11... | collective-permute-start | bytes 12296 | tf_op jit(solution)/shard_map/third/ppermute | solution.py:70
  77.5 18.3 %all-to-all-start.2 = ((f32[8,1,4,64,128]{4,3,2,1,0:T(8,128)}), f32[8,1,4,64,128]{4,3,2,1,0:T(8,128)}, u32[]{:S(2)}, u32[]{:S(2)}) async-start(f32[8,1,4,64,128]{4,3,2,1,0:T(8,128)} %bitcast.7), calls=%async_computation.2 | async-start | bytes 2097152 | tf_op jit(solution)/shard_map/third/all_to_all | solution.py:697
  95.8 17.9 %all-to-all-start.1 = ((f32[8,1,4,64,128]{4,3,2,1,0:T(8,128)}), f32[8,1,4,64,128]{4,3,2,1,0:T(8,128)S(1)}, u32[]{:S(2)}, u32[]{:S(2)}) async-start(f32[8,1,4,64,128]{4,3,2,1,0:T(8,128)} %bitcast.4), calls=%async_computation.1 | async-start | bytes 2097152 | tf_op jit(solution)/shard_map/third/all_to_all | solution.py:697
  100.1 1.2 collective-permute-start.12
  114.8 2.2 %collective-permute-start.13 = (f32[640,128]{1,0:T(8,128)S(1)}, f32[640,128]{1,0:T(8,128)S(1)}, u32[]{:S(2)}, u32[]{:S(2)}) collective-permute-start(f32[640,128]{1,0:T(8,128)S(1)} %constant_dynamic-slice_fusion.3), channel_id=1, source_target_pairs={{0,1},{1,0},{2,3},{3,2},{4,5},{5,4},{6,7},{7,6},{8,9},{9,8},{10,11... | collective-permute-start | bytes 983048 | tf_op jit(solution)/shard_map/gram/ppermute | solution.py:597
  117.1 4.6 %collective-permute-start.14 = (f32[160,128]{1,0:T(8,128)S(1)}, f32[160,128]{1,0:T(8,128)S(1)}, u32[]{:S(2)}, u32[]{:S(2)}) collective-permute-start(f32[160,128]{1,0:T(8,128)S(1)} %get-tuple-element.37), channel_id=1, source_target_pairs={{0,2},{2,4},{4,6},{6,0},{1,3},{3,5},{5,7},{7,1},{8,10},{10,12},{12... | collective-permute-start | bytes 245768 | tf_op jit(solution)/shard_map/gram/ppermute | solution.py:597
  118.3 3.6 %collective-permute-start.15 = (f32[160,128]{1,0:T(8,128)S(1)}, f32[160,128]{1,0:T(8,128)S(1)}, u32[]{:S(2)}, u32[]{:S(2)}) collective-permute-start(f32[160,128]{1,0:T(8,128)S(1)} %get-tuple-element.39), channel_id=1, source_target_pairs={{0,4},{2,6},{4,0},{6,2},{1,5},{3,7},{5,1},{7,3},{8,12},{10,14},{12... | collective-permute-start | bytes 245768 | tf_op jit(solution)/shard_map/gram/ppermute | solution.py:597
  118.6 5.2 %collective-permute-start.16 = (f32[160,128]{1,0:T(8,128)S(1)}, f32[160,128]{1,0:T(8,128)S(1)}, u32[]{:S(2)}, u32[]{:S(2)}) collective-permute-start(f32[160,128]{1,0:T(8,128)S(1)} %get-tuple-element.38), channel_id=1, source_target_pairs={{0,6},{2,0},{4,2},{6,4},{1,7},{3,1},{5,3},{7,5},{8,14},{10,8},{12,... | collective-permute-start | bytes 245768 | tf_op jit(solution)/shard_map/gram/ppermute | solution.py:597
  123.8 3.4 %collective-permute-start.17 = (f32[160,128]{1,0:T(8,128)S(1)}, f32[160,128]{1,0:T(8,128)S(1)}, u32[]{:S(2)}, u32[]{:S(2)}) collective-permute-start(f32[160,128]{1,0:T(8,128)S(1)} %add_add_fusion), channel_id=1, source_target_pairs={{0,8},{8,0},{16,24},{24,16},{1,9},{9,1},{17,25},{25,17},{2,10},{10... | collective-permute-start | bytes 245768 | tf_op jit(solution)/shard_map/gram/ppermute | solution.py:584
  127.2 4.3 %collective-permute-start.18 = (f32[160,128]{1,0:T(8,128)S(1)}, f32[160,128]{1,0:T(8,128)S(1)}, u32[]{:S(2)}, u32[]{:S(2)}) collective-permute-start(f32[160,128]{1,0:T(8,128)S(1)} %add.142), channel_id=1, source_target_pairs={{0,16},{8,24},{16,0},{24,8},{1,17},{9,25},{17,1},{25,9},{2,18},{10... | collective-permute-start | bytes 245768 | tf_op jit(solution)/shard_map/gram/ppermute | solution.py:584
  131.5 3.3 %collective-permute-start.19 = (f32[160,128]{1,0:T(8,128)S(1)}, f32[160,128]{1,0:T(8,128)S(1)}, u32[]{:S(2)}, u32[]{:S(2)}) collective-permute-start(f32[160,128]{1,0:T(8,128)S(1)} %get-tuple-element.36), channel_id=1, source_target_pairs={{0,6},{2,0},{4,2},{6,4},{1,7},{3,1},{5,3},{7,5},{8,14},{10,8},{12,... | collective-permute-start | bytes 245768 | tf_op jit(solution)/shard_map/gram/ppermute | solution.py:604
  132.6 4.1 %collective-permute-start.20 = (f32[160,128]{1,0:T(8,128)S(1)}, f32[160,128]{1,0:T(8,128)S(1)}, u32[]{:S(2)}, u32[]{:S(2)}) collective-permute-start(f32[160,128]{1,0:T(8,128)S(1)} %get-tuple-element.36), channel_id=1, source_target_pairs={{0,4},{2,6},{4,0},{6,2},{1,5},{3,7},{5,1},{7,3},{8,12},{10,14},{12... | collective-permute-start | bytes 245768 | tf_op jit(solution)/shard_map/gram/ppermute | solution.py:604
  134.1 4.3 %collective-permute-start.21 = (f32[160,128]{1,0:T(8,128)S(1)}, f32[160,128]{1,0:T(8,128)S(1)}, u32[]{:S(2)}, u32[]{:S(2)}) collective-permute-start(f32[160,128]{1,0:T(8,128)S(1)} %get-tuple-element.36), channel_id=1, source_target_pairs={{0,2},{2,4},{4,6},{6,0},{1,3},{3,5},{5,7},{7,1},{8,10},{10,12},{12... | collective-permute-start | bytes 245768 | tf_op jit(solution)/shard_map/gram/ppermute | solution.py:604
  138.4 7.1 %collective-permute-start.22 = (f32[640,128]{1,0:T(8,128)S(1)}, f32[640,128]{1,0:T(8,128)S(1)}, u32[]{:S(2)}, u32[]{:S(2)}) collective-permute-start(f32[640,128]{1,0:T(8,128)S(1)} %constant_dynamic-update-slice_fusion.3), channel_id=1, source_target_pairs={{0,1},{1,0},{2,3},{3,2},{4,5},{5,4},{6,7},{7,6},{8,9},{9,8},{10,11... | collective-permute-start | bytes 983048 | tf_op jit(solution)/shard_map/gram/ppermute | solution.py:604
  (15 other events, 42.2 us)
